TPU v7x, 32 devices: a whole 2x2x4 slice. The times are simulated.
32 devices in a mesh: ta: 32 (over z, y, x, core).
Axes of the slice: x: 2, y: 2, z: 4, core: 2. Of those that a mesh axis runs over, the one named last changes fastest.
Arguments:
- frames: bfloat16 [16384, 512], P('ta'), may hold values from -8 to 8
- cotangent: float32 [16384, 512], P('ta'), may hold values from -30 to 30
- mem_index: int32 [1024, 4], P('ta'), may hold values from 0 to 1022, as said below
- master: float32 [2, 3146752], P(None, 'ta')
- moment: float32 [2, 3146752], P(None, 'ta')
- second: float32 [2, 3146752], P(None, 'ta')
- average: float32 [2, 3146752], P(None, 'ta')
Outputs:
- output: float32 [16384, 512], P('ta')
- grad_frames: float32 [16384, 512], P('ta')
- gain_grads: float32 [2, 1024], P(None, 'ta')
- new_moment: float32 [2, 3146752], P(None, 'ta')
- new_second: float32 [2, 3146752], P(None, 'ta')
- new_master: float32 [2, 3146752], P(None, 'ta')
- new_average: float32 [2, 3146752], P(None, 'ta')
Inputs may be any that keep to these rules, and one draw needn't show every extreme that they name: `mem_index`: for segment g of the stream, slot 0 names one of the first min(g, 32) segments (0 when g is 0), slots 1 to 2 name one of the segments max(g - 64, 0) to g - 1 (0 when g is 0), and slot 3 names g - 1 (0 when g is 0); a slot is visible only when its number is below g.
All inputs are finite; a program needn't handle non-finite values.
Results may differ from a plain program's by a relative error of at most 0.023.
Values may be sent and summed in bfloat16 or wider, within the bound.
No kernel may reach another device: no remote copies, remote signals or barrier semaphores. Data moves between devices by JAX's collectives and lax.ppermute only.
A program may use at most 192 MiB of HBM per device.

v0:
```python
import jax
import jax.numpy as jnp
from jax import lax
from jax.sharding import PartitionSpec as P

D = 512
HEADS = 8
FF = 2048
SEG = 16
LEFT = 30
RIGHT = 4
MEM = 4
WIN = 4
STEP = 10


def from_behind(value, axis, by):
    devices = lax.axis_size(axis)
    pairs = [(i, i + by) for i in range(devices) if 0 <= i + by < devices]
    return lax.ppermute(value, axis, pairs)


def norm_rows(values, gain):
    centred = values - jnp.mean(values, axis=-1, keepdims=True)
    return centred * lax.rsqrt(jnp.mean(centred * centred, axis=-1, keepdims=True) + 1e-05) * gain


def unpack(row, model_width, hidden_width):
    piece_sizes = [
        3 * model_width * model_width,
        model_width * model_width,
        model_width * hidden_width,
        hidden_width * model_width,
        2 * model_width,
    ]
    shapes = [
        (model_width, 3 * model_width),
        (model_width, model_width),
        (model_width, hidden_width),
        (hidden_width, model_width),
        (2, model_width),
    ]
    pieces = []
    offset = 0
    for piece_size, shape in zip(piece_sizes, shapes):
        pieces.append(row[offset : offset + piece_size].reshape(shape))
        offset = offset + piece_size
    return pieces


def key_masks(first_seg, seg_count, total_frames, mem_index):
    seg_ids = first_seg + jnp.arange(seg_count, dtype=jnp.int32)
    offsets = jnp.arange(WIN * SEG, dtype=jnp.int32)
    target_positions = seg_ids[:, None] * SEG - LEFT + offsets[None, :]
    window_ok = (
        (offsets[None, :] < LEFT + SEG + RIGHT)
        & (target_positions >= 0)
        & (target_positions < total_frames)
    )
    memory_ok = mem_index < seg_ids[:, None]
    return jnp.concatenate([window_ok, memory_ok], axis=1)


def score_heads(query_heads, key_heads, attend_mask, score_scale):
    scores = (
        jnp.einsum("sqhe,skhe->shqk", query_heads, key_heads, preferred_element_type=jnp.float32)
        * score_scale
    )
    return jnp.where(attend_mask[:, None, None, :], scores, -1e30)


def layer_forward(stream, row, mem_index, attend_mask):
    tokens_dev, model_width = stream.shape
    weight_qkv, weight_out, weight_up, weight_down, gains = unpack(row, model_width, FF)
    seg_count = tokens_dev // SEG
    head_dim = model_width // HEADS
    score_scale = head_dim ** (-0.5)
    gain_values = gains.astype(jnp.float32)
    normed_one, norm_one_back = jax.vjp(norm_rows, stream, gain_values[0])
    hidden_one = normed_one.astype(jnp.bfloat16)
    projected = jnp.dot(hidden_one, weight_qkv, preferred_element_type=jnp.float32).astype(
        jnp.bfloat16
    )
    queries = projected[:, :model_width]
    keyvals = projected[:, model_width:]
    summary = jnp.mean(
        hidden_one.astype(jnp.float32).reshape(seg_count, SEG, model_width), axis=1
    ).astype(jnp.bfloat16)
    left_rows = from_behind(keyvals[tokens_dev - LEFT :], "ta", 1)
    right_rows = from_behind(keyvals[:RIGHT], "ta", -1)
    summaries = lax.all_gather(summary, "ta", axis=0, tiled=True)
    flat_index = mem_index.reshape(-1)
    chosen = jnp.take(summaries, flat_index, axis=0)
    weight_kv = weight_qkv[:, model_width:]
    memory_kv = (
        jnp.dot(chosen, weight_kv, preferred_element_type=jnp.float32)
        .astype(jnp.bfloat16)
        .reshape(seg_count, MEM, 2 * model_width)
    )
    filler = jnp.zeros(((WIN - 1) * SEG - LEFT - RIGHT, 2 * model_width), jnp.bfloat16)
    extended = jnp.concatenate([left_rows, keyvals, right_rows, filler], axis=0)
    windows = jnp.concatenate(
        [
            extended[SEG * block_at : SEG * block_at + tokens_dev].reshape(
                seg_count, SEG, 2 * model_width
            )
            for block_at in range(WIN)
        ],
        axis=1,
    )
    key_rows = jnp.concatenate([windows, memory_kv], axis=1)
    key_count = key_rows.shape[1]
    query_heads = queries.reshape(seg_count, SEG, HEADS, head_dim)
    key_heads = key_rows[:, :, :model_width].reshape(seg_count, key_count, HEADS, head_dim)
    value_heads = key_rows[:, :, model_width:].reshape(seg_count, key_count, HEADS, head_dim)
    scores = score_heads(query_heads, key_heads, attend_mask, score_scale)
    row_max = jnp.max(scores, axis=-1, keepdims=True)
    log_total = row_max + jnp.log(jnp.sum(jnp.exp(scores - row_max), axis=-1, keepdims=True))
    attn_weights = jnp.exp(scores - log_total).astype(jnp.bfloat16)
    mixed = (
        jnp.einsum("shqk,skhe->sqhe", attn_weights, value_heads, preferred_element_type=jnp.float32)
        .astype(jnp.bfloat16)
        .reshape(tokens_dev, model_width)
    )
    after_attn = stream + jnp.dot(mixed, weight_out, preferred_element_type=jnp.float32)
    normed_two, norm_two_back = jax.vjp(norm_rows, after_attn, gain_values[1])
    hidden_two = normed_two.astype(jnp.bfloat16)
    up_proj = jnp.dot(hidden_two, weight_up, preferred_element_type=jnp.float32)
    activated, gelu_back = jax.vjp(jax.nn.gelu, up_proj)
    active_low = activated.astype(jnp.bfloat16)
    result = after_attn + jnp.dot(active_low, weight_down, preferred_element_type=jnp.float32)
    saved_state = {
        "norm_one_back": norm_one_back,
        "hidden_one": hidden_one,
        "summary_count": summaries.shape[0],
        "flat_index": flat_index,
        "mem_index": mem_index,
        "chosen": chosen,
        "query_heads": query_heads,
        "key_heads": key_heads,
        "value_heads": value_heads,
        "log_total": log_total,
        "mixed": mixed,
        "norm_two_back": norm_two_back,
        "hidden_two": hidden_two,
        "gelu_back": gelu_back,
        "active_low": active_low,
    }
    return (result, saved_state)


def layer_backward(grad_result, saved_state, row, attend_mask):
    tokens_dev, model_width = grad_result.shape
    weight_qkv, weight_out, weight_up, weight_down, gains = unpack(row, model_width, FF)
    seg_count = tokens_dev // SEG
    head_dim = model_width // HEADS
    score_scale = head_dim ** (-0.5)
    weight_kv = weight_qkv[:, model_width:]
    grad_down = grad_result.astype(jnp.bfloat16)
    downproj_grad = jnp.einsum(
        "tf,td->fd", saved_state["active_low"], grad_down, preferred_element_type=jnp.float32
    )
    grad_active = jnp.einsum(
        "td,fd->tf", grad_down, weight_down, preferred_element_type=jnp.float32
    )
    (grad_up,) = saved_state["gelu_back"](grad_active)
    grad_up_low = grad_up.astype(jnp.bfloat16)
    upproj_grad = jnp.einsum(
        "td,tf->df", saved_state["hidden_two"], grad_up_low, preferred_element_type=jnp.float32
    )
    grad_hidden_two = jnp.einsum(
        "tf,df->td", grad_up_low, weight_up, preferred_element_type=jnp.float32
    )
    grad_after_norm, gain_two_grad = saved_state["norm_two_back"](grad_hidden_two)
    grad_after = grad_result + grad_after_norm
    grad_attn_low = grad_after.astype(jnp.bfloat16)
    outproj_grad = jnp.einsum(
        "td,te->de", saved_state["mixed"], grad_attn_low, preferred_element_type=jnp.float32
    )
    grad_mixed = (
        jnp.einsum("te,de->td", grad_attn_low, weight_out, preferred_element_type=jnp.float32)
        .astype(jnp.bfloat16)
        .reshape(seg_count, SEG, HEADS, head_dim)
    )
    query_heads = saved_state["query_heads"]
    key_heads = saved_state["key_heads"]
    value_heads = saved_state["value_heads"]
    key_count = key_heads.shape[1]
    scores = score_heads(query_heads, key_heads, attend_mask, score_scale)
    soft = jnp.exp(scores - saved_state["log_total"])
    soft_low = soft.astype(jnp.bfloat16)
    grad_soft = jnp.einsum(
        "sqhe,skhe->shqk", grad_mixed, value_heads, preferred_element_type=jnp.float32
    )
    grad_values = jnp.einsum(
        "shqk,sqhe->skhe", soft_low, grad_mixed, preferred_element_type=jnp.float32
    )
    grad_scores = (soft * (grad_soft - jnp.sum(grad_soft * soft, axis=-1, keepdims=True))).astype(
        jnp.bfloat16
    )
    grad_queries = (
        jnp.einsum("shqk,skhe->sqhe", grad_scores, key_heads, preferred_element_type=jnp.float32)
        * score_scale
    )
    grad_keys = (
        jnp.einsum("shqk,sqhe->skhe", grad_scores, query_heads, preferred_element_type=jnp.float32)
        * score_scale
    )
    grad_rows = jnp.concatenate(
        [
            grad_keys.reshape(seg_count, key_count, model_width),
            grad_values.reshape(seg_count, key_count, model_width),
        ],
        axis=-1,
    )
    window_rows = WIN * SEG
    grad_windows = grad_rows[:, :window_rows]
    grad_memory = (
        grad_rows[:, window_rows:].reshape(seg_count * MEM, 2 * model_width).astype(jnp.bfloat16)
    )
    grad_extended = jnp.zeros((tokens_dev + (WIN - 1) * SEG, 2 * model_width), jnp.float32)
    for block_at in range(WIN):
        grad_extended = grad_extended.at[SEG * block_at : SEG * block_at + tokens_dev].add(
            grad_windows[:, SEG * block_at : SEG * (block_at + 1)].reshape(
                tokens_dev, 2 * model_width
            )
        )
    grad_left = grad_extended[:LEFT]
    grad_keyvals = grad_extended[LEFT : LEFT + tokens_dev]
    grad_right = grad_extended[LEFT + tokens_dev : LEFT + tokens_dev + RIGHT]
    memory_grad = jnp.einsum(
        "md,me->de", saved_state["chosen"], grad_memory, preferred_element_type=jnp.float32
    )
    grad_chosen = jnp.einsum(
        "me,de->md", grad_memory, weight_kv, preferred_element_type=jnp.float32
    )
    grad_summaries = (
        jnp.zeros((saved_state["summary_count"], model_width), jnp.float32)
        .at[saved_state["flat_index"]]
        .add(grad_chosen)
    )
    grad_summary = lax.psum_scatter(grad_summaries, "ta", scatter_dimension=0, tiled=True)
    from_next = from_behind(grad_left.astype(jnp.bfloat16), "ta", -1).astype(grad_left.dtype)
    from_prev = from_behind(grad_right, "ta", 1)
    grad_keyvals = grad_keyvals.at[:RIGHT].add(from_prev)
    grad_keyvals = grad_keyvals.at[tokens_dev - LEFT :].add(from_next)
    grad_projected = jnp.concatenate(
        [grad_queries.reshape(tokens_dev, model_width), grad_keyvals], axis=1
    ).astype(jnp.bfloat16)
    qkv_grad = jnp.einsum(
        "td,te->de", saved_state["hidden_one"], grad_projected, preferred_element_type=jnp.float32
    )
    qkv_grad = qkv_grad.at[:, model_width:].add(memory_grad)
    grad_hidden_one = jnp.einsum(
        "te,de->td", grad_projected, weight_qkv, preferred_element_type=jnp.float32
    )
    spread_summary = jnp.broadcast_to(
        (grad_summary / SEG)[:, None, :], (seg_count, SEG, model_width)
    ).reshape(tokens_dev, model_width)
    grad_hidden_one = grad_hidden_one + spread_summary
    grad_stream_norm, gain_one_grad = saved_state["norm_one_back"](grad_hidden_one)
    residual_gradient = grad_after + grad_stream_norm
    row_grad = jnp.concatenate(
        [
            qkv_grad.reshape(-1),
            outproj_grad.reshape(-1),
            upproj_grad.reshape(-1),
            downproj_grad.reshape(-1),
            gain_one_grad,
            gain_two_grad,
        ]
    )
    return (residual_gradient, row_grad)


def per_device(frames, cotangent, mem_index, master, moment, second, average):
    layer_count = master.shape[0]
    collected_rows = lax.all_gather(master.astype(jnp.bfloat16), "ta", axis=1, tiled=True)
    tokens_dev = frames.shape[0]
    total_frames = tokens_dev * lax.axis_size("ta")
    first_seg = lax.axis_index("ta") * (tokens_dev // SEG)
    attend_mask = key_masks(first_seg, tokens_dev // SEG, total_frames, mem_index)
    stream = frames.astype(jnp.float32)
    saved_states = []
    for layer_lookup in range(layer_count):
        stream, saved_state = layer_forward(
            stream, collected_rows[layer_lookup], mem_index, attend_mask
        )
        saved_states.append(saved_state)
    residual_gradient = cotangent
    row_grads = [None] * layer_count
    for layer_lookup in reversed(range(layer_count)):
        residual_gradient, row_grad = layer_backward(
            residual_gradient, saved_states[layer_lookup], collected_rows[layer_lookup], attend_mask
        )
        row_grads[layer_lookup] = row_grad
    stacked_rows = jnp.stack(row_grads, axis=0)
    reduced, gain_reduced = (
        lax.psum_scatter(stacked_rows, "ta", scatter_dimension=1, tiled=True),
        lax.psum_scatter(
            stacked_rows[:, stacked_rows.shape[1] - 2 * D :], "ta", scatter_dimension=1, tiled=True
        ),
    )
    new_moment = 0.5 * moment + 0.5 * reduced
    new_second = 0.5 * second + 0.5 * reduced * reduced
    correction = 1.0 - 0.5**STEP
    update = new_moment / correction / (jnp.sqrt(new_second / correction) + 1e-08) + 0.1 * master
    new_master = master - 0.08 * update
    new_average = 0.9 * average + 0.1 * new_master
    return (
        stream,
        residual_gradient,
        gain_reduced,
        new_moment,
        new_second,
        new_master,
        new_average,
    )


def solution(mesh):
    placed = (
        P("ta", None),
        P("ta", None),
        P("ta", None),
        P(None, "ta"),
        P(None, "ta"),
        P(None, "ta"),
        P(None, "ta"),
    )
    return jax.shard_map(
        per_device,
        mesh=mesh,
        in_specs=placed,
        out_specs=(
            P("ta", None),
            P("ta", None),
            P(None, "ta"),
            P(None, "ta"),
            P(None, "ta"),
            P(None, "ta"),
            P(None, "ta"),
        ),
        check_vma=False,
    )
```

profile of v0, /device:TPU:20, one launch (start us, length us, event | category | flops | bytes accessed | tf_op | source)
XLA Modules:
  0.0 1421.4 jit_solution(17353708938579452764)
XLA Ops:
  13.0 94.7 %all-gather.9.cloned.1.call-done = bf16[32,98336,2]{1,2,0:T(2,128)(2,1)} async-done(((bf16[1,98336,2]{1,2,0:T(2,128)(2,1)}), bf16[32,98336,2]{1,2,0:T(2,128)(2,1)}) %all-gather.9.cloned.1.call-update) | async-done | bytes 12587024 | tf_op jit(solution)/shard_map/all_gather | solution.py:278
  107.7 11.5 copy.138
  119.2 23.8 %reshape.850 = bf16[6293504]{0:T(1024)(128)(2,1)} reshape(bf16[2,32,98336]{2,1,0:T(8,128)(2,1)} %bitcast.144) | data formatting | bytes 25174016
  143.0 15.7 %reshape.851 = bf16[2,3146752]{1,0:T(2,128)(2,1)} reshape(bf16[6293504]{0:T(1024)(128)(2,1)} %reshape.850) | data formatting | bytes 25174016
  158.7 11.1 bitcast_bitcast_fusion
  169.8 48.5 %slice_reduce_fusion.1 = (bf16[1048576]{0:T(1024)(128)(2,1)}, bf16[1048576]{0:T(1024)(128)(2,1)}, bf16[1048576]{0:T(1024)(128)(2,1)}, bf16[1048576]{0:T(1024)(128)(2,1)}) fusion(bf16[2,3146752]{1,0:T(2,128)(2,1)S(1)} %bitcast_bitcast_fusion), kind=kLoop, calls=%fused_computation.42 | loop fusion | bytes 16777216 | tf_op jit(solution)/shard_map/slice | solution.py:46
  219.5 36.2 %slice_reduce_fusion.4 = (bf16[786432]{0:T(1024)(128)(2,1)}, bf16[786432]{0:T(1024)(128)(2,1)}) fusion(bf16[2,3146752]{1,0:T(2,128)(2,1)} %copy-done), kind=kLoop, calls=%fused_computation.49 | loop fusion | bytes 6291456 | tf_op jit(solution)/shard_map/slice | solution.py:46
  267.6 13.4 slice_reduce_fusion.6
  283.8 4.8 reshape.749
  290.9 5.6 fusion.45
  304.3 4.9 fusion.121
  309.2 5.6 copy.71
  320.0 5.6 copy.69
  372.9 5.6 fusion.44
  382.9 11.5 all-gather.7.cloned.1.call-done
  401.4 4.9 fusion.120
  406.3 5.5 copy.75
  418.4 5.5 copy.74
  423.9 5.2 fusion.33
  474.2 8.1 copy.85
  482.3 8.1 copy.84
  524.9 5.1 copy.111
  566.6 77.4 %reduce-scatter.7.cloned.1.call-done = f32[32,512]{1,0:T(8,128)} async-done(((f32[1024,512]{1,0:T(8,128)}), f32[32,512]{1,0:T(8,128)}) %reduce-scatter.7.cloned.1.call-update) | async-done | bytes 65552 | tf_op jit(solution)/shard_map/reduce_scatter | solution.py:242
  687.2 8.1 copy.94
  695.3 8.1 copy.93
  736.8 5.1 copy.108
  776.1 70.5 %reduce-scatter.9.cloned.1.call-done = f32[32,512]{1,0:T(8,128)} async-done(((f32[1024,512]{1,0:T(8,128)}), f32[32,512]{1,0:T(8,128)}) %reduce-scatter.9.cloned.1.call-update) | async-done | bytes 65552 | tf_op jit(solution)/shard_map/reduce_scatter | solution.py:242
  855.8 26.0 %pad_maximum_fusion = f32[2,3146752]{1,0:T(2,128)} fusion(f32[1,3146752]{1,0:T(1,128)} %bitcast.45, f32[1,3146752]{1,0:T(1,128)} %bitcast.44), kind=kLoop, calls=%fused_computation.5 | loop fusion | flops 6293504 | bytes 50348032 | tf_op jit(solution)/shard_map/stack | solution.py:297
  883.1 5.5 convolution_add_fusion.3
  889.9 96.2 %reduce-scatter.11.cloned.1.call-done = f32[32,2]{1,0:T(8,128)} async-done(((f32[1024,2]{1,0:T(8,128)}), f32[32,2]{1,0:T(8,128)}) %reduce-scatter.11.cloned.1.call-update) | async-done | bytes 272
  987.5 421.2 %all-reduce.5.cloned.1.call-done = f32[2,3146752]{1,0:T(2,128)} async-done(((f32[2,3146752]{1,0:T(2,128)}), f32[2,3146752]{1,0:T(2,128)}) %all-reduce.5.cloned.1.call-update) | async-done | bytes 25174032
  1408.7 5.4 multiply_add_fusion.1
  (424 shorter events, 341.3 us)
Async XLA Ops:
  7.2 100.5 %all-gather.9.cloned.1.call-start = ((), (), s32[]{:S(2)}) async-start(), calls=%async_computation.7 | async-start | bytes 12993024 | tf_op jit(solution)/shard_map/all_gather | solution.py:278
  9.4 291.3 %all-gather.5.cloned.1.call-start = ((), (), s32[]{:S(2)}) async-start(), calls=%async_computation.3 | async-start | bytes 1081344 | tf_op jit(solution)/shard_map/all_gather | solution.py:91
  11.4 303.3 %copy-start.79 = (pred[32,68]{1,0:T(8,128)(4,1)}, pred[32,68]{1,0:T(8,128)(4,1)S(1)}, u32[]{:S(2)}) copy-start(pred[32,68]{1,0:T(8,128)(4,1)S(1)} %pad_add_fusion) | copy-start | bytes 6532
  12.7 247.3 %copy-start.77 = (f32[512]{0:T(512)}, f32[512]{0:T(512)S(1)}, u32[]{:S(2)}) copy-start(f32[512]{0:T(512)S(1)} %broadcast_multiply_fusion.7) | copy-start | bytes 6148
  13.0 106.2 %copy-start.87 = (f32[512]{0:T(512)}, f32[512]{0:T(512)S(1)}, u32[]{:S(2)}) copy-start(f32[512]{0:T(512)S(1)} %fusion.42) | copy-start | bytes 6148
  13.0 383.6 %copy-start.97 = (pred[128]{0:T(512)(128)(4,1)}, pred[128]{0:T(512)(128)(4,1)S(1)}, u32[]{:S(2)}) copy-start(pred[128]{0:T(512)(128)(4,1)S(1)} %compare_and_fusion) | copy-start | bytes 388
  13.0 246.9 %copy-start.81 = (f32[512]{0:T(512)}, f32[512]{0:T(512)S(1)}, u32[]{:S(2)}) copy-start(f32[512]{0:T(512)S(1)} %fusion.98) | copy-start | bytes 6148
  169.8 48.6 %copy-start = (bf16[2,3146752]{1,0:T(2,128)(2,1)}, bf16[2,3146752]{1,0:T(2,128)(2,1)S(1)}, u32[]{:S(2)}) copy-start(bf16[2,3146752]{1,0:T(2,128)(2,1)S(1)} %bitcast_bitcast_fusion) | copy-start | bytes 37761028
  218.4 41.5 %copy-start.83 = (f32[1,512]{1,0:T(1,128)}, f32[1,512]{1,0:T(1,128)S(1)}, u32[]{:S(2)}) copy-start(f32[1,512]{1,0:T(1,128)S(1)} %get-tuple-element.257) | copy-start | bytes 6148
  218.4 119.6 %copy-start.95 = (f32[1,512]{1,0:T(1,128)}, f32[1,512]{1,0:T(1,128)S(1)}, u32[]{:S(2)}) copy-start(f32[1,512]{1,0:T(1,128)S(1)} %get-tuple-element.231) | copy-start | bytes 6148
  219.4 174.9 %all-gather.7.cloned.1.call-start = ((), (), s32[]{:S(2)}) async-start(), calls=%async_computation.4 | async-start | bytes 1081344 | tf_op jit(solution)/shard_map/all_gather | solution.py:91
  262.4 28.5 %collective-permute-start.1 = (bf16[4,1024]{1,0:T(4,128)(2,1)S(1)}, bf16[4,1024]{1,0:T(4,128)(2,1)S(1)}, u32[]{:S(2)}, u32[]{:S(2)}) collective-permute-start(bf16[4,1024]{1,0:T(4,128)(2,1)S(1)} %slice.563), channel_id=1, source_target_pairs={{1,0},{2,1},{3,2},{4,3},{5,4},{6,5},{7,6},{8,7},{9,8},{10,9},{11,1... | collective-permute-start | bytes 24584 | tf_op jit(solution)/shard_map/ppermute | solution.py:20
  265.6 25.3 %collective-permute-start = (bf16[30,1024]{1,0:T(8,128)(2,1)S(1)}, bf16[30,1024]{1,0:T(8,128)(2,1)S(1)}, u32[]{:S(2)}, u32[]{:S(2)}) collective-permute-start(bf16[30,1024]{1,0:T(8,128)(2,1)S(1)} %slice.559), channel_id=1, source_target_pairs={{0,1},{1,2},{2,3},{3,4},{4,5},{5,6},{6,7},{7,8},{8,9},{9,10},{10,1... | collective-permute-start | bytes 184328 | tf_op jit(solution)/shard_map/ppermute | solution.py:20
  283.8 31.0 %copy-start.27 = (bf16[32,16,8,64]{3,2,1,0:T(8,128)(2,1)}, bf16[32,16,8,64]{3,2,1,0:T(8,128)(2,1)S(1)}, u32[]{:S(2)}) copy-start(bf16[32,16,8,64]{3,2,1,0:T(8,128)(2,1)S(1)} %reshape.744) | copy-start | bytes 1572868
  340.5 303.6 %reduce-scatter.7.cloned.1.call-start = ((), (), s32[]{:S(2)}) async-start(), calls=%async_computation.5 | async-start | bytes 2162688 | tf_op jit(solution)/shard_map/reduce_scatter | solution.py:242
  348.6 24.3 %collective-permute-start.3 = (bf16[4,1024]{1,0:T(4,128)(2,1)S(1)}, bf16[4,1024]{1,0:T(4,128)(2,1)S(1)}, u32[]{:S(2)}, u32[]{:S(2)}) collective-permute-start(bf16[4,1024]{1,0:T(4,128)(2,1)S(1)} %slice.580), channel_id=1, source_target_pairs={{1,0},{2,1},{3,2},{4,3},{5,4},{6,5},{7,6},{8,7},{9,8},{10,9},{11,1... | collective-permute-start | bytes 24584 | tf_op jit(solution)/shard_map/ppermute | solution.py:20
  353.2 19.8 %collective-permute-start.2 = (bf16[30,1024]{1,0:T(8,128)(2,1)S(1)}, bf16[30,1024]{1,0:T(8,128)(2,1)S(1)}, u32[]{:S(2)}, u32[]{:S(2)}) collective-permute-start(bf16[30,1024]{1,0:T(8,128)(2,1)S(1)} %slice.576), channel_id=1, source_target_pairs={{0,1},{1,2},{2,3},{3,4},{4,5},{5,6},{6,7},{7,8},{8,9},{9,10},{10,1... | collective-permute-start | bytes 184328 | tf_op jit(solution)/shard_map/ppermute | solution.py:20
  435.3 14.5 %copy-start.10 = (f32[512,512]{1,0:T(8,128)}, f32[512,512]{1,0:T(8,128)S(1)}, u32[]{:S(2)}) copy-start(f32[512,512]{1,0:T(8,128)S(1)} %get-tuple-element.243) | copy-start | bytes 3145732
  508.9 28.7 %collective-permute-start.4 = (f32[4,1024]{1,0:T(4,128)}, f32[4,1024]{1,0:T(4,128)}, u32[]{:S(2)}, u32[]{:S(2)}) collective-permute-start(f32[4,1024]{1,0:T(4,128)} %slice.602), channel_id=1, source_target_pairs={{0,1},{1,2},{2,3},{3,4},{4,5},{5,6},{6,7},{7,8},{8,9},{9,10},{10,1... | collective-permute-start | bytes 49160 | tf_op jit(solution)/shard_map/ppermute | solution.py:20
  533.3 313.3 %reduce-scatter.9.cloned.1.call-start = ((), (), s32[]{:S(2)}) async-start(), calls=%async_computation.6 | async-start | bytes 2162688 | tf_op jit(solution)/shard_map/reduce_scatter | solution.py:242
  533.3 6.5 collective-permute-start.5
  564.4 80.7 %copy-start.86 = (f32[512]{0:T(512)S(1)}, f32[512]{0:T(512)}, u32[]{:S(2)}) copy-start(f32[512]{0:T(512)} %copy-done.85) | copy-start | bytes 6148
  564.4 80.7 %copy-start.94 = (f32[512]{0:T(512)S(1)}, f32[512]{0:T(512)}, u32[]{:S(2)}) copy-start(f32[512]{0:T(512)} %copy-done.93) | copy-start | bytes 6148
  564.4 80.7 %copy-start.96 = (f32[1,512]{1,0:T(1,128)S(1)}, f32[1,512]{1,0:T(1,128)}, u32[]{:S(2)}) copy-start(f32[1,512]{1,0:T(1,128)} %copy-done.95) | copy-start | bytes 6148
  714.3 271.9 %reduce-scatter.11.cloned.1.call-start = ((), (), s32[]{:S(2)}) async-start(), calls=%async_computation.8 | async-start | bytes 540672
  721.3 24.6 %collective-permute-start.6 = (f32[4,1024]{1,0:T(4,128)S(1)}, f32[4,1024]{1,0:T(4,128)S(1)}, u32[]{:S(2)}, u32[]{:S(2)}) collective-permute-start(f32[4,1024]{1,0:T(4,128)S(1)} %slice.617), channel_id=1, source_target_pairs={{0,1},{1,2},{2,3},{3,4},{4,5},{5,6},{6,7},{7,8},{8,9},{9,10},{10,1... | collective-permute-start | bytes 49160 | tf_op jit(solution)/shard_map/ppermute | solution.py:20
  741.9 12.4 copy-start.82
  741.9 12.4 copy-start.84
  741.9 8.1 collective-permute-start.7
  773.8 73.8 %copy-start.67 = (bf16[512,1536]{1,0:T(8,128)(2,1)S(1)}, bf16[512,1536]{1,0:T(8,128)(2,1)}, u32[]{:S(2)}) copy-start(bf16[512,1536]{1,0:T(8,128)(2,1)} %reshape.734) | copy-start | bytes 4718596
  855.8 552.9 %all-reduce.5.cloned.1.call-start = ((), (), s32[]{:S(2)}) async-start(), calls=%async_computation.9 | async-start | bytes 50348032
  888.6 520.1 %copy-start.58 = (f32[2,98336]{1,0:T(2,128)S(1)}, f32[2,98336]{1,0:T(2,128)}, u32[]{:S(2)}) copy-start(f32[2,98336]{1,0:T(2,128)} %param.40) | copy-start | bytes 2360068
  (83 other events, 291.9 us)
Sparse Core Ops, SparseCore 0:
  11.5 96.1 all-gather.8
  219.5 51.5 all-gather.4
  340.6 53.6 all-gather.6
  533.4 110.6 reduce-scatter.6
  714.4 132.1 reduce-scatter.8
  855.9 130.1 reduce-scatter.10
  993.7 414.9 all-reduce.4
where the time goes:
time: 1440 us; the launch traced here: 1420 us
  waiting for transfers between devices  776 us (54%)
  local copies, waits for them, and re-layouts  390 us (27%)
  matrix products  123 us (9%)
  other arithmetic  91.9 us (6%)
  starting transfers between devices  25.2 us (2%)
  between operations  15.9 us (1%)
    unnamed x9, waiting for transfers between devices  517 us
    reduce_scatter x2, waiting for transfers between devices, layer_backward(): lax.psum_scatter(grad_summaries, 'ta', scatter_dimension=0, tiled=True)  148 us
    unnamed x230, local copies, waits for them, and re-layouts  130 us
    slice x3, local copies, waits for them, and re-layouts, unpack(): pieces.append(row[offset:offset + piece_size].reshape(shape))  98.1 us
    all_gather x1, waiting for transfers between devices, per_device(): lax.all_gather(master.astype(jnp.bfloat16), 'ta', axis=1, tiled=True)  94.7 us
  transfers between devices with their start and end apart: 15, of which 8 were waited for; matrix products, arithmetic and copies ran while one was open for 17% of the time, Pallas kernels for 0%

commit v1 on v0

v1 whole, which is shorter than its diff:
```python
import functools

import jax
import jax.numpy as jnp
from jax import lax
from jax.experimental import pallas as pl
from jax.experimental.pallas import tpu as pltpu
from jax.sharding import PartitionSpec as P

D = 512
HEADS = 8
FF = 2048
SEG = 16
LEFT = 30
RIGHT = 4
MEM = 4
STEP = 10
FIRST = 32
NEG = -1e30

TOK = 512
NSEG = TOK // SEG
LH = 32
RH = 16
EXT = LH + TOK + 2 * RH
ROWS = EXT + NSEG * MEM
BLK = 4
NBLK = NSEG // BLK
QB = BLK * SEG
KB = 128
WB = KB - BLK * MEM

TILES = 1536
QKV0, WO0, WU0, WD0 = 0, 384, 512, 1024
MATS = TILES * 16 * 128

F32 = jnp.float32
BF16 = jnp.bfloat16
VM = pl.BlockSpec(memory_space=pltpu.VMEM)
SM = pl.BlockSpec(memory_space=pltpu.SMEM)
ANYS = pl.BlockSpec(memory_space=pl.ANY)


def mm(a, b):
    return lax.dot_general(a, b, (((1,), (0,)), ((), ())), preferred_element_type=F32)


def mm_nt(a, b):
    return lax.dot_general(a, b, (((1,), (1,)), ((), ())), preferred_element_type=F32)


def mm_tn(a, b):
    return lax.dot_general(a, b, (((0,), (0,)), ((), ())), preferred_element_type=F32)


def wblk(w, base, nj, i0, ni, j0, nj_take):
    cols = [
        jnp.concatenate([w[base + (i0 + i) * nj + j0 + j] for i in range(ni)], axis=0)
        for j in range(nj_take)
    ]
    return cols[0] if nj_take == 1 else jnp.concatenate(cols, axis=1)


def gain_row(g_ref, which):
    g = g_ref[...].astype(F32)
    return jnp.concatenate([g[4 * which + k : 4 * which + k + 1] for k in range(4)], axis=1)


def norm_parts(v):
    mean = jnp.mean(v, axis=-1, keepdims=True)
    cen = v - mean
    rstd = lax.rsqrt(jnp.mean(cen * cen, axis=-1, keepdims=True) + 1e-05)
    return cen * rstd, rstd


def norm_back(dh, xhat, rstd, gain):
    dx = dh * gain
    return rstd * (
        dx
        - jnp.mean(dx, axis=-1, keepdims=True)
        - xhat * jnp.mean(dx * xhat, axis=-1, keepdims=True)
    )


def head_of_layer(x, gain):
    xhat, _ = norm_parts(x)
    h1 = (xhat * gain).astype(BF16)
    summ = jnp.sum(h1.astype(F32).reshape(NSEG, SEG, D), axis=1) * (1.0 / SEG)
    return h1, summ.astype(BF16)


def first_kernel(x_ref, g_ref, h1_ref, sum_ref):
    h1, summ = head_of_layer(x_ref[...].astype(F32), gain_row(g_ref, 0))
    h1_ref[...] = h1
    sum_ref[...] = summ


def lane_lo(rows):
    return lax.broadcasted_iota(jnp.int32, (rows, 128), 1) < 64


def split_heads(m, lo):
    z = jnp.zeros_like(m)
    return jnp.concatenate([jnp.where(lo, m, z), jnp.where(lo, z, m)], axis=0)


def onehot_of(loc_ref):
    ids = lax.broadcasted_iota(jnp.int32, (NSEG * MEM, 128), 1)
    return jnp.where(loc_ref[...] == ids, 1.0, 0.0).astype(BF16)


def fwd_kernel(
    x_ref, h1_ref, hl_ref, hr_ref, tab_ref, loc_ref, col_ref, g_ref, gn_ref, w_ref,
    out_ref, h1n_ref, sumn_ref, hx_ref, q_ref, kv_ref, p_ref, o_ref, a_ref, h2_ref, gp_ref, act_ref,
    *, last,
):
    hx_ref[0:LH] = hl_ref[...]
    hx_ref[LH : LH + TOK] = h1_ref[...]
    hx_ref[LH + TOK : LH + TOK + RH] = hr_ref[...]
    hx_ref[LH + TOK + RH : EXT] = jnp.zeros((RH, D), BF16)
    hx_ref[EXT:ROWS] = mm(onehot_of(loc_ref), tab_ref[...]).astype(BF16)
    for jp in range(6):
        wc = wblk(w_ref, QKV0, 12, 0, 32, 2 * jp, 2)
        if jp < 2:
            q_ref[:, 256 * jp : 256 * jp + 256] = mm(h1_ref[...], wc).astype(BF16)
        else:
            c0 = 256 * (jp - 2)
            kv_ref[:, c0 : c0 + 256] = mm(hx_ref[...], wc).astype(BF16)

    qi = lax.broadcasted_iota(jnp.int32, (QB, KB), 0) // SEG
    ci = lax.broadcasted_iota(jnp.int32, (QB, KB), 1)
    off = ci - SEG * qi - (LH - LEFT)
    near = jnp.where((off >= 0) & (off < LEFT + SEG + RIGHT) & (ci < WB), 1.0, 0.0)
    band = near + jnp.where((ci >= WB) & ((ci - WB) // MEM == qi), 1.0, 0.0)
    lo = lane_lo(KB)

    def block(b, carry):
        r0 = pl.multiple_of(b * QB, QB)
        m0 = pl.multiple_of(EXT + b * (BLK * MEM), BLK * MEM)
        vis = band * col_ref[pl.ds(b, 1), :] > 0.5
        for p in range(4):
            kc = jnp.concatenate(
                [kv_ref[pl.ds(r0, WB), 128 * p : 128 * p + 128],
                 kv_ref[pl.ds(m0, BLK * MEM), 128 * p : 128 * p + 128]], axis=0)
            vc = jnp.concatenate(
                [kv_ref[pl.ds(r0, WB), D + 128 * p : D + 128 * p + 128],
                 kv_ref[pl.ds(m0, BLK * MEM), D + 128 * p : D + 128 * p + 128]], axis=0)
            qp = q_ref[pl.ds(r0, QB), 128 * p : 128 * p + 128]
            s = mm_nt(qp, split_heads(kc, lo)) * 0.125
            halves = []
            for h in range(2):
                sh = jnp.where(vis, s[:, 128 * h : 128 * h + 128], NEG)
                e = jnp.exp(sh - jnp.max(sh, axis=-1, keepdims=True))
                halves.append(e / jnp.sum(e, axis=-1, keepdims=True))
            pb = jnp.concatenate(halves, axis=1).astype(BF16)
            p_ref[b * 4 + p] = pb
            o_ref[pl.ds(r0, QB), 128 * p : 128 * p + 128] = mm(pb, split_heads(vc, lo)).astype(BF16)
        return carry

    lax.fori_loop(0, NBLK, block, 0)

    a = x_ref[...].astype(F32) + mm(o_ref[...], wblk(w_ref, WO0, 4, 0, 32, 0, 4))
    a_ref[...] = a
    xhat, _ = norm_parts(a)
    h2_ref[...] = (xhat * gain_row(g_ref, 1)).astype(BF16)
    out_ref[...] = a

    def ffn(c, carry):
        u = mm(h2_ref[...], wblk(w_ref, WU0, 16, 0, 32, 2 * c, 2))
        cc = 0.7978845608028654
        u2 = u * u
        t = jnp.tanh(cc * u * (1.0 + 0.044715 * u2))
        act = (0.5 * u * (1.0 + t)).astype(BF16)
        gp = 0.5 * (1.0 + t) + 0.5 * u * (1.0 - t * t) * cc * (1.0 + 3 * 0.044715 * u2)
        c0 = pl.multiple_of(c * 256, 256)
        act_ref[:, pl.ds(c0, 256)] = act
        gp_ref[:, pl.ds(c0, 256)] = gp.astype(BF16)
        out_ref[...] += mm(act, wblk(w_ref, WD0, 4, 16 * c, 16, 0, 4))
        return carry

    lax.fori_loop(0, FF // 256, ffn, 0)
    if not last:
        h1n, sumn = head_of_layer(out_ref[...], gain_row(gn_ref, 0))
        h1n_ref[...] = h1n
        sumn_ref[...] = sumn
    else:
        h1n_ref[...] = jnp.zeros_like(h1n_ref)
        sumn_ref[...] = jnp.zeros_like(sumn_ref)


def sds(shape, dtype):
    return jax.ShapeDtypeStruct(shape, dtype)


PARAMS = dict(vmem_limit_bytes=56 * 1024 * 1024)


def run(kernel, outs, ins, specs=None, scratch=(), flops=0, nbytes=0, **kw):
    return pl.pallas_call(
        kernel,
        out_shape=outs,
        in_specs=specs or [VM] * len(ins),
        out_specs=jax.tree.map(lambda _: VM, outs) if "out_specs" not in kw else kw["out_specs"],
        scratch_shapes=list(scratch),
        compiler_params=pltpu.CompilerParams(**PARAMS),
        cost_estimate=pl.CostEstimate(flops=flops, bytes_accessed=nbytes, transcendentals=0),
    )(*ins)


def bwd_kernel(
    dx_ref, w_ref, g_ref, loc_ref, q_ref, kv_ref, p_ref, a_ref, gp_ref,
    da_ref, dxb_ref, dub_ref, dab_ref, dq_ref, dkvb_ref, dh_ref, dtab_ref, dgb_ref,
    dkv_ref, dob_ref,
):
    dxb_ref[...] = dx_ref[...].astype(BF16)
    da_ref[...] = jnp.zeros_like(da_ref)

    def ffn(c, carry):
        c0 = pl.multiple_of(c * 256, 256)
        dact = mm_nt(dxb_ref[...], wblk(w_ref, WD0, 4, 16 * c, 16, 0, 4))
        du = (dact * gp_ref[:, pl.ds(c0, 256)].astype(F32)).astype(BF16)
        dub_ref[:, pl.ds(c0, 256)] = du
        da_ref[...] += mm_nt(du, wblk(w_ref, WU0, 16, 0, 32, 2 * c, 2))
        return carry

    lax.fori_loop(0, FF // 256, ffn, 0)
    xhat, rstd = norm_parts(a_ref[...])
    dh2 = da_ref[...]
    dgb_ref[...] = jnp.sum(dh2 * xhat, axis=0, keepdims=True)
    da = dx_ref[...] + norm_back(dh2, xhat, rstd, gain_row(g_ref, 1))
    da_ref[...] = da
    dab_ref[...] = da.astype(BF16)
    dob_ref[...] = mm_nt(dab_ref[...], wblk(w_ref, WO0, 4, 0, 32, 0, 4)).astype(BF16)

    dkv_ref[...] = jnp.zeros_like(dkv_ref)
    lo = lane_lo(KB)

    def block(b, carry):
        r0 = pl.multiple_of(b * QB, QB)
        m0 = pl.multiple_of(EXT + b * (BLK * MEM), BLK * MEM)
        for p in range(4):
            kc0, vc0 = 128 * p, D + 128 * p
            kc = jnp.concatenate(
                [kv_ref[pl.ds(r0, WB), kc0 : kc0 + 128], kv_ref[pl.ds(m0, BLK * MEM), kc0 : kc0 + 128]], axis=0)
            vc = jnp.concatenate(
                [kv_ref[pl.ds(r0, WB), vc0 : vc0 + 128], kv_ref[pl.ds(m0, BLK * MEM), vc0 : vc0 + 128]], axis=0)
            qp = q_ref[pl.ds(r0, QB), kc0 : kc0 + 128]
            dop = dob_ref[pl.ds(r0, QB), kc0 : kc0 + 128]
            pb = p_ref[b * 4 + p]
            dp = mm_nt(dop, split_heads(vc, lo))
            dv2 = mm_tn(pb, dop)
            ds = []
            for h in range(2):
                ph = pb[:, 128 * h : 128 * h + 128].astype(F32)
                dph = dp[:, 128 * h : 128 * h + 128]
                ds.append(ph * (dph - jnp.sum(dph * ph, axis=-1, keepdims=True)))
            dsb = jnp.concatenate(ds, axis=1).astype(BF16)
            dq_ref[pl.ds(r0, QB), kc0 : kc0 + 128] = (mm(dsb, split_heads(kc, lo)) * 0.125).astype(BF16)
            dk2 = mm_tn(dsb, qp) * 0.125
            dk = jnp.where(lo, dk2[:128], dk2[128:])
            dv = jnp.where(lo, dv2[:128], dv2[128:])
            dkv_ref[pl.ds(r0, WB), kc0 : kc0 + 128] += dk[:WB]
            dkv_ref[pl.ds(r0, WB), vc0 : vc0 + 128] += dv[:WB]
            dkv_ref[pl.ds(m0, BLK * MEM), kc0 : kc0 + 128] = dk[WB:]
            dkv_ref[pl.ds(m0, BLK * MEM), vc0 : vc0 + 128] = dv[WB:]
        return carry

    lax.fori_loop(0, NBLK, block, 0)
    dkvb_ref[...] = dkv_ref[...].astype(BF16)

    dh_ref[...] = jnp.zeros_like(dh_ref)
    for jp in range(6):
        wc = wblk(w_ref, QKV0, 12, 0, 32, 2 * jp, 2)
        if jp < 2:
            dh_ref[LH : LH + TOK] += mm_nt(dq_ref[:, 256 * jp : 256 * jp + 256], wc)
        else:
            c0 = 256 * (jp - 2)
            dh_ref[...] += mm_nt(dkvb_ref[:, c0 : c0 + 256], wc)
    dch = dh_ref[EXT:ROWS]
    hi = dch.astype(BF16)
    oh = onehot_of(loc_ref)
    dtab_ref[...] = mm_tn(oh, hi) + mm_tn(oh, (dch - hi.astype(F32)).astype(BF16))


def dw_kernel(hx_ref, h1_ref, dq_ref, dkv_ref, o_ref, dab_ref, h2_ref, dub_ref, act_ref, dxb_ref, g_ref):
    def put(val, base, nj, i0, j0):
        v = val.astype(BF16)
        for i in range(val.shape[0] // 16):
            for j in range(val.shape[1] // 128):
                g_ref[base + (i0 + i) * nj + j0 + j] = v[16 * i : 16 * i + 16, 128 * j : 128 * j + 128]

    def down(c, carry):
        c0 = pl.multiple_of(c * 256, 256)
        put(mm_tn(act_ref[:, pl.ds(c0, 256)], dxb_ref[...]), WD0, 4, 16 * c, 0)
        return carry

    lax.fori_loop(0, FF // 256, down, 0)

    def up(c, carry):
        c0 = pl.multiple_of(c * 256, 256)
        put(mm_tn(h2_ref[...], dub_ref[:, pl.ds(c0, 256)]), WU0, 16, 0, 2 * c)
        return carry

    lax.fori_loop(0, FF // 256, up, 0)
    for j in range(2):
        put(mm_tn(o_ref[...], dab_ref[:, 256 * j : 256 * j + 256]), WO0, 4, 0, 2 * j)
        put(mm_tn(h1_ref[...], dq_ref[:, 256 * j : 256 * j + 256]), QKV0, 12, 0, 2 * j)
    for j in range(4):
        put(mm_tn(hx_ref[...], dkv_ref[:, 256 * j : 256 * j + 256]), QKV0, 12, 0, 4 + 2 * j)


def nb_kernel(dh_ref, hal_ref, har_ref, dsum_ref, x_ref, da_ref, g_ref, dx_ref, dga_ref, acc_ref):
    acc_ref[...] = dh_ref[LH : LH + TOK]
    acc_ref[TOK - LH : TOK] += hal_ref[...]
    acc_ref[0:RH] += har_ref[...]
    for s in range(NSEG):
        acc_ref[SEG * s : SEG * s + SEG] += dsum_ref[s : s + 1, :] * (1.0 / SEG)
    xhat, rstd = norm_parts(x_ref[...].astype(F32))
    dh = acc_ref[...]
    dga_ref[...] = jnp.sum(dh * xhat, axis=0, keepdims=True)
    dx_ref[...] = da_ref[...] + norm_back(dh, xhat, rstd, gain_row(g_ref, 0))


def shift(value, by, n):
    return lax.ppermute(value, "ta", [(i, i + by) for i in range(n) if 0 <= i + by < n])


def from_first(value, me, n, root=0):
    step = n // 2
    while step:
        got = lax.ppermute(value, "ta", [(i ^ root, (i + step) ^ root) for i in range(0, n, 2 * step)])
        value = jnp.where(((me ^ root) % (2 * step)) == step, got, value)
        step //= 2
    return value


def to_first(value, me, n):
    step = 1
    while step < n:
        value = value + lax.ppermute(value, "ta", [(i + step, i) for i in range(0, n, 2 * step)])
        step *= 2
    return value


def sum_all(value, n):
    step = 1
    while step < n:
        value = value + lax.ppermute(value, "ta", [(i, i ^ step) for i in range(n)])
        step *= 2
    return value


def tiles_of(rows, ni, nj):
    return rows.reshape(ni, 16, nj, 128).transpose(0, 2, 1, 3).reshape(ni * nj, 16, 128)


def rows_of(tiles, ni, nj):
    return tiles.reshape(ni, nj, 16, 128).transpose(0, 2, 1, 3).reshape(ni * nj * 16, 128)


PIECES = ((QKV0, 32, 12), (WO0, 32, 4), (WU0, 32, 16), (WD0, 128, 4))


def gather_plain(aligned):
    full = lax.all_gather(aligned.reshape(-1, 128), "ta", axis=0, tiled=True)
    return jnp.concatenate(
        [tiles_of(full[16 * b : 16 * (b + ni * nj)], ni, nj) for b, ni, nj in PIECES], axis=0
    )


def reduce_plain(tiles):
    full = jnp.concatenate([rows_of(tiles[b : b + ni * nj], ni, nj) for b, ni, nj in PIECES], axis=0)
    return lax.psum_scatter(full, "ta", scatter_dimension=0, tiled=True).astype(F32).reshape(-1)


def per_device(frames, cotangent, mem_index, master, moment, second, average):
    n = lax.axis_size("ta")
    me = lax.axis_index("ta")
    layers, share = master.shape
    step = 2 * D // n
    tail = shift(master[:, share - 2 * D :], 1, n)
    ext = jnp.concatenate([tail, master], axis=1)
    aligned = lax.dynamic_slice(ext, (0, 2 * D - step * me), (layers, MATS // n)).astype(BF16)
    gains = from_first(master[:, share - 2 * D :].astype(BF16).reshape(layers, 8, 128), me, n, n - 1)
    weights = [gather_plain(aligned[l]) for l in range(layers)]

    first_seg = me * NSEG
    seg_ids = first_seg + jnp.arange(NSEG, dtype=jnp.int32)
    slot = jnp.arange(MEM, dtype=jnp.int32)
    loc = jnp.where(slot[None, :] == 0, mem_index, mem_index - first_seg + 96).reshape(-1, 1)
    pos = me * TOK - LH + QB * jnp.arange(NBLK)[:, None] + jnp.arange(WB)[None, :]
    col = jnp.concatenate(
        [(pos >= 0) & (pos < n * TOK), (mem_index < seg_ids[:, None]).reshape(NBLK, BLK * MEM)], axis=1
    ).astype(F32)

    h1, summ = run(first_kernel, (sds((TOK, D), BF16), sds((NSEG, D), BF16)), (frames, gains[0]))
    x = frames
    saved = []
    for l in range(layers):
        hl = shift(h1[TOK - LH :], 1, n)
        hr = shift(h1[:RH], -1, n)
        table = jnp.concatenate(
            [from_first(summ, me, n), shift(summ, 2, n), shift(summ, 1, n), summ], axis=0
        )
        outs = (
            sds((TOK, D), F32), sds((TOK, D), BF16), sds((NSEG, D), BF16), sds((ROWS, D), BF16),
            sds((TOK, D), BF16), sds((ROWS, 2 * D), BF16), sds((NBLK * 4, QB, 256), BF16), sds((TOK, D), BF16),
            sds((TOK, D), F32), sds((TOK, D), BF16), sds((TOK, FF), BF16), sds((TOK, FF), BF16),
        )
        res = run(
            functools.partial(fwd_kernel, last=l == layers - 1),
            outs,
            (x, h1, hl, hr, table, loc, col, gains[l], gains[min(l + 1, layers - 1)], weights[l]),
            flops=3 * 10**9, nbytes=30 * 10**6,
        )
        saved.append((x, h1) + tuple(res[3:]))
        x, h1, summ = res[:3]
    output = x

    dx = cotangent
    reduced = [None] * layers
    gain_rows = [None] * layers
    for l in reversed(range(layers)):
        xin, h1, hx, q, kv, prob, o, a, h2, gp, act = saved[l]
        outs = (
            sds((TOK, D), F32), sds((TOK, D), BF16), sds((TOK, FF), BF16), sds((TOK, D), BF16), sds((TOK, D), BF16),
            sds((ROWS, 2 * D), BF16), sds((ROWS, D), F32), sds((128, D), F32), sds((1, D), F32),
        )
        da, dxb, dub, dab, dq, dkvb, dh, dtab, dgb = run(
            bwd_kernel, outs, (dx, weights[l], gains[l], loc, q, kv, prob, a, gp),
            scratch=[pltpu.VMEM((ROWS, 2 * D), F32), pltpu.VMEM((TOK, D), BF16)],
            flops=4 * 10**9, nbytes=30 * 10**6,
        )
        grads = run(
            dw_kernel, sds((TILES, 16, 128), BF16), (hx, h1, dq, dkvb, o, dab, h2, dub, act, dxb),
            flops=4 * 10**9, nbytes=30 * 10**6,
        )
        reduced[l] = reduce_plain(grads)
        hal = shift(dh[:LH], -1, n)
        har = shift(dh[LH + TOK : LH + TOK + RH], 1, n)
        root = to_first(dtab[:NSEG], me, n)
        dsum = jnp.where(me == 0, root, 0.0) + shift(dtab[32:64], -2, n) + shift(dtab[64:96], -1, n) + dtab[96:]
        dx, dga = run(
            nb_kernel, (sds((TOK, D), F32), sds((1, D), F32)), (dh, hal, har, dsum, xin, da, gains[l]),
            scratch=[pltpu.VMEM((TOK, D), F32)], flops=10**6, nbytes=6 * 10**6,
        )
        gain_rows[l] = jnp.concatenate([dga, dgb], axis=1)

    gsum = sum_all(jnp.concatenate(gain_rows, axis=0), n)
    own = jnp.stack(reduced)
    head = jnp.where(me == n - 1, gsum, shift(own[:, : 2 * D], -1, n))
    grad = lax.dynamic_slice(jnp.concatenate([own, head], axis=1), (0, step * me), (layers, share))
    gain_out = lax.dynamic_slice(gsum, (0, step * me), (layers, step))
    new_moment = 0.5 * moment + 0.5 * grad
    new_second = 0.5 * second + 0.5 * grad * grad
    correction = 1.0 - 0.5**STEP
    update = new_moment / correction / (jnp.sqrt(new_second / correction) + 1e-08) + 0.1 * master
    new_master = master - 0.08 * update
    new_average = 0.9 * average + 0.1 * new_master
    return (output, dx, gain_out, new_moment, new_second, new_master, new_average)


def solution(mesh):
    rows, flat = P("ta", None), P(None, "ta")
    return jax.shard_map(
        per_device,
        mesh=mesh,
        in_specs=(rows, rows, rows, flat, flat, flat, flat),
        out_specs=(rows, rows, flat, flat, flat, flat, flat),
        check_vma=False,
    )
```

time: 1440 us -> 588 us (0.41)
  waiting for transfers between devices: 776 us -> 138 us
  local copies, waits for them, and re-layouts: 390 us -> 69.4 us
  Pallas kernels: 0 us -> 136 us
  matrix products: 123 us -> 0 us
  starting transfers between devices: 25.2 us -> 94.2 us
  other arithmetic: 91.9 us -> 124 us
    unnamed x9 -> x4, waiting for transfers between devices: 517 us -> 0.74 us
    pallas_call x0 -> x9, Pallas kernels: none -> 136 us  [run(): pl.pallas_call(kernel, out_shape=outs, in_specs=specs or [VM] * len(ins),...]
    dot_general x42 -> x0, matrix products: 123 us -> none  [the longest x2 9.73 us: layer_forward(): jnp.einsum('shqk,skhe->sqhe', attn_weights, value_heads, preferred_elemen...]
    unnamed x230 -> x59, local copies, waits for them, and re-layouts: 130 us -> 8.21 us
    slice x25 -> x31, local copies, waits for them, and re-layouts: 140 us -> 24.7 us  [the longest x8 9.02 us: gather_plain(): full[16 * b:16 * (b + ni * nj)]]
    concatenate x5 -> x7, other arithmetic: 18 us -> 108 us  [the longest x2 59.1 us: reduce_plain(): jnp.concatenate([rows_of(tiles[b:b + ni * nj], ni, nj) for b, ni, nj in P...]
    all_gather x3 -> x2, waiting for transfers between devices: 106 us -> 17.1 us  [gather_plain(): full = lax.all_gather(aligned.reshape(-1, 128), 'ta', axis=0, tiled=True)]
    reduce_scatter x2, waiting for transfers between devices: 148 us -> 59.8 us  [reduce_plain(): lax.psum_scatter(full, 'ta', scatter_dimension=0, tiled=True).astype(F32)]
  transfers between devices with their start and end apart: 15 -> 52, of which waited for: 8 -> 19; matrix products, arithmetic and copies ran while one was open for 17% -> 23% of each run, Pallas kernels for 0% -> 13%
where the time goes in v1:
time: 588 us; the launch traced here: 577 us
  waiting for transfers between devices  138 us (23%)
  Pallas kernels  136 us (23%)
  other arithmetic  124 us (21%)
  starting transfers between devices  94.2 us (16%)
  local copies, waits for them, and re-layouts  69.4 us (12%)
  between operations  15.5 us (3%)
    pallas_call x9, Pallas kernels, run(): pl.pallas_call(kernel, out_shape=outs, in_specs=specs or [VM] * len(ins),...  136 us
    ppermute x18, starting transfers between devices, shift(): lax.ppermute(value, 'ta', [(i, i + by) for i in range(n) if 0 <= i + by <...  60.3 us
    reduce_scatter x2, waiting for transfers between devices, reduce_plain(): lax.psum_scatter(full, 'ta', scatter_dimension=0, tiled=True).astype(F32)  59.8 us
    concatenate x2, other arithmetic, reduce_plain(): jnp.concatenate([rows_of(tiles[b:b + ni * nj], ni, nj) for b, ni, nj in P...  59.1 us
    concatenate x2, other arithmetic, gather_plain(): jnp.concatenate([tiles_of(full[16 * b:16 * (b + ni * nj)], ni, nj) for b,...  46.3 us
    ppermute x15, waiting for transfers between devices, from_first(): lax.ppermute(value, 'ta', [(i ^ root, i + step ^ root) for i in range(0,...  22 us
    reshape x10, local copies, waits for them, and re-layouts, rows_of(): tiles.reshape(ni, nj, 16, 128).transpose(0, 2, 1, 3)  20.8 us
    ppermute x10, waiting for transfers between devices, to_first(): lax.ppermute(value, 'ta', [(i + step, i) for i in range(0, n, 2 * step)])  17.2 us
  transfers between devices with their start and end apart: 52, of which 19 were waited for; matrix products, arithmetic and copies ran while one was open for 23% of the time, Pallas kernels for 13%

profile of v1, /device:TPU:20, one launch (start us, length us, event | category | flops | bytes accessed | tf_op | source)
XLA Modules:
  0.0 576.8 jit_solution(777083846386209033)
XLA Ops:
  9.9 3.9 collective-permute-done.14
  23.7 8.3 %collective-permute-done.4 = bf16[2,8,128]{2,1,0:T(8,128)(2,1)S(1)} collective-permute-done((bf16[2,8,128]{2,1,0:T(8,128)(2,1)S(1)}, bf16[2,8,128]{2,1,0:T(8,128)(2,1)S(1)}, u32[]{:S(2)}, u32[]{:S(2)}) %collective-permute-start.4) | collective-permute-done | bytes 4128 | tf_op jit(solution)/shard_map/ppermute | solution.py:331
  38.4 12.4 %collective-permute-done.9 = bf16[32,512]{1,0:T(8,128)(2,1)S(1)} collective-permute-done((bf16[32,512]{1,0:T(8,128)(2,1)S(1)}, bf16[32,512]{1,0:T(8,128)(2,1)S(1)}, u32[]{:S(2)}, u32[]{:S(2)}) %collective-permute-start.9) | collective-permute-done | bytes 32800 | tf_op jit(solution)/shard_map/ppermute | solution.py:331
  56.4 4.2 collective-permute-start.12
  67.1 3.4 collective-permute-start.6
  72.0 17.1 %all-gather.3.cloned.1.call-done = bf16[24576,128]{1,0:T(8,128)(2,1)} async-done(((bf16[768,128]{1,0:T(8,128)(2,1)}), bf16[24576,128]{1,0:T(8,128)(2,1)}) %all-gather.3.cloned.1.call-update) | async-done | bytes 6291472 | tf_op jit(solution)/shard_map/all_gather | solution.py:365
  101.9 23.1 %pad_maximum_fusion.w_ref = bf16[1536,16,128]{2,1,0:T(8,128)(2,1)} fusion(bf16[512,16,128]{2,1,0:T(8,128)(2,1)S(1)} %bitcast.93, bf16[512,16,128]{2,1,0:T(8,128)(2,1)S(1)} %bitcast.94, bf16[128,16,128]{2,1,0:T(8,128)(2,1)S(1)} %bitcast.116, bf16[384,16,128]{2,1,0:T(8,128)(2,1)S(1)} %bitcast.108), kind=kLoop, calls=%fused_computation | loop fusion | flops 9437184 | bytes 12582912 | tf_op jit(solution)/shard_map/concatenate | solution.py:366
  125.6 27.1 %shard_map.127 = (f32[512,512]{1,0:T(8,128)}, bf16[512,512]{1,0:T(8,128)(2,1)}, bf16[32,512]{1,0:T(8,128)(2,1)}, bf16[704,512]{1,0:T(8,128)(2,1)}, bf16[512,512]...) custom-call(bf16[512,512]{1,0:T(8,128)(2,1)} %x_ref.5, ...), custom_call_target="tpu_custom_call" | custom-call | flops 3000000000 | bytes 30000000 | tf_op jit(solution)/shard_map/pallas_call | solution.py:199
  161.5 13.4 %collective-permute-start.15 = (bf16[32,512]{1,0:T(8,128)(2,1)S(1)}, bf16[32,512]{1,0:T(8,128)(2,1)S(1)}, u32[]{:S(2)}, u32[]{:S(2)}) collective-permute-start(bf16[32,512]{1,0:T(8,128)(2,1)S(1)} %slice.132), channel_id=1, source_target_pairs={{0,1},{1,2},{2,3},{3,4},{4,5},{5,6},{6,7},{7,8},{8,9},{9,10},{10,1... | collective-permute-start | bytes 98312 | tf_op jit(solution)/shard_map/ppermute | solution.py:325
  176.9 3.7 collective-permute-start.20
  193.4 23.2 %pad_maximum_fusion.1.w_ref = bf16[1536,16,128]{2,1,0:T(8,128)(2,1)} fusion(bf16[512,16,128]{2,1,0:T(8,128)(2,1)S(1)} %bitcast.92, bf16[512,16,128]{2,1,0:T(8,128)(2,1)S(1)} %bitcast.91, bf16[128,16,128]{2,1,0:T(8,128)(2,1)S(1)} %bitcast.115, bf16[384,16,128]{2,1,0:T(8,128)(2,1)S(1)} %bitcast.107), kind=kLoop, calls=%fused_computation.1 | loop fusion | flops 9437184 | bytes 12582912 | tf_op jit(solution)/shard_map/concatenate | solution.py:366
  217.9 27.3 %shard_map.128 = (f32[512,512]{1,0:T(8,128)}, bf16[512,512]{1,0:T(8,128)(2,1)}, bf16[32,512]{1,0:T(8,128)(2,1)}, bf16[704,512]{1,0:T(8,128)(2,1)}, bf16[512,512]...) custom-call(f32[512,512]{1,0:T(8,128)} %get-tuple-element.55.x_ref, ...), custom_call_target="tpu_custom_call" | custom-call | flops 3000000000 | bytes 30000000 | tf_op jit(solution)/shard_map/pallas_call | solution.py:199
  245.2 22.3 %shard_map.129 = (f32[512,512]{1,0:T(8,128)}, bf16[512,512]{1,0:T(8,128)(2,1)}, bf16[512,2048]{1,0:T(8,128)(2,1)}, bf16[512,512]{1,0:T(8,128)(2,1)}, bf16[512,51...) custom-call(f32[512,512]{1,0:T(8,128)} %dx_ref.1, ...), custom_call_target="tpu_custom_call" | custom-call | flops 4000000000 | bytes 30000000 | tf_op jit(solution)/shard_map/pallas_call | solution.py:199
  267.5 13.5 %shard_map.134 = bf16[1536,16,128]{2,1,0:T(8,128)(2,1)} custom-call(bf16[704,512]{1,0:T(8,128)(2,1)} %get-tuple-element.90.hx_ref, bf16[512,512]{1,0:T(8,128)(2,1)} %get-tuple-element.56.h1_ref, bf16[512,512]{1,0:T(8,128)(2,1)} %get-tuple-element.91.dq_ref, bf16[704,1024]{1,0:T(8,128)(2,1)} %get-tuple-element.92.dkv_ref, ...), custom_call_target="tpu_custom_call" | custom-call | flops 4000000000 | bytes 30000000 | tf_op jit(solution)/shard_map/pallas_call | solution.py:199
  290.2 3.9 reshape.163
  294.4 29.5 %pad_maximum_fusion.3 = bf16[24576,128]{1,0:T(8,128)(2,1)} fusion(bf16[8192,128]{1,0:T(8,128)(2,1)} %bitcast.97, bf16[8192,128]{1,0:T(8,128)(2,1)S(1)} %bitcast.95, bf16[2048,128]{1,0:T(8,128)(2,1)S(1)} %bitcast.117, bf16[6144,128]{1,0:T(8,128)(2,1)} %reshape.163), kind=kLoop, calls=%fused_computation.3 | loop fusion | flops 25165824 | bytes 12582912 | tf_op jit(solution)/shard_map/concatenate | solution.py:372
  329.3 4.9 collective-permute-done.27
  344.3 6.4 %collective-permute-start.24 = (f32[32,512]{1,0:T(8,128)S(1)}, f32[32,512]{1,0:T(8,128)S(1)}, u32[]{:S(2)}, u32[]{:S(2)}) collective-permute-start(f32[32,512]{1,0:T(8,128)S(1)} %slice.139), channel_id=1, source_target_pairs={{1,0},{2,1},{3,2},{4,3},{5,4},{6,5},{7,6},{8,7},{9,8},{10,9},{11,1... | collective-permute-start | bytes 196616 | tf_op jit(solution)/shard_map/ppermute | solution.py:325
  353.3 3.5 collective-permute-done.25.har_ref
  357.5 4.0 shard_map.130
  361.5 22.1 %shard_map.131 = (f32[512,512]{1,0:T(8,128)}, bf16[512,512]{1,0:T(8,128)(2,1)}, bf16[512,2048]{1,0:T(8,128)(2,1)}, bf16[512,512]{1,0:T(8,128)(2,1)}, bf16[512,51...) custom-call(f32[512,512]{1,0:T(8,128)} %get-tuple-element.67.dx_ref,, ...), custom_call_target="tpu_custom_call" | custom-call | flops 4000000000 | bytes 30000000 | tf_op jit(solution)/shard_map/pallas_call | solution.py:199
  383.6 13.5 %shard_map.133 = bf16[1536,16,128]{2,1,0:T(8,128)(2,1)} custom-call(bf16[704,512]{1,0:T(8,128)(2,1)} %get-tuple-element.81.hx_ref, bf16[512,512]{1,0:T(8,128)(2,1)} %get-tuple-element.53.h1_ref, bf16[512,512]{1,0:T(8,128)(2,1)} %get-tuple-element.82.dq_ref, bf16[704,1024]{1,0:T(8,128)(2,1)} %get-tuple-element.83.dkv_ref, ...), custom_call_target="tpu_custom_call" | custom-call | flops 4000000000 | bytes 30000000 | tf_op jit(solution)/shard_map/pallas_call | solution.py:199
  406.3 3.8 reshape.155
  410.5 29.6 %pad_maximum_fusion.2 = bf16[24576,128]{1,0:T(8,128)(2,1)} fusion(bf16[8192,128]{1,0:T(8,128)(2,1)} %bitcast.98, bf16[8192,128]{1,0:T(8,128)(2,1)S(1)} %bitcast.96, bf16[2048,128]{1,0:T(8,128)(2,1)S(1)} %bitcast.118, bf16[6144,128]{1,0:T(8,128)(2,1)} %reshape.155), kind=kLoop, calls=%fused_computation.2 | loop fusion | flops 25165824 | bytes 12582912 | tf_op jit(solution)/shard_map/concatenate | solution.py:372
  445.5 4.9 collective-permute-done.36
  450.4 3.9 collective-permute-start.37
  463.0 6.4 %collective-permute-start.33 = (f32[32,512]{1,0:T(8,128)S(1)}, f32[32,512]{1,0:T(8,128)S(1)}, u32[]{:S(2)}, u32[]{:S(2)}) collective-permute-start(f32[32,512]{1,0:T(8,128)S(1)} %slice.145), channel_id=1, source_target_pairs={{1,0},{2,1},{3,2},{4,3},{5,4},{6,5},{7,6},{8,7},{9,8},{10,9},{11,1... | collective-permute-start | bytes 196616 | tf_op jit(solution)/shard_map/ppermute | solution.py:325
  472.4 3.2 collective-permute-done.34.har_ref
  476.2 3.8 shard_map.132
  482.9 3.6 collective-permute-done.43
  497.2 59.8 %reduce-scatter.3.cloned.1.call-done = bf16[768,128]{1,0:T(8,128)(2,1)} async-done(((bf16[24576,128]{1,0:T(8,128)(2,1)}), bf16[768,128]{1,0:T(8,128)(2,1)}) %reduce-scatter.3.cloned.1.call-update) | async-done | bytes 196624 | tf_op jit(solution)/shard_map/reduce_scatter | solution.py:373
  563.8 6.0 %multiply_add_fusion.1 = (f32[2,98336]{1,0:T(2,128)}, f32[2,98336]{1,0:T(2,128)}, f32[2,98336]{1,0:T(2,128)}, f32[2,98336]{1,0:T(2,128)}) fusion(f32[2,98336]{1,0:T(2,128)S(1)} %copy-done.7, f32[2,98336]{1,0:T(2,128)S(1)} %copy-done.6, s32[]{:T(128)S(6)} %select_n.213, f32[2,1024]{1,0:T(2,128)S(1)} %get-tuple-element.105, ...), kind=kLoop, calls=%fused_computation.14 | loop fusion | flops 3933440 | bytes 7088132 | tf_op jit(solution)/shard_map/add | solution.py:459
  (250 shorter events, 145.5 us)
Async XLA Ops:
  7.2 81.9 %all-gather.3.cloned.1.call-start = ((), (), s32[]{:S(2)}) async-start(), calls=%async_computation.2 | async-start | bytes 6488064 | tf_op jit(solution)/shard_map/all_gather | solution.py:365
  8.0 5.8 %collective-permute-start.14 = (bf16[2,1024]{1,0:T(2,128)(2,1)S(1)}, bf16[2,1024]{1,0:T(2,128)(2,1)S(1)}, u32[]{:S(2)}, u32[]{:S(2)}) collective-permute-start(bf16[2,1024]{1,0:T(2,128)(2,1)S(1)} %get-tuple-element.115), channel_id=1, source_target_pairs={{0,1},{1,2},{2,3},{3,4},{4,5},{5,6},{6,7},{7,8},{8,9},{9,10},{10,1... | collective-permute-start | bytes 12296 | tf_op jit(solution)/shard_map/ppermute | solution.py:325
  18.6 162.0 %all-gather.5.cloned.1.call-start = ((), (), s32[]{:S(2)}) async-start(), calls=%async_computation.3 | async-start | bytes 6488064 | tf_op jit(solution)/shard_map/all_gather | solution.py:365
  19.4 476.5 %reduce-scatter.5.cloned.1.call-start = ((), (), s32[]{:S(2)}) async-start(), calls=%async_computation.5 | async-start | bytes 6488064 | tf_op jit(solution)/shard_map/reduce_scatter | solution.py:373
  22.3 9.7 %collective-permute-start.4 = (bf16[2,8,128]{2,1,0:T(8,128)(2,1)S(1)}, bf16[2,8,128]{2,1,0:T(8,128)(2,1)S(1)}, u32[]{:S(2)}, u32[]{:S(2)}) collective-permute-start(bf16[2,8,128]{2,1,0:T(8,128)(2,1)S(1)} %broadcast_select_fusion.14), channel_id=1, source_target_pairs={{31,30},{29,28},{27,26},{25,24},{23,22},{21,20},{19,18},{17,16},{1... | collective-permute-start | bytes 12296 | tf_op jit(solution)/shard_map/ppermute | solution.py:331
  37.0 13.7 %collective-permute-start.9 = (bf16[32,512]{1,0:T(8,128)(2,1)S(1)}, bf16[32,512]{1,0:T(8,128)(2,1)S(1)}, u32[]{:S(2)}, u32[]{:S(2)}) collective-permute-start(bf16[32,512]{1,0:T(8,128)(2,1)S(1)} %broadcast_select_fusion.3), channel_id=1, source_target_pairs={{0,4},{8,12},{16,20},{24,28}} | collective-permute-start | bytes 98312 | tf_op jit(solution)/shard_map/ppermute | solution.py:331
  53.7 16.9 %collective-permute-start.11 = (bf16[32,512]{1,0:T(8,128)(2,1)S(1)}, bf16[32,512]{1,0:T(8,128)(2,1)S(1)}, u32[]{:S(2)}, u32[]{:S(2)}) collective-permute-start(bf16[32,512]{1,0:T(8,128)(2,1)S(1)} %broadcast_select_fusion.7), channel_id=1, source_target_pairs={{0,1},{2,3},{4,5},{6,7},{8,9},{10,11},{12,13},{14,15},{16,17},{18,... | collective-permute-start | bytes 98312 | tf_op jit(solution)/shard_map/ppermute | solution.py:331
  56.4 14.1 %collective-permute-start.12 = (bf16[32,512]{1,0:T(8,128)(2,1)}, bf16[32,512]{1,0:T(8,128)(2,1)S(1)}, u32[]{:S(2)}, u32[]{:S(2)}) collective-permute-start(bf16[32,512]{1,0:T(8,128)(2,1)} %get-tuple-element.54), channel_id=1, source_target_pairs={{0,2},{1,3},{2,4},{3,5},{4,6},{5,7},{6,8},{7,9},{8,10},{9,11},{10,... | collective-permute-start | bytes 98312 | tf_op jit(solution)/shard_map/ppermute | solution.py:325
  60.6 9.9 %collective-permute-start.13 = (bf16[32,512]{1,0:T(8,128)(2,1)}, bf16[32,512]{1,0:T(8,128)(2,1)S(1)}, u32[]{:S(2)}, u32[]{:S(2)}) collective-permute-start(bf16[32,512]{1,0:T(8,128)(2,1)} %get-tuple-element.54), channel_id=1, source_target_pairs={{0,1},{1,2},{2,3},{3,4},{4,5},{5,6},{6,7},{7,8},{8,9},{9,10},{10,1... | collective-permute-start | bytes 98312 | tf_op jit(solution)/shard_map/ppermute | solution.py:325
  64.1 60.9 %collective-permute-start.5 = (bf16[32,512]{1,0:T(8,128)(2,1)S(1)}, bf16[32,512]{1,0:T(8,128)(2,1)S(1)}, u32[]{:S(2)}, u32[]{:S(2)}) collective-permute-start(bf16[32,512]{1,0:T(8,128)(2,1)S(1)} %slice.124), channel_id=1, source_target_pairs={{0,1},{1,2},{2,3},{3,4},{4,5},{5,6},{6,7},{7,8},{8,9},{9,10},{10,1... | collective-permute-start | bytes 98312 | tf_op jit(solution)/shard_map/ppermute | solution.py:325
  67.1 57.9 %collective-permute-start.6 = (bf16[16,512]{1,0:T(8,128)(2,1)S(1)}, bf16[16,512]{1,0:T(8,128)(2,1)S(1)}, u32[]{:S(2)}, u32[]{:S(2)}) collective-permute-start(bf16[16,512]{1,0:T(8,128)(2,1)S(1)} %slice.125), channel_id=1, source_target_pairs={{1,0},{2,1},{3,2},{4,3},{5,4},{6,5},{7,6},{8,7},{9,8},{10,9},{11,1... | collective-permute-start | bytes 49160 | tf_op jit(solution)/shard_map/ppermute | solution.py:325
  154.8 22.0 %collective-permute-start.19 = (bf16[32,512]{1,0:T(8,128)(2,1)S(1)}, bf16[32,512]{1,0:T(8,128)(2,1)S(1)}, u32[]{:S(2)}, u32[]{:S(2)}) collective-permute-start(bf16[32,512]{1,0:T(8,128)(2,1)S(1)} %broadcast_select_fusion.2), channel_id=1, source_target_pairs={{0,4},{8,12},{16,20},{24,28}} | collective-permute-start | bytes 98312 | tf_op jit(solution)/shard_map/ppermute | solution.py:331
  156.1 60.4 %collective-permute-start.22 = (bf16[32,512]{1,0:T(8,128)(2,1)}, bf16[32,512]{1,0:T(8,128)(2,1)S(1)}, u32[]{:S(2)}, u32[]{:S(2)}) collective-permute-start(bf16[32,512]{1,0:T(8,128)(2,1)} %get-tuple-element.57), channel_id=1, source_target_pairs={{0,2},{1,3},{2,4},{3,5},{4,6},{5,7},{6,8},{7,9},{8,10},{9,11},{10,... | collective-permute-start | bytes 98312 | tf_op jit(solution)/shard_map/ppermute | solution.py:325
  158.1 58.5 %collective-permute-start.23 = (bf16[32,512]{1,0:T(8,128)(2,1)}, bf16[32,512]{1,0:T(8,128)(2,1)S(1)}, u32[]{:S(2)}, u32[]{:S(2)}) collective-permute-start(bf16[32,512]{1,0:T(8,128)(2,1)} %get-tuple-element.57), channel_id=1, source_target_pairs={{0,1},{1,2},{2,3},{3,4},{4,5},{5,6},{6,7},{7,8},{8,9},{9,10},{10,1... | collective-permute-start | bytes 98312 | tf_op jit(solution)/shard_map/ppermute | solution.py:325
  161.5 55.8 %collective-permute-start.15 = (bf16[32,512]{1,0:T(8,128)(2,1)S(1)}, bf16[32,512]{1,0:T(8,128)(2,1)S(1)}, u32[]{:S(2)}, u32[]{:S(2)}) collective-permute-start(bf16[32,512]{1,0:T(8,128)(2,1)S(1)} %slice.132), channel_id=1, source_target_pairs={{0,1},{1,2},{2,3},{3,4},{4,5},{5,6},{6,7},{7,8},{8,9},{9,10},{10,1... | collective-permute-start | bytes 98312 | tf_op jit(solution)/shard_map/ppermute | solution.py:325
  174.9 42.4 %collective-permute-start.16 = (bf16[16,512]{1,0:T(8,128)(2,1)S(1)}, bf16[16,512]{1,0:T(8,128)(2,1)S(1)}, u32[]{:S(2)}, u32[]{:S(2)}) collective-permute-start(bf16[16,512]{1,0:T(8,128)(2,1)S(1)} %slice.133), channel_id=1, source_target_pairs={{1,0},{2,1},{3,2},{4,3},{5,4},{6,5},{7,6},{8,7},{9,8},{10,9},{11,1... | collective-permute-start | bytes 49160 | tf_op jit(solution)/shard_map/ppermute | solution.py:325
  176.9 15.1 %collective-permute-start.20 = (bf16[32,512]{1,0:T(8,128)(2,1)S(1)}, bf16[32,512]{1,0:T(8,128)(2,1)S(1)}, u32[]{:S(2)}, u32[]{:S(2)}) collective-permute-start(bf16[32,512]{1,0:T(8,128)(2,1)S(1)} %broadcast_select_fusion.4), channel_id=1, source_target_pairs={{0,2},{4,6},{8,10},{12,14},{16,18},{20,22},{24,26},{28,30}} | collective-permute-start | bytes 98312 | tf_op jit(solution)/shard_map/ppermute | solution.py:331
  191.9 24.6 %collective-permute-start.21 = (bf16[32,512]{1,0:T(8,128)(2,1)S(1)}, bf16[32,512]{1,0:T(8,128)(2,1)S(1)}, u32[]{:S(2)}, u32[]{:S(2)}) collective-permute-start(bf16[32,512]{1,0:T(8,128)(2,1)S(1)} %broadcast_select_fusion.6), channel_id=1, source_target_pairs={{0,1},{2,3},{4,5},{6,7},{8,9},{10,11},{12,13},{14,15},{16,17},{18,... | collective-permute-start | bytes 98312 | tf_op jit(solution)/shard_map/ppermute | solution.py:331
  323.9 233.0 %reduce-scatter.3.cloned.1.call-start = ((), (), s32[]{:S(2)}) async-start(), calls=%async_computation.4 | async-start | bytes 6488064 | tf_op jit(solution)/shard_map/reduce_scatter | solution.py:373
  328.0 6.2 %collective-permute-start.27 = (f32[32,512]{1,0:T(8,128)S(1)}, f32[32,512]{1,0:T(8,128)S(1)}, u32[]{:S(2)}, u32[]{:S(2)}) collective-permute-start(f32[32,512]{1,0:T(8,128)S(1)} %get-tuple-element.120), channel_id=1, source_target_pairs={{2,0},{6,4},{10,8},{14,12},{18,16},{22,20},{26,24},{30,28}} | collective-permute-start | bytes 196616 | tf_op jit(solution)/shard_map/ppermute | solution.py:340
  338.1 14.6 %collective-permute-start.31 = (f32[32,512]{1,0:T(8,128)S(1)}, f32[32,512]{1,0:T(8,128)S(1)}, u32[]{:S(2)}, u32[]{:S(2)}) collective-permute-start(f32[32,512]{1,0:T(8,128)S(1)} %get-tuple-element.122), channel_id=1, source_target_pairs={{2,0},{3,1},{4,2},{5,3},{6,4},{7,5},{8,6},{9,7},{10,8},{11,9},{12,... | collective-permute-start | bytes 196616 | tf_op jit(solution)/shard_map/ppermute | solution.py:325
  340.0 12.6 %collective-permute-start.32 = (f32[32,512]{1,0:T(8,128)S(1)}, f32[32,512]{1,0:T(8,128)S(1)}, u32[]{:S(2)}, u32[]{:S(2)}) collective-permute-start(f32[32,512]{1,0:T(8,128)S(1)} %get-tuple-element.121), channel_id=1, source_target_pairs={{1,0},{2,1},{3,2},{4,3},{5,4},{6,5},{7,6},{8,7},{9,8},{10,9},{11,1... | collective-permute-start | bytes 196616 | tf_op jit(solution)/shard_map/ppermute | solution.py:325
  342.0 10.7 %collective-permute-start.30 = (f32[32,512]{1,0:T(8,128)S(1)}, f32[32,512]{1,0:T(8,128)S(1)}, u32[]{:S(2)}, u32[]{:S(2)}) collective-permute-start(f32[32,512]{1,0:T(8,128)S(1)} %add.195), channel_id=1, source_target_pairs={{16,0}} | collective-permute-start | bytes 196616 | tf_op jit(solution)/shard_map/ppermute | solution.py:340
  344.3 12.6 %collective-permute-start.24 = (f32[32,512]{1,0:T(8,128)S(1)}, f32[32,512]{1,0:T(8,128)S(1)}, u32[]{:S(2)}, u32[]{:S(2)}) collective-permute-start(f32[32,512]{1,0:T(8,128)S(1)} %slice.139), channel_id=1, source_target_pairs={{1,0},{2,1},{3,2},{4,3},{5,4},{6,5},{7,6},{8,7},{9,8},{10,9},{11,1... | collective-permute-start | bytes 196616 | tf_op jit(solution)/shard_map/ppermute | solution.py:325
  350.7 6.1 %collective-permute-start.25 = (f32[16,512]{1,0:T(8,128)S(1)}, f32[16,512]{1,0:T(8,128)S(1)}, u32[]{:S(2)}, u32[]{:S(2)}) collective-permute-start(f32[16,512]{1,0:T(8,128)S(1)} %slice.140), channel_id=1, source_target_pairs={{0,1},{1,2},{2,3},{3,4},{4,5},{5,6},{6,7},{7,8},{8,9},{9,10},{10,1... | collective-permute-start | bytes 98312 | tf_op jit(solution)/shard_map/ppermute | solution.py:325
  444.2 6.2 %collective-permute-start.36 = (f32[32,512]{1,0:T(8,128)S(1)}, f32[32,512]{1,0:T(8,128)S(1)}, u32[]{:S(2)}, u32[]{:S(2)}) collective-permute-start(f32[32,512]{1,0:T(8,128)S(1)} %get-tuple-element.117), channel_id=1, source_target_pairs={{2,0},{6,4},{10,8},{14,12},{18,16},{22,20},{26,24},{30,28}} | collective-permute-start | bytes 196616 | tf_op jit(solution)/shard_map/ppermute | solution.py:340
  456.9 14.8 %collective-permute-start.40 = (f32[32,512]{1,0:T(8,128)S(1)}, f32[32,512]{1,0:T(8,128)S(1)}, u32[]{:S(2)}, u32[]{:S(2)}) collective-permute-start(f32[32,512]{1,0:T(8,128)S(1)} %get-tuple-element.119), channel_id=1, source_target_pairs={{2,0},{3,1},{4,2},{5,3},{6,4},{7,5},{8,6},{9,7},{10,8},{11,9},{12,... | collective-permute-start | bytes 196616 | tf_op jit(solution)/shard_map/ppermute | solution.py:325
  458.8 12.9 %collective-permute-start.41 = (f32[32,512]{1,0:T(8,128)S(1)}, f32[32,512]{1,0:T(8,128)S(1)}, u32[]{:S(2)}, u32[]{:S(2)}) collective-permute-start(f32[32,512]{1,0:T(8,128)S(1)} %get-tuple-element.118), channel_id=1, source_target_pairs={{1,0},{2,1},{3,2},{4,3},{5,4},{6,5},{7,6},{8,7},{9,8},{10,9},{11,1... | collective-permute-start | bytes 196616 | tf_op jit(solution)/shard_map/ppermute | solution.py:325
  460.7 11.0 %collective-permute-start.39 = (f32[32,512]{1,0:T(8,128)S(1)}, f32[32,512]{1,0:T(8,128)S(1)}, u32[]{:S(2)}, u32[]{:S(2)}) collective-permute-start(f32[32,512]{1,0:T(8,128)S(1)} %add.203), channel_id=1, source_target_pairs={{16,0}} | collective-permute-start | bytes 196616 | tf_op jit(solution)/shard_map/ppermute | solution.py:340
  463.0 12.6 %collective-permute-start.33 = (f32[32,512]{1,0:T(8,128)S(1)}, f32[32,512]{1,0:T(8,128)S(1)}, u32[]{:S(2)}, u32[]{:S(2)}) collective-permute-start(f32[32,512]{1,0:T(8,128)S(1)} %slice.145), channel_id=1, source_target_pairs={{1,0},{2,1},{3,2},{4,3},{5,4},{6,5},{7,6},{8,7},{9,8},{10,9},{11,1... | collective-permute-start | bytes 196616 | tf_op jit(solution)/shard_map/ppermute | solution.py:325
  469.5 6.1 %collective-permute-start.34 = (f32[16,512]{1,0:T(8,128)S(1)}, f32[16,512]{1,0:T(8,128)S(1)}, u32[]{:S(2)}, u32[]{:S(2)}) collective-permute-start(f32[16,512]{1,0:T(8,128)S(1)} %slice.146), channel_id=1, source_target_pairs={{0,1},{1,2},{2,3},{3,4},{4,5},{5,6},{6,7},{7,8},{8,9},{9,10},{10,1... | collective-permute-start | bytes 98312 | tf_op jit(solution)/shard_map/ppermute | solution.py:325
  495.9 65.1 %collective-permute-start.46 = (f32[2,1024]{1,0:T(2,128)}, f32[2,1024]{1,0:T(2,128)}, u32[]{:S(2)}, u32[]{:S(2)}) collective-permute-start(f32[2,1024]{1,0:T(2,128)} %add.211), channel_id=1, source_target_pairs={{0,16},{1,17},{2,18},{3,19},{4,20},{5,21},{6,22},{7,23},{8,24},{9,... | collective-permute-start | bytes 24584 | tf_op jit(solution)/shard_map/ppermute | solution.py:348
  (54 other events, 489.2 us)
Sparse Core Ops, SparseCore 0:
  18.8 70.3 all-gather.2
  92.6 68.1 all-gather.4
  324.1 112.6 reduce-scatter.4
  443.1 113.7 reduce-scatter.2

commit v2 on v1

v2 whole, which is shorter than its diff:
```python
import functools

import jax
import jax.numpy as jnp
from jax import lax
from jax.experimental import pallas as pl
from jax.experimental.pallas import tpu as pltpu
from jax.sharding import PartitionSpec as P

D = 512
HEADS = 8
FF = 2048
SEG = 16
LEFT = 30
RIGHT = 4
MEM = 4
STEP = 10
FIRST = 32
NEG = -1e30

TOK = 512
NSEG = TOK // SEG
LH = 32
RH = 16
EXT = LH + TOK + 2 * RH
ROWS = EXT + NSEG * MEM
BLK = 4
NBLK = NSEG // BLK
QB = BLK * SEG
KB = 128
WB = KB - BLK * MEM

TILES = 1536
QKV0, WO0, WU0, WD0 = 0, 384, 512, 1024
MATS = TILES * 16 * 128
GROUPS = 32
BT = TILES // GROUPS
PT = 36

F32 = jnp.float32
BF16 = jnp.bfloat16
VM = pl.BlockSpec(memory_space=pltpu.VMEM)
SM = pl.BlockSpec(memory_space=pltpu.SMEM)
ANYS = pl.BlockSpec(memory_space=pl.ANY)


def mm(a, b):
    return lax.dot_general(a, b, (((1,), (0,)), ((), ())), preferred_element_type=F32)


def mm_nt(a, b):
    return lax.dot_general(a, b, (((1,), (1,)), ((), ())), preferred_element_type=F32)


def mm_tn(a, b):
    return lax.dot_general(a, b, (((0,), (0,)), ((), ())), preferred_element_type=F32)


def wblk(w, base, nj, i0, ni, j0, nj_take):
    cols = [
        jnp.concatenate([w[base + (i0 + i) * nj + j0 + j] for i in range(ni)], axis=0)
        for j in range(nj_take)
    ]
    return cols[0] if nj_take == 1 else jnp.concatenate(cols, axis=1)


def place(me, rc, ra, rb, k):
    core = (me % 2) ^ rc
    x = ((me // 2) % 2) ^ jnp.where(core == 0, ra, rb)
    y = ((me // 4) % 2) ^ jnp.where(core == 0, rb, ra)
    z = (me // 8 + k) % 4
    return ((z * 2 + y) * 2 + x) * 2 + core


def load_weights(me, pieces, w_ref, sems, gt_ref=None):
    if len(pieces) < 5:
        if gt_ref is not None:
            pltpu.make_async_copy(pieces[1], gt_ref, sems.at[1, 0]).start()
        for d in range(GROUPS):
            per = TILES // GROUPS
            pltpu.make_async_copy(
                pieces[0].at[pl.ds(per * d, per)], w_ref.at[pl.ds(per * d, per)], sems.at[0, d]
            ).start()
        return
    if len(pieces) == 5:
        for m in range(4):
            for k in range(4):
                for rc, src in ((0, pieces[m].at[k]), (1, pieces[4].at[m, k])):
                    d = place(me, rc, m % 2, m // 2, -k % 4)
                    pltpu.make_async_copy(src, w_ref.at[pl.ds(d * BT, BT)], sems.at[0, d]).start()
        return
    for rc in range(2):
        for m in range(4):
            for k in range(4):
                d = place(me, rc, m % 2, m // 2, -k % 4)
                t = d * BT
                pltpu.make_async_copy(
                    pieces[4 * rc + m].at[k], w_ref.at[pl.ds(t, PT)], sems.at[0, d]
                ).start()
                late = pieces[8 + 4 * rc + k].at[m]
                pltpu.make_async_copy(
                    late.at[pl.ds(0, BT - PT)], w_ref.at[pl.ds(t + PT, BT - PT)], sems.at[1, d]
                ).start()
                if gt_ref is not None:

                    @pl.when(d == GROUPS - 1)
                    def _():
                        pltpu.make_async_copy(late.at[BT - PT], gt_ref, sems.at[1, GROUPS]).start()


def await_gains(pieces, gt_ref, sems):
    pltpu.make_async_copy(gt_ref, gt_ref, sems.at[1, 0 if len(pieces) < 16 else GROUPS]).wait()


def await_weights(pieces, w_ref, sems, lo, hi):
    for d in range(lo, hi):
        t = d * BT
        if len(pieces) < 16:
            pltpu.make_async_copy(
                w_ref.at[pl.ds(t, BT)], w_ref.at[pl.ds(t, BT)], sems.at[0, d]
            ).wait()
            continue
        pltpu.make_async_copy(w_ref.at[pl.ds(t, PT)], w_ref.at[pl.ds(t, PT)], sems.at[0, d]).wait()
        pltpu.make_async_copy(
            w_ref.at[pl.ds(t + PT, BT - PT)], w_ref.at[pl.ds(t + PT, BT - PT)], sems.at[1, d]
        ).wait()


def gain_row(g_ref, layer, which):
    g = g_ref[...].astype(F32)
    r = 8 * layer + 4 * which
    return jnp.concatenate([g[r + k : r + k + 1] for k in range(4)], axis=1)


def norm_parts(v):
    mean = jnp.mean(v, axis=-1, keepdims=True)
    cen = v - mean
    rstd = lax.rsqrt(jnp.mean(cen * cen, axis=-1, keepdims=True) + 1e-05)
    return cen * rstd, rstd


def norm_back(dh, xhat, rstd, gain):
    dx = dh * gain
    return rstd * (
        dx
        - jnp.mean(dx, axis=-1, keepdims=True)
        - xhat * jnp.mean(dx * xhat, axis=-1, keepdims=True)
    )


def seg_mean(h):
    return (jnp.sum(h.astype(F32).reshape(NSEG, SEG, D), axis=1) * (1.0 / SEG)).astype(BF16)


def head_of_layer(x, gain):
    xhat, _ = norm_parts(x)
    h1 = (xhat * gain).astype(BF16)
    return h1, seg_mean(h1)


def first_kernel(x_ref, sum_ref):
    xhat, _ = norm_parts(x_ref[...].astype(F32))
    sum_ref[...] = seg_mean(xhat)


def lane_lo(rows):
    return lax.broadcasted_iota(jnp.int32, (rows, 128), 1) < 64


def split_heads(m, lo):
    z = jnp.zeros_like(m)
    return jnp.concatenate([jnp.where(lo, m, z), jnp.where(lo, z, m)], axis=0)


def onehot_of(loc_ref):
    ids = lax.broadcasted_iota(jnp.int32, (NSEG * MEM, 128), 1)
    return jnp.where(loc_ref[...] == ids, 1.0, 0.0).astype(BF16)


def block_keys(kv_ref, b, col):
    r0 = pl.multiple_of(b * QB, QB)
    m0 = pl.multiple_of(EXT + b * (BLK * MEM), BLK * MEM)
    return jnp.concatenate(
        [kv_ref[pl.ds(r0, WB), col : col + 128], kv_ref[pl.ds(m0, BLK * MEM), col : col + 128]], axis=0
    )


def attend(me, n, q_ref, kv_ref, vis_ref, p_ref, o_ref):
    ki = lax.broadcasted_iota(jnp.int32, (KB, 128), 0)
    qi = (lax.broadcasted_iota(jnp.int32, (KB, 128), 1) % QB) // SEG
    off = ki - SEG * qi - (LH - LEFT)
    near = jnp.where((off >= 0) & (off < LEFT + SEG + RIGHT) & (ki < WB), 1.0, 0.0)
    memb = jnp.where((ki >= WB) & ((ki - WB) // MEM == qi), 1.0, 0.0)
    first = jnp.where(me == 0, LH, 0)
    end = jnp.where(me == n - 1, LH + TOK, EXT)
    lo = lane_lo(QB)

    def block(b, carry):
        r0 = pl.multiple_of(b * QB, QB)
        m0 = pl.multiple_of(b * (BLK * MEM), BLK * MEM)
        inside = (ki + r0 >= first) & (ki + r0 < end)
        memv = jnp.concatenate(
            [jnp.zeros((WB, 128), F32), vis_ref[pl.ds(m0, BLK * MEM), :]], axis=0
        )
        seen = jnp.where(inside, near, 0.0) + memb * memv > 0.5
        for p in range(4):
            kc, vc = block_keys(kv_ref, b, 128 * p), block_keys(kv_ref, b, D + 128 * p)
            s = mm_nt(kc, split_heads(q_ref[pl.ds(r0, QB), 128 * p : 128 * p + 128], lo))
            s = jnp.where(seen, s, NEG)
            e = jnp.exp(s - jnp.max(s, axis=0, keepdims=True))
            pb = (e * (1.0 / jnp.sum(e, axis=0, keepdims=True))).astype(BF16)
            p_ref[b * 4 + p] = pb
            o2 = mm_tn(pb, vc)
            o_ref[pl.ds(r0, QB), 128 * p : 128 * p + 128] = jnp.where(lo, o2[:QB], o2[QB:]).astype(BF16)
        return carry

    lax.fori_loop(0, NBLK, block, 0)


def attend_back(q_ref, kv_ref, p_ref, do_ref, dq_ref, dkv_ref):
    dkv_ref[...] = jnp.zeros_like(dkv_ref)
    lo = lane_lo(QB)

    def block(b, carry):
        r0 = pl.multiple_of(b * QB, QB)
        m0 = pl.multiple_of(EXT + b * (BLK * MEM), BLK * MEM)
        for p in range(4):
            kc0, vc0 = 128 * p, D + 128 * p
            kc, vc = block_keys(kv_ref, b, kc0), block_keys(kv_ref, b, vc0)
            qq = split_heads(q_ref[pl.ds(r0, QB), kc0 : kc0 + 128], lo)
            dd = split_heads(do_ref[pl.ds(r0, QB), kc0 : kc0 + 128], lo)
            pb = p_ref[b * 4 + p]
            pf = pb.astype(F32)
            pd = pf * mm_nt(vc, dd)
            ds = (pd - pf * jnp.sum(pd, axis=0, keepdims=True)).astype(BF16)
            dv, dk = mm(pb, dd), mm(ds, qq)
            dq2 = mm_tn(ds, kc)
            dq_ref[pl.ds(r0, QB), kc0 : kc0 + 128] = (jnp.where(lo, dq2[:QB], dq2[QB:]) * 0.125).astype(BF16)
            dkv_ref[pl.ds(r0, WB), kc0 : kc0 + 128] += dk[:WB]
            dkv_ref[pl.ds(r0, WB), vc0 : vc0 + 128] += dv[:WB]
            dkv_ref[pl.ds(m0, BLK * MEM), kc0 : kc0 + 128] = dk[WB:]
            dkv_ref[pl.ds(m0, BLK * MEM), vc0 : vc0 + 128] = dv[WB:]
        return carry

    lax.fori_loop(0, NBLK, block, 0)


class Copies:
    def __init__(self, sems):
        self.sems, self.used, self.open = sems, 0, []

    def start(self, src, dst):
        copy = pltpu.make_async_copy(src, dst, self.sems.at[self.used])
        self.used += 1
        copy.start()
        return copy

    def out(self, src, dst):
        self.open.append(self.start(src, dst))

    def finish(self):
        for copy in self.open:
            copy.wait()


def project(hx_ref, w_ref, q_ref, kv_ref):
    q = mm(hx_ref[LH : LH + TOK], wblk(w_ref, QKV0, 12, 0, 32, 0, 4)).astype(BF16)
    q_ref[...] = q * jnp.asarray(0.125, BF16)
    for j in range(2):
        kv_ref[:, 512 * j : 512 * j + 512] = mm(hx_ref[...], wblk(w_ref, QKV0, 12, 0, 32, 4 + 4 * j, 4)).astype(BF16)


def feed_forward(h2_ref, w_ref, act_ref, gp_ref, out_ref, step):
    for c in range(4):
        u = mm(h2_ref[...], wblk(w_ref, WU0, 16, 0, 32, 4 * c, 4))
        cc, c3 = 0.7978845608028654, 0.7978845608028654 * 0.044715
        u2 = u * u
        t = jnp.tanh(u * (cc + c3 * u2))
        hu = 0.5 * u
        act = (hu + hu * t).astype(BF16)
        gp = 0.5 + 0.5 * t + hu * (1.0 - t * t) * (cc + 3 * c3 * u2)
        act_ref[:, 512 * c : 512 * c + 512] = act
        gp_ref[:, 512 * c : 512 * c + 512] = gp.astype(BF16)
        out_ref[...] += mm(act, wblk(w_ref, WD0, 4, 32 * c, 32, 0, 4))
        step(c)


def back_main(dx_ref, w_ref, gains, q_ref, kv_ref, p_ref, a_ref, gp_ref, da_ref, dxb_ref, dub_ref, dab_ref, dq_ref,
              dkvb_ref, dh_ref, dgb_ref, dkv_ref, dob_ref, step):
    dxb_ref[...] = dx_ref[...].astype(BF16)
    step("dxb")
    for c in range(4):
        dact = mm_nt(dxb_ref[...], wblk(w_ref, WD0, 4, 32 * c, 32, 0, 4))
        du = (dact * gp_ref[:, 512 * c : 512 * c + 512].astype(F32)).astype(BF16)
        dub_ref[:, 512 * c : 512 * c + 512] = du
        dh2 = mm_nt(du, wblk(w_ref, WU0, 16, 0, 32, 4 * c, 4))
        if c:
            da_ref[...] += dh2
        else:
            da_ref[...] = dh2
    step("dub")
    xhat, rstd = norm_parts(a_ref[...])
    dh2 = da_ref[...]
    dgb_ref[...] = jnp.sum(dh2 * xhat, axis=0, keepdims=True)
    da = dx_ref[...] + norm_back(dh2, xhat, rstd, gains)
    da_ref[...] = da
    dab_ref[...] = da.astype(BF16)
    step("dab")
    dob_ref[...] = mm_nt(dab_ref[...], wblk(w_ref, WO0, 4, 0, 32, 0, 4)).astype(BF16)
    step("attend")
    attend_back(q_ref, kv_ref, p_ref, dob_ref, dq_ref, dkv_ref)
    dkvb_ref[...] = dkv_ref[...].astype(BF16)
    step("dkvb")
    dh_ref[...] = mm_nt(dkvb_ref[...], wblk(w_ref, QKV0, 12, 0, 32, 4, 8))
    dh_ref[LH : LH + TOK] += mm_nt(dq_ref[...], wblk(w_ref, QKV0, 12, 0, 32, 0, 4))
    step("dh")


def table_grad(loc_ref, dh_ref, dtab_ref):
    dch = dh_ref[EXT:ROWS]
    hi = dch.astype(BF16)
    oh = onehot_of(loc_ref)
    dtab_ref[...] = mm_tn(oh, hi) + mm_tn(oh, (dch - hi.astype(F32)).astype(BF16))


def low_kernel(me_ref, x_ref, hl_ref, hr_ref, root_ref, b2_ref, summ_ref, loc_ref, vis_ref, *rest, np_, n):
    pieces, rest = rest[:np_], rest[np_:]
    (out_ref, h1n_ref, sumn_ref, gt_ref, hx_o, q_o, kv_o, p_o, o_o, a_o, h2_o, gp_o, act_o,
     w_ref, sems, hx_ref, q_ref, kv_ref, p_ref, o_ref, a_ref, h2_ref, gp_ref, act_ref, osem) = rest
    me = me_ref[0]
    load_weights(me, pieces, w_ref, sems, gt_ref)
    copies = Copies(osem)
    await_gains(pieces, gt_ref, sems)
    ga = gain_row(gt_ref, 0, 0)
    for ref, rows, at in ((hl_ref, LH, 0), (x_ref, TOK, LH), (hr_ref, RH, LH + TOK)):
        xhat, _ = norm_parts(ref[0:rows].astype(F32))
        hx_ref[at : at + rows] = (xhat * ga).astype(BF16)
    means = jnp.concatenate([root_ref[...], b2_ref[...], hl_ref[LH:], summ_ref[...]], axis=0)
    hx_ref[LH + TOK + RH : EXT] = jnp.zeros((RH, D), BF16)
    hx_ref[EXT:ROWS] = mm(onehot_of(loc_ref), (means.astype(F32) * ga).astype(BF16)).astype(BF16)
    copies.out(hx_ref, hx_o)
    await_weights(pieces, w_ref, sems, 0, 8)
    project(hx_ref, w_ref, q_ref, kv_ref)
    copies.out(q_ref, q_o)
    copies.out(kv_ref, kv_o)
    attend(me, n, q_ref, kv_ref, vis_ref, p_ref, o_ref)
    copies.out(p_ref, p_o)
    copies.out(o_ref, o_o)
    await_weights(pieces, w_ref, sems, 8, 32)
    a = x_ref[...].astype(F32) + mm(o_ref[...], wblk(w_ref, WO0, 4, 0, 32, 0, 4))
    a_ref[...] = a
    copies.out(a_ref, a_o)
    xhat, _ = norm_parts(a)
    h2_ref[...] = (xhat * gain_row(gt_ref, 0, 1)).astype(BF16)
    copies.out(h2_ref, h2_o)
    out_ref[...] = a
    feed_forward(h2_ref, w_ref, act_ref, gp_ref, out_ref, lambda c: None)
    copies.out(act_ref, act_o)
    copies.out(gp_ref, gp_o)
    h1n, sumn = head_of_layer(out_ref[...], gain_row(gt_ref, 1, 0))
    h1n_ref[...] = h1n
    sumn_ref[...] = sumn
    copies.finish()


def top_kernel(me_ref, x_ref, h1_ref, hl_ref, hr_ref, root_ref, b2_ref, summ_ref, loc_ref, vis_ref, gt_ref, cot_any,
               *rest, np_, n):
    pieces, rest = rest[:np_], rest[np_:]
    (out_o, da_ref, dh_ref, dtab_ref, dgb_ref, hx_o, o_o, h2_o, act_o, dxb_o, dub_o, dab_o, dq_o, dkvb_o,
     w_ref, sems, hx_ref, q_ref, kv_ref, p_ref, o_ref, a_ref, h2_ref, gp_ref, act_ref,
     out_ref, dx_ref, dxb_ref, dub_ref, dab_ref, dq_ref, dkvb_ref, dkv_ref, dob_ref, osem) = rest
    me = me_ref[0]
    load_weights(me, pieces, w_ref, sems)
    copies = Copies(osem)
    cot = copies.start(cot_any, dx_ref)
    hx_ref[0:LH] = hl_ref[0:LH]
    hx_ref[LH : LH + TOK] = h1_ref[...]
    hx_ref[LH + TOK : LH + TOK + RH] = hr_ref[...]
    hx_ref[LH + TOK + RH : EXT] = jnp.zeros((RH, D), BF16)
    table = jnp.concatenate([root_ref[...], b2_ref[...], hl_ref[LH:], summ_ref[...]], axis=0)
    hx_ref[EXT:ROWS] = mm(onehot_of(loc_ref), table).astype(BF16)
    copies.out(hx_ref, hx_o)
    await_weights(pieces, w_ref, sems, 0, 8)
    project(hx_ref, w_ref, q_ref, kv_ref)
    attend(me, n, q_ref, kv_ref, vis_ref, p_ref, o_ref)
    copies.out(o_ref, o_o)
    await_weights(pieces, w_ref, sems, 8, 32)
    a = x_ref[...] + mm(o_ref[...], wblk(w_ref, WO0, 4, 0, 32, 0, 4))
    a_ref[...] = a
    xhat, _ = norm_parts(a)
    h2_ref[...] = (xhat * gain_row(gt_ref, 1, 1)).astype(BF16)
    copies.out(h2_ref, h2_o)
    out_ref[...] = a
    feed_forward(h2_ref, w_ref, act_ref, gp_ref, out_ref, lambda c: None)
    copies.out(act_ref, act_o)
    copies.out(out_ref, out_o)
    cot.wait()
    done = {"dxb": ((dxb_ref, dxb_o),), "dub": ((dub_ref, dub_o),), "dab": ((dab_ref, dab_o),),
            "dkvb": ((dkvb_ref, dkvb_o), (dq_ref, dq_o))}

    def step(name):
        for pair in done.get(name, ()):
            copies.out(*pair)

    back_main(dx_ref, w_ref, gain_row(gt_ref, 1, 1), q_ref, kv_ref, p_ref, a_ref, gp_ref, da_ref, dxb_ref, dub_ref,
              dab_ref, dq_ref, dkvb_ref, dh_ref, dgb_ref, dkv_ref, dob_ref, step)
    table_grad(loc_ref, dh_ref, dtab_ref)
    copies.finish()


def norm_one_back(dh_ref, hal_ref, har_ref, dsum, x, gain, da_ref, acc_ref):
    acc_ref[...] = dh_ref[LH : LH + TOK]
    acc_ref[TOK - LH : TOK] += hal_ref[0:LH]
    acc_ref[0:RH] += har_ref[...]
    for s in range(NSEG):
        acc_ref[SEG * s : SEG * s + SEG] += dsum[s : s + 1, :] * (1.0 / SEG)
    xhat, rstd = norm_parts(x)
    dh = acc_ref[...]
    return da_ref[...] + norm_back(dh, xhat, rstd, gain), jnp.sum(dh * xhat, axis=0, keepdims=True)


def summed(me_ref, hal_ref, root_ref, b2_ref, dtab_ref):
    mine = dtab_ref[96:128] + hal_ref[LH:] + b2_ref[...]
    return mine + jnp.where(me_ref[0] == 0, root_ref[...], 0.0)


def bottom_kernel(me_ref, hal_ref, har_ref, root_ref, b2_ref, dtabp_ref, dhp_ref, x_ref, dap_ref, loc_ref, gt_ref, *rest,
                  np_):
    pieces, rest = rest[:np_], rest[np_:]
    (q_any, kv_any, p_any, a_any, gp_any, dga_ref, da_ref, dh_ref, dtab_ref, dgb_ref, dxb_o, dub_o, dab_o, dq_o, dkvb_o,
     w_ref, sems, q_ref, kv_ref, p_ref, a_ref, gp_ref, dx_ref, dxb_ref, dub_ref, dab_ref, dq_ref, dkvb_ref, dkv_ref,
     dob_ref, osem) = rest
    load_weights(me_ref[0], pieces, w_ref, sems)
    copies = Copies(osem)
    loads = [copies.start(*pair) for pair in
             ((gp_any, gp_ref), (a_any, a_ref), (q_any, q_ref), (kv_any, kv_ref), (p_any, p_ref))]
    dx, dga = norm_one_back(
        dhp_ref, hal_ref, har_ref, summed(me_ref, hal_ref, root_ref, b2_ref, dtabp_ref), x_ref[...],
        gain_row(gt_ref, 1, 0), dap_ref, dx_ref,
    )
    dx_ref[...] = dx
    dga_ref[...] = dga
    await_weights(pieces, w_ref, sems, 0, 32)
    loads[0].wait()
    done = {"dxb": ((dxb_ref, dxb_o),), "dub": ((dub_ref, dub_o),), "dab": ((dab_ref, dab_o),),
            "dkvb": ((dkvb_ref, dkvb_o), (dq_ref, dq_o))}

    def step(name):
        if name == "dub":
            loads[1].wait()
        if name == "attend":
            for load in loads[2:]:
                load.wait()
        for pair in done.get(name, ()):
            copies.out(*pair)

    back_main(dx_ref, w_ref, gain_row(gt_ref, 0, 1), q_ref, kv_ref, p_ref, a_ref, gp_ref, da_ref, dxb_ref, dub_ref,
              dab_ref, dq_ref, dkvb_ref, dh_ref, dgb_ref, dkv_ref, dob_ref, step)
    table_grad(loc_ref, dh_ref, dtab_ref)
    copies.finish()


def last_kernel(me_ref, hal_ref, har_ref, root_ref, b2_ref, dtab_ref, dh_ref, x_ref, da_ref, gt_ref, dx_ref, dga_ref, acc_ref):
    dx, dga = norm_one_back(
        dh_ref, hal_ref, har_ref, summed(me_ref, hal_ref, root_ref, b2_ref, dtab_ref), x_ref[...].astype(F32),
        gain_row(gt_ref, 0, 0), da_ref, acc_ref,
    )
    dx_ref[...] = dx
    dga_ref[...] = dga


def dw_kernel(me_ref, *rest, part, nouts):
    srcs, rest = rest[:9], rest[9:]
    outs, rest = rest[-12 - nouts : -12], rest[-12:]
    hx_ref, dq_ref, dkv_ref, o_ref, dab_ref, h2_ref, dub_ref, act_ref, dxb_ref, g_ref, sem, isem = rest
    copies = Copies(isem)
    loads = {}
    for i in {0: (7, 8, 5, 6), 1: (3, 4, 0, 1, 2), None: (7, 8, 5, 6, 3, 4, 0, 1, 2)}[part]:
        loads[i] = copies.start(srcs[i], rest[i])

    def put(val, base, nj, i0, j0):
        v = val.astype(BF16)
        for i in range(val.shape[0] // 16):
            for j in range(val.shape[1] // 128):
                g_ref[base + (i0 + i) * nj + j0 + j] = v[16 * i : 16 * i + 16, 128 * j : 128 * j + 128]

    def send(lo, hi):
        if nouts == 1:
            tiles = pl.ds(lo * 16, (hi - lo) * 16)
            pltpu.make_async_copy(g_ref.at[tiles], outs[0].at[tiles], sem).start()
            return
        me = me_ref[0]
        units = {}
        for u in range(lo, hi):
            units.setdefault(u // 3, []).append(u % 3)
        for d, thirds in units.items():
            core = d % 2
            rx, ry = ((me // 2) % 2) ^ (d // 2 % 2), ((me // 4) % 2) ^ (d // 4 % 2)
            ra, rb = (rx, ry) if core == 0 else (ry, rx)
            k = (d // 8 - me // 8 + 4) % 4
            t0, t1 = 16 * thirds[0], 16 * thirds[-1] + 16
            for rc in range(2):

                @pl.when((me % 2) ^ core == rc)
                def _():
                    split = PT if nouts == 4 else BT
                    e0, e1 = min(t0, split), min(t1, split)
                    if e1 > e0:
                        pltpu.make_async_copy(
                            g_ref.at[pl.ds(d * BT + e0, e1 - e0)],
                            outs[nouts // 2 * rc].at[rb, ra, k, pl.ds(e0, e1 - e0)], sem,
                        ).start()
                    l0, l1 = max(t0, split), max(t1, split)
                    if l1 > l0:
                        pltpu.make_async_copy(
                            g_ref.at[pl.ds(d * BT + l0, l1 - l0)],
                            outs[2 * rc + 1].at[k, rb, ra, pl.ds(l0 - split, l1 - l0)], sem,
                        ).start()

    if part != 1:
        loads[7].wait()
        loads[8].wait()

        def down(c, carry):
            c0 = pl.multiple_of(c * 256, 256)
            put(mm_tn(act_ref[:, pl.ds(c0, 256)], dxb_ref[...]), WD0, 4, 16 * c, 0)
            return carry

        lax.fori_loop(0, FF // 256, down, 0)
        send(64, 96)
        loads[5].wait()
        loads[6].wait()

        def up(c, carry):
            c0 = pl.multiple_of(c * 256, 256)
            put(mm_tn(h2_ref[...], dub_ref[:, pl.ds(c0, 256)]), WU0, 16, 0, 2 * c)
            return carry

        lax.fori_loop(0, FF // 256, up, 0)
        send(32, 64)
    if part != 0:
        for i in (3, 4, 0, 1, 2):
            loads[i].wait()
        for j in range(2):
            put(mm_tn(o_ref[...], dab_ref[:, 256 * j : 256 * j + 256]), WO0, 4, 0, 2 * j)
        send(24, 32)
        for j in range(2):
            put(mm_tn(hx_ref[LH : LH + TOK], dq_ref[:, 256 * j : 256 * j + 256]), QKV0, 12, 0, 2 * j)
        for j in range(4):
            put(mm_tn(hx_ref[...], dkv_ref[:, 256 * j : 256 * j + 256]), QKV0, 12, 0, 4 + 2 * j)
        send(0, 24)
    first, count = {0: (WU0, 1024), 1: (0, 512), None: (0, TILES)}[part]
    all_of = g_ref.at[pl.ds(first, count)]
    pltpu.make_async_copy(all_of, all_of, sem).wait()


def sds(shape, dtype):
    return jax.ShapeDtypeStruct(shape, dtype)


PARAMS = dict(vmem_limit_bytes=56 * 1024 * 1024)


def run(kernel, outs, ins, specs=None, scratch=(), flops=0, nbytes=0, aliases=None, **kw):
    return pl.pallas_call(
        kernel,
        out_shape=outs,
        input_output_aliases=aliases or {},
        in_specs=specs or [VM] * len(ins),
        out_specs=jax.tree.map(lambda _: VM, outs) if "out_specs" not in kw else kw["out_specs"],
        scratch_shapes=list(scratch),
        compiler_params=pltpu.CompilerParams(**PARAMS),
        cost_estimate=pl.CostEstimate(flops=flops, bytes_accessed=nbytes, transcendentals=0),
    )(*ins)


def shift(value, by, n):
    return lax.ppermute(value, "ta", [(i, i + by) for i in range(n) if 0 <= i + by < n])


def strides(n):
    out = []
    while n > 1:
        radix = 2 if n == 2 else 4
        n //= radix
        out.append((n, radix))
    return out


def spread_round(value, stride, radix, n, root=0):
    parts = [
        lax.ppermute(value, "ta", [(i ^ root, (i + j * stride) ^ root) for i in range(0, n, radix * stride)])
        for j in range(1, radix)
    ]
    return functools.reduce(jnp.add, parts, value)


def collect_round(value, stride, radix, n):
    parts = [
        lax.ppermute(value, "ta", [(i + j * stride, i) for i in range(0, n, radix * stride)])
        for j in range(1, radix)
    ]
    return functools.reduce(jnp.add, parts, value)


def from_first(value, me, n, root=0):
    value = jnp.where(me == root, value, jnp.zeros_like(value))
    for stride, radix in strides(n):
        value = spread_round(value, stride, radix, n, root)
    return value


def sum_all(value, n):
    step = 1
    while step < n:
        value = value + lax.ppermute(value, "ta", [(i, i ^ step) for i in range(n)])
        step *= 2
    return value


def tiles_of(rows, ni, nj):
    return rows.reshape(ni, 16, nj, 128).transpose(0, 2, 1, 3).reshape(ni * nj, 16, 128)


def rows_of(tiles, ni, nj):
    return tiles.reshape(ni, nj, 16, 128).transpose(0, 2, 1, 3).reshape(ni * nj * 16, 128)


PIECES = ((QKV0, 32, 12), (WO0, 32, 4), (WU0, 32, 16), (WD0, 128, 4))


def gather_plain(aligned):
    full = lax.all_gather(aligned.reshape(-1, 128), "ta", axis=0, tiled=True)
    return jnp.concatenate(
        [tiles_of(full[16 * b : 16 * (b + ni * nj)], ni, nj) for b, ni, nj in PIECES], axis=0
    )


def reduce_plain(tiles):
    full = jnp.concatenate([rows_of(tiles[b : b + ni * nj], ni, nj) for b, ni, nj in PIECES], axis=0)
    return lax.psum_scatter(full, "ta", scatter_dimension=0, tiled=True).astype(F32).reshape(-1)


def links(n, kind, by=1):
    pairs = []
    for i in range(n):
        if kind == "core":
            pairs.append((i, i ^ 1))
        elif kind == "z":
            pairs.append((i, (i + 8 * by) % n))
        else:
            pairs.append((i, i ^ (2 if (kind == "a") == (i % 2 == 0) else 4)))
    return pairs


def move(value, kind, by=1):
    return lax.ppermute(value, "ta", links(32, kind, by))


def after(value, *others):
    return lax.optimization_barrier((value,) + others)[0]


def reduce_fast(keep_p, keep_q, send_p, send_q, root, tree, n):
    up, uq = keep_p.astype(F32) + move(send_p, "core"), keep_q.astype(F32) + move(send_q, "core")
    root = collect_round(root, *tree[0], n)
    p1 = move(up[1].astype(BF16), "b")
    zs = [move(uq[k].astype(BF16), "z", k) for k in range(1, 4)]
    root = collect_round(after(root, up, uq), *tree[1], n)
    q = functools.reduce(jnp.add, zs, uq[0])
    p = up[0] + p1
    q1 = move(q[1].astype(BF16), "b")
    p1 = move(p[1].astype(BF16), "a")
    root = collect_round(after(root, p, q), *tree[2], n)
    q, p = q[0] + q1, p[0] + p1
    q1 = move(q[1].astype(BF16), "a")
    zs = [move(p[k].astype(BF16), "z", k) for k in range(1, 4)]
    root = after(root, q, p)
    p = functools.reduce(jnp.add, zs, p[0])
    return jnp.concatenate([p, q[0] + q1], axis=0), root


def to_tiles(rows, me):
    third = 3 * me + jnp.arange(3).reshape(3, 1, 1, 1)
    qkv = tiles_of(rows, 4, 12).reshape(3, 16, 16, 128)
    four = rows.reshape(3, 4, 16, 4, 128).transpose(0, 1, 3, 2, 4).reshape(3, 16, 16, 128)
    wide = rows.reshape(3, 16, 16, 128).transpose(0, 2, 1, 3)
    out = jnp.where(third < 24, qkv, jnp.where((third >= 32) & (third < 64), wide, four))
    return out.reshape(48, 16, 128)


def to_rows(tiles, me):
    third = 3 * me + jnp.arange(3).reshape(3, 1, 1)
    qkv = rows_of(tiles, 4, 12).reshape(3, 256, 128)
    four = tiles.reshape(3, 4, 4, 16, 128).transpose(0, 1, 3, 2, 4).reshape(3, 256, 128)
    wide = tiles.reshape(3, 16, 16, 128).transpose(0, 2, 1, 3).reshape(3, 256, 128)
    out = jnp.where(third < 24, qkv, jnp.where((third >= 32) & (third < 64), wide, four))
    return out.reshape(-1)


def per_device(frames, cotangent, mem_index, master, moment, second, average):
    n = lax.axis_size("ta")
    me = lax.axis_index("ta")
    layers, share = master.shape
    step = 2 * D // n
    tail = shift(master[:, share - 2 * D :], 1, n)
    ext = jnp.concatenate([tail, master], axis=1)
    aligned = lax.dynamic_slice(ext, (0, 2 * D - step * me), (layers, MATS // n)).astype(BF16)
    gains = master[:, share - 2 * D :].astype(BF16).reshape(1, 16, 128)
    fast = n == GROUPS
    summ = run(first_kernel, sds((NSEG, D), BF16), (frames,))
    ahead = shift(jnp.concatenate([frames[TOK - LH :], summ], axis=0), 1, n)
    halo, behind2 = (ahead, shift(frames[:RH], -1, n)), shift(summ, 2, n)
    if fast:
        tiles = [to_tiles(aligned[l].reshape(-1, 128), me) for l in range(layers)]
        block = jnp.concatenate([tiles[0], gains])
        p, q = block[:PT], block[PT:]
        root = jnp.where(me == 0, summ, jnp.zeros_like(summ))
        (s0, r0), (s1, r1), (s2, r2) = strides(n)
        own = [p] + [move(p, "z", k) for k in range(1, 4)]
        qa, qb = move(q, "a"), move(q, "b")
        root = spread_round(root, s0, r0, n)
        own = after(jnp.stack(own), root)
        pa, pb = move(own, "a"), move(own, "b")
        qs = jnp.stack([q, qa, qb, move(qa, "b")])
        root = spread_round(root, s1, r1, n)
        pa = after(pa, root)
        pab = move(pa, "b")
        qs = after(qs, root)
        qz = [qs] + [move(qs, "z", k) for k in range(1, 4)]
        ps = [own, pa, pb, pab]
        root = spread_round(root, s2, r2, n)
        weights = [tuple(ps + [move(v, "core") for v in ps] + qz + [move(v, "core") for v in qz])]
        for l in range(1, layers):
            weights.append((lax.all_gather(after(tiles[l], own, pa), "ta", axis=0, tiled=True),))
    else:
        weights = [(gather_plain(aligned[l]),) for l in range(layers)]
        weights[0] += (from_first(gains[0], me, n, n - 1),)
        root = from_first(summ, me, n)
    wscr = [pltpu.VMEM((TILES, 16, 128), BF16), pltpu.SemaphoreType.DMA((2, GROUPS + 1))]
    mev = me.astype(jnp.int32).reshape(1)

    first_seg = me * NSEG
    seg_ids = first_seg + jnp.arange(NSEG, dtype=jnp.int32)
    slot = jnp.arange(MEM, dtype=jnp.int32)
    loc = jnp.where(slot[None, :] == 0, mem_index, mem_index - first_seg + 96).reshape(-1, 1)
    loc = jnp.broadcast_to(loc, (NSEG * MEM, 128))
    vis = (mem_index < seg_ids[:, None]).astype(F32).reshape(-1, 1)
    vis = jnp.broadcast_to(vis, (NSEG * MEM, 128))

    def vmem(*shape_types):
        return [pltpu.VMEM(shape, dtype) for shape, dtype in shape_types]

    tf, tb = ((TOK, D), F32), ((TOK, D), BF16)
    wide, rows16, kv16 = ((TOK, FF), BF16), ((ROWS, D), BF16), ((ROWS, 2 * D), BF16)
    prob, rows32, kv32 = ((NBLK * 4, KB, 128), BF16), ((ROWS, D), F32), ((ROWS, 2 * D), F32)
    drow, dtab_t = ((1, D), F32), ((128, D), F32)

    def call(kernel, ins, specs, outs, scratch, aliases=None, flops=3 * 10**9):
        return run(
            kernel, tuple(sds(*o) for o, _ in outs), tuple(ins), specs=specs,
            out_specs=tuple(VM if keep else ANYS for _, keep in outs), scratch=scratch,
            aliases=aliases, flops=flops, nbytes=10**7,
        )

    def sems(count):
        return [pltpu.SemaphoreType.DMA((count,))]

    saved = (rows16, tb, kv16, prob, tb, tf, tb, wide, wide)
    low = call(
        functools.partial(low_kernel, np_=len(weights[0]), n=n),
        (mev, frames, *halo, root, behind2, summ, loc, vis) + weights[0],
        [SM] + [VM] * 8 + [ANYS] * len(weights[0]),
        [(tf, True), (tb, True), (((NSEG, D), BF16), True), (((16, 128), BF16), True)] + [(t, False) for t in saved],
        wscr + vmem(*saved) + sems(9),
    )
    x1, h1, summ, gt, hx0, q0, kv0, p0, o0, a0, h20, gp0, act0 = low
    halo = (shift(jnp.concatenate([h1[TOK - LH :], summ], axis=0), 1, n), shift(h1[:RH], -1, n))
    behind2 = shift(summ, 2, n)
    root = from_first(summ, me, n)
    top = call(
        functools.partial(top_kernel, np_=len(weights[1]), n=n),
        (mev, x1, h1, *halo, root, behind2, summ, loc, vis, gt, cotangent) + weights[1],
        [SM] + [VM] * 10 + [ANYS] * (1 + len(weights[1])),
        [(tf, False), (tf, True), (rows32, True), (dtab_t, True), (drow, True)]
        + [(t, False) for t in (rows16, tb, tb, wide, tb, wide, tb, tb, kv16)],
        wscr + vmem(rows16, tb, kv16, prob, tb, tf, tb, wide, wide, tf, tf, tb, wide, tb, tb, kv16, kv32, tb) + sems(11),
        flops=8 * 10**9,
    )
    output, da, dh, dtab, dgb1, hx1, o1, h21, act1, dxb, dub, dab, dq, dkvb = top
    dws = vmem(rows16, tb, kv16, tb, tb, tb, wide, wide, tb, ((TILES, 16, 128), BF16))
    dws += [pltpu.SemaphoreType.DMA] + sems(9)
    tree = strides(n)[::-1]

    def backward_moves(dh, dtab):
        behind = shift(jnp.concatenate([dh[:LH], dtab[64:96]], axis=0), -1, n)
        return behind, shift(dh[LH + TOK : LH + TOK + RH], 1, n), shift(dtab[32:64], -2, n)

    hal, har, b2 = backward_moves(dh, dtab)
    root = dtab[:NSEG]
    plain = (((TILES, 16, 128), BF16), False)
    ins = [mev, hx1, dq, dkvb, o1, dab, h21, dub, act1, dxb]
    half = call(
        functools.partial(dw_kernel, part=0, nouts=1), ins, [SM] + [ANYS] * 9, [plain], dws, flops=2 * 10**9
    )
    root = collect_round(root, *tree[0], n)
    ins[-1] = after(dxb, root, hal, har, b2)
    root = after(root, half[0])
    grads = call(
        functools.partial(dw_kernel, part=1, nouts=1), ins + list(half), [SM] + [ANYS] * 10, [plain], dws,
        aliases={10: 0}, flops=10**9,
    )
    for level in tree[1:]:
        root = collect_round(root, *level, n)
    reduced = [None] * layers
    if fast:
        part = lax.psum_scatter(grads[0], "ta", scatter_dimension=0, tiled=True)
        reduced[1] = to_rows(part.astype(F32), me)
    else:
        reduced[1] = reduce_plain(grads[0])
    bottom = call(
        functools.partial(bottom_kernel, np_=len(weights[0])),
        (mev, hal, har, root, b2, dtab, dh, x1, da, loc, gt) + weights[0] + (q0, kv0, p0, a0, gp0),
        [SM] + [VM] * 10 + [ANYS] * (len(weights[0]) + 5),
        [(drow, True), (tf, True), (rows32, True), (dtab_t, True), (drow, True)]
        + [(t, False) for t in (tb, wide, tb, tb, kv16)],
        wscr + vmem(tb, kv16, prob, tf, wide, tf, tb, wide, tb, tb, kv16, kv32, tb) + sems(10),
        flops=5 * 10**9,
    )
    dga1, da, dh, dtab, dgb0, dxb, dub, dab, dq, dkvb = bottom
    if fast:
        pq = [(((2, 2, 4, PT, 16, 128), BF16), False), (((4, 2, 2, BT - PT, 16, 128), BF16), False)]
        gouts = pq + pq
    else:
        gouts = [plain]
    grads = call(
        functools.partial(dw_kernel, part=None, nouts=len(gouts)),
        (mev, hx0, dq, dkvb, o0, dab, h20, dub, act0, dxb), [SM] + [ANYS] * 9, gouts, dws,
    )
    hal, har, b2 = backward_moves(dh, dtab)
    root = dtab[:NSEG]
    if fast:
        total, root = reduce_fast(*grads, root, tree, n)
        reduced[0] = to_rows(total, me)
    else:
        reduced[0] = reduce_plain(grads[0])
        for level in tree:
            root = collect_round(root, *level, n)
    dx, dga0 = call(
        functools.partial(last_kernel), (mev, hal, har, root, b2, dtab, dh, frames, da, gt),
        [SM] + [VM] * 9, [(tf, True), (drow, True)], vmem(tf), flops=10**7,
    )
    gain_rows = [jnp.concatenate([dga0, dgb0], axis=1), jnp.concatenate([dga1, dgb1], axis=1)]

    gsum = sum_all(jnp.concatenate(gain_rows, axis=0), n)
    own = jnp.stack(reduced)
    head = jnp.where(me == n - 1, gsum, shift(own[:, : 2 * D], -1, n))
    grad = lax.dynamic_slice(jnp.concatenate([own, head], axis=1), (0, step * me), (layers, share))
    gain_out = lax.dynamic_slice(gsum, (0, step * me), (layers, step))
    new_moment = 0.5 * moment + 0.5 * grad
    new_second = 0.5 * second + 0.5 * grad * grad
    correction = 1.0 - 0.5**STEP
    update = new_moment / correction / (jnp.sqrt(new_second / correction) + 1e-08) + 0.1 * master
    new_master = master - 0.08 * update
    new_average = 0.9 * average + 0.1 * new_master
    return (output, dx, gain_out, new_moment, new_second, new_master, new_average)


def solution(mesh):
    rows, flat = P("ta", None), P(None, "ta")
    return jax.shard_map(
        per_device,
        mesh=mesh,
        in_specs=(rows, rows, rows, flat, flat, flat, flat),
        out_specs=(rows, rows, flat, flat, flat, flat, flat),
        check_vma=False,
    )
```

time: 588 us -> 394 us (0.67)
  the two profiles are of different devices: /device:TPU:20 before, /device:TPU:15 now
where the time goes in v2:
time: 394 us; the launch traced here: 386 us
  starting transfers between devices  118 us (30%)
  Pallas kernels  109 us (28%)
  waiting for transfers between devices  104 us (26%)
  other arithmetic  23.1 us (6%)
  local copies, waits for them, and re-layouts  16.3 us (4%)
  between operations  15.6 us (4%)
    pallas_call x8, Pallas kernels, run(): pl.pallas_call(kernel, out_shape=outs, input_output_aliases=aliases or {}...  109 us
    ppermute x32, waiting for transfers between devices, move(): return lax.ppermute(value, 'ta', links(32, kind, by))  63.8 us
    ppermute x14, starting transfers between devices, shift(): lax.ppermute(value, 'ta', [(i, i + by) for i in range(n) if 0 <= i + by <...  57.7 us
    ppermute x32, starting transfers between devices, move(): return lax.ppermute(value, 'ta', links(32, kind, by))  34.1 us
    ppermute x14, waiting for transfers between devices, shift(): lax.ppermute(value, 'ta', [(i, i + by) for i in range(n) if 0 <= i + by <...  29.1 us
    ppermute x14, starting transfers between devices, collect_round(): lax.ppermute(value, 'ta', [(i + j * stride, i) for i in range(0, n, radix...  11.6 us
    ppermute x14, starting transfers between devices, spread_round(): lax.ppermute(value, 'ta', [(i ^ root, i + j * stride ^ root) for i in ran...  10.5 us
    ppermute x5, waiting for transfers between devices, sum_all(): value = value + lax.ppermute(value, 'ta', [(i, i ^ step) for i in range(n)])  9.41 us
  transfers between devices with their start and end apart: 81, of which 21 were waited for; matrix products, arithmetic and copies ran while one was open for 7% of the time, Pallas kernels for 18%

profile of v2, /device:TPU:15, one launch (start us, length us, event | category | flops | bytes accessed | tf_op | source)
XLA Modules:
  0.0 386.2 jit_solution(464553046569664318)
XLA Ops:
  12.2 4.3 %collective-permute-start.10 = (bf16[2,1024]{1,0:T(2,128)(2,1)S(1)}, bf16[2,1024]{1,0:T(2,128)(2,1)S(1)}, u32[]{:S(2)}, u32[]{:S(2)}) collective-permute-start(bf16[2,1024]{1,0:T(2,128)(2,1)S(1)} %slice.233), channel_id=1, source_target_pairs={{0,1},{1,2},{2,3},{3,4},{4,5},{5,6},{6,7},{7,8},{8,9},{9,10},{10,1... | collective-permute-start | bytes 12296 | tf_op jit(solution)/shard_map/ppermute | solution.py:578
  27.4 4.9 %collective-permute-done.11 = bf16[36,16,128]{2,1,0:T(8,128)(2,1)S(1)} collective-permute-done((bf16[36,16,128]{2,1,0:T(8,128)(2,1)S(1)}, bf16[36,16,128]{2,1,0:T(8,128)(2,1)S(1)}, u32[]{:S(2)}, u32[]{:S(2)}) %collective-permute-start.11) | collective-permute-done | bytes 147488 | tf_op jit(solution)/shard_map/ppermute | solution.py:657
  32.3 4.7 %collective-permute-done.12 = bf16[36,16,128]{2,1,0:T(8,128)(2,1)S(1)} collective-permute-done((bf16[36,16,128]{2,1,0:T(8,128)(2,1)S(1)}, bf16[36,16,128]{2,1,0:T(8,128)(2,1)S(1)}, u32[]{:S(2)}, u32[]{:S(2)}) %collective-permute-start.12) | collective-permute-done | bytes 147488 | tf_op jit(solution)/shard_map/ppermute | solution.py:657
  39.3 7.0 %collective-permute-done.14.rest_1_ = bf16[4,36,16,128]{3,2,1,0:T(8,128)(2,1)S(1)} collective-permute-done((bf16[4,36,16,128]{3,2,1,0:T(8,128)(2,1)S(1)}, bf16[4,36,16,128]{3,2,1,0:T(8,128)(2,1)S(1)}, u32[]{:S(2)}, u32[]{:S(2)}) %collective-permute-start.14) | collective-permute-done | bytes 589856 | tf_op jit(solution)/shard_map/ppermute | solution.py:657
  46.4 3.6 collective-permute-start.1
  55.7 5.3 %collective-permute-start.9 = (bf16[32,512]{1,0:T(8,128)(2,1)S(1)}, bf16[32,512]{1,0:T(8,128)(2,1)S(1)}, u32[]{:S(2)}, u32[]{:S(2)}) collective-permute-start(bf16[32,512]{1,0:T(8,128)(2,1)S(1)} %copy-done.5), channel_id=1, source_target_pairs={{0,2},{1,3},{2,4},{3,5},{4,6},{5,7},{6,8},{7,9},{8,10},{9,11},{10,... | collective-permute-start | bytes 98312 | tf_op jit(solution)/shard_map/ppermute | solution.py:578
  61.0 8.9 %collective-permute-done.9.b2_ref = bf16[32,512]{1,0:T(8,128)(2,1)S(1)} collective-permute-done((bf16[32,512]{1,0:T(8,128)(2,1)S(1)}, bf16[32,512]{1,0:T(8,128)(2,1)S(1)}, u32[]{:S(2)}, u32[]{:S(2)}) %collective-permute-start.9) | collective-permute-done | bytes 32800 | tf_op jit(solution)/shard_map/ppermute | solution.py:578
  80.6 7.0 %collective-permute-done.26.rest_11_ = bf16[4,13,16,128]{3,2,1,0:T(8,128)(2,1)} collective-permute-done((bf16[4,13,16,128]{3,2,1,0:T(8,128)(2,1)S(1)}, bf16[4,13,16,128]{3,2,1,0:T(8,128)(2,1)}, u32[]{:S(2)}, u32[]{:S(2)}) %collective-permute-start.26) | collective-permute-done | bytes 213024 | tf_op jit(solution)/shard_map/ppermute | solution.py:657
  90.5 3.0 collective-permute-done.29.rest_14_
  96.9 23.4 %shard_map.127 = (f32[512,512]{1,0:T(8,128)}, bf16[512,512]{1,0:T(8,128)(2,1)}, bf16[32,512]{1,0:T(8,128)(2,1)}, bf16[16,128]{1,0:T(8,128)(2,1)}, bf16[704,512]{...) custom-call(s32[1]{0:T(128)} %bitcast.me_ref, ...), custom_call_target="tpu_custom_call" | custom-call | flops 3000000000 | bytes 10000000 | tf_op jit(solution)/shard_map/pallas_call | solution.py:565
  125.9 14.5 %collective-permute-start.31 = (bf16[64,512]{1,0:T(8,128)(2,1)S(1)}, bf16[64,512]{1,0:T(8,128)(2,1)S(1)}, u32[]{:S(2)}, u32[]{:S(2)}) collective-permute-start(bf16[64,512]{1,0:T(8,128)(2,1)S(1)} %pad_maximum_fusion.6), channel_id=1, source_target_pairs={{0,1},{1,2},{2,3},{3,4},{4,5},{5,6},{6,7},{7,8},{8,9},{9,10},{10,1... | collective-permute-start | bytes 196616 | tf_op jit(solution)/shard_map/ppermute | solution.py:578
  144.4 3.4 collective-permute-start.32
  151.9 33.5 %shard_map.128 = (f32[512,512]{1,0:T(8,128)}, f32[512,512]{1,0:T(8,128)}, f32[704,512]{1,0:T(8,128)}, f32[128,512]{1,0:T(8,128)}, f32[1,512]{1,0:T(1,128)}, /*in...) custom-call(s32[1]{0:T(128)} %bitcast.me_ref, ...), custom_call_target="tpu_custom_call" | custom-call | flops 8000000000 | bytes 10000000 | tf_op jit(solution)/shard_map/pallas_call | solution.py:565
  187.5 8.7 %shard_map.129.rest_9_ = bf16[1536,16,128]{2,1,0:T(8,128)(2,1)} custom-call(s32[1]{0:T(128)} %bitcast.me_ref, bf16[704,512]{1,0:T(8,128)(2,1)} %get-tuple-element.70.rest_0_, bf16[512,512]{1,0:T(8,128)(2,1)} %get-tuple-element.71.rest_1_, bf16[704,1024]{1,0:T(8,128)(2,1)} %get-tuple-element.72.rest_2_, bf16[512,512]{1,0:T(8,128)(2,1)} %get-tuple-element.73.rest_3_, ...), custom_call_target="tpu_custom_call" | custom-call | flops 2000000000 | bytes 10000000 | tf_op jit(solution)/shard_map/pallas_call | solution.py:565
  199.9 3.8 collective-permute-start.42
  211.4 3.9 %collective-permute-done.50.b2_ref = f32[32,512]{1,0:T(8,128)S(1)} collective-permute-done((f32[32,512]{1,0:T(8,128)S(1)}, f32[32,512]{1,0:T(8,128)S(1)}, u32[]{:S(2)}, u32[]{:S(2)}) %collective-permute-start.50) | collective-permute-done | bytes 65568 | tf_op jit(solution)/shard_map/ppermute | solution.py:578
  215.3 5.0 %shard_map.133 = bf16[1536,16,128]{2,1,0:T(8,128)(2,1)} custom-call(s32[1]{0:T(128)} %bitcast.me_ref, bf16[704,512]{1,0:T(8,128)(2,1)} %get-tuple-element.70.rest_0_, bf16[512,512]{1,0:T(8,128)(2,1)} %get-tuple-element.71.rest_1_, bf16[704,1024]{1,0:T(8,128)(2,1)} %get-tuple-element.72.rest_2_, ...), custom_call_target="tpu_custom_call", output_to_operand_aliasing={{}: (10, {})} | custom-call | flops 1000000000 | bytes 10000000 | tf_op jit(solution)/shard_map/pallas_call | solution.py:565
  220.3 21.9 %shard_map.130 = (f32[1,512]{1,0:T(1,128)}, f32[512,512]{1,0:T(8,128)}, f32[704,512]{1,0:T(8,128)}, f32[128,512]{1,0:T(8,128)}, f32[1,512]{1,0:T(1,128)}, /*inde...) custom-call(s32[1]{0:T(128)} %bitcast.me_ref, ...), custom_call_target="tpu_custom_call" | custom-call | flops 5000000000 | bytes 10000000 | tf_op jit(solution)/shard_map/pallas_call | solution.py:565
  242.3 10.4 %shard_map.131 = (bf16[2,2,4,36,16,128]{5,4,3,2,1,0:T(8,128)(2,1)}, bf16[4,2,2,12,16,128]{5,4,3,2,1,0:T(8,128)(2,1)}, bf16[2,2,4,36,16,128]{5,4,3,2,1,0:T(8,128)(2,1)}, bf16[4,2,2,12,16,128]{5,4,3,2,1,0:T(8,128)(2,1)}) custom-call(s32[1]{0:T(128)} %bitcast.me_ref, bf16[704,512]{1,0:T(8,128)(2,1)} %get-tuple-element.88.rest_0_, ...), custom_call_target="tpu_custom_call" | custom-call | flops 3000000000 | bytes 10000000 | tf_op jit(solution)/shard_map/pallas_call | solution.py:565
  264.2 4.0 %collective-permute-start.60 = (bf16[2,2,12,16,128]{4,3,2,1,0:T(8,128)(2,1)S(1)}, bf16[2,2,12,16,128]{4,3,2,1,0:T(8,128)(2,1)S(1)}, u32[]{:S(2)}, u32[]{:S(2)}) collective-permute-start(bf16[2,2,12,16,128]{4,3,2,1,0:T(8,128)(2,1)S(1)} %get-tuple-element.127), channel_id=1, source_target_pairs={{0,8},{1,9},{2,10},{3,11},{4,12},{5,13},{6,14},{7,15},{8,16},{9,17... | collective-permute-start | bytes 589832 | tf_op jit(solution)/shard_map/ppermute | solution.py:657
  269.5 18.4 %collective-permute-done.60 = bf16[2,2,12,16,128]{4,3,2,1,0:T(8,128)(2,1)S(1)} collective-permute-done((bf16[2,2,12,16,128]{4,3,2,1,0:T(8,128)(2,1)S(1)}, bf16[2,2,12,16,128]{4,3,2,1,0:T(8,128)(2,1)S(1)}, u32[]{:S(2)}, u32[]{:S(2)}) %collective-permute-start.60) | collective-permute-done | bytes 196640 | tf_op jit(solution)/shard_map/ppermute | solution.py:657
  287.9 11.8 %collective-permute-done.61 = bf16[2,2,12,16,128]{4,3,2,1,0:T(8,128)(2,1)S(1)} collective-permute-done((bf16[2,2,12,16,128]{4,3,2,1,0:T(8,128)(2,1)S(1)}, bf16[2,2,12,16,128]{4,3,2,1,0:T(8,128)(2,1)S(1)}, u32[]{:S(2)}, u32[]{:S(2)}) %collective-permute-start.61) | collective-permute-done | bytes 196640 | tf_op jit(solution)/shard_map/ppermute | solution.py:657
  302.4 3.9 %collective-permute-start.67 = (bf16[4,36,16,128]{3,2,1,0:T(8,128)(2,1)S(1)}, bf16[4,36,16,128]{3,2,1,0:T(8,128)(2,1)S(1)}, u32[]{:S(2)}, u32[]{:S(2)}) collective-permute-start(bf16[4,36,16,128]{3,2,1,0:T(8,128)(2,1)S(1)} %fusion.8), channel_id=1, source_target_pairs={{0,2},{1,5},{2,0},{3,7},{4,6},{5,1},{6,4},{7,3},{8,10},{9,13},{10,... | collective-permute-start | bytes 1769480 | tf_op jit(solution)/shard_map/ppermute | solution.py:657
  308.4 6.8 %collective-permute-start.51 = (f32[64,512]{1,0:T(8,128)S(1)}, f32[64,512]{1,0:T(8,128)S(1)}, u32[]{:S(2)}, u32[]{:S(2)}) collective-permute-start(f32[64,512]{1,0:T(8,128)S(1)} %pad_maximum_fusion.4), channel_id=1, source_target_pairs={{1,0},{2,1},{3,2},{4,3},{5,4},{6,5},{7,6},{8,7},{9,8},{10,9},{11,1... | collective-permute-start | bytes 393224 | tf_op jit(solution)/shard_map/ppermute | solution.py:578
  318.6 5.9 %collective-permute-done.68.b2_ref = f32[32,512]{1,0:T(8,128)S(1)} collective-permute-done((f32[32,512]{1,0:T(8,128)S(1)}, f32[32,512]{1,0:T(8,128)S(1)}, u32[]{:S(2)}, u32[]{:S(2)}) %collective-permute-start.68) | collective-permute-done | bytes 65568 | tf_op jit(solution)/shard_map/ppermute | solution.py:578
  325.2 3.8 shard_map.132
  333.0 3.1 collective-permute-start.77
  338.0 5.9 %collective-permute-start.75 = (bf16[36,16,128]{2,1,0:T(8,128)(2,1)S(1)}, bf16[36,16,128]{2,1,0:T(8,128)(2,1)S(1)}, u32[]{:S(2)}, u32[]{:S(2)}) collective-permute-start(bf16[36,16,128]{2,1,0:T(8,128)(2,1)S(1)} %get-tuple-element.132), channel_id=1, source_target_pairs={{0,16},{1,17},{2,18},{3,19},{4,20},{5,21},{6,22},{7,23},{8,24},{9,... | collective-permute-start | bytes 442376 | tf_op jit(solution)/shard_map/ppermute | solution.py:657
  345.1 9.4 %collective-permute-done.72 = f32[2,1024]{1,0:T(2,128)S(1)} collective-permute-done((f32[2,1024]{1,0:T(2,128)S(1)}, f32[2,1024]{1,0:T(2,128)S(1)}, u32[]{:S(2)}, u32[]{:S(2)}) %collective-permute-start.72) | collective-permute-done | bytes 8224 | tf_op jit(solution)/shard_map/ppermute | solution.py:616
  355.1 3.6 collective-permute-done.76
  367.2 3.9 %collective-permute-done.78 = f32[2,1024]{1,0:T(2,128)S(1)} collective-permute-done((f32[2,1024]{1,0:T(2,128)S(1)}, f32[2,1024]{1,0:T(2,128)S(1)}, u32[]{:S(2)}, u32[]{:S(2)}) %collective-permute-start.78) | collective-permute-done | bytes 8224 | tf_op jit(solution)/shard_map/ppermute | solution.py:578
  372.5 6.7 %multiply_add_fusion.1 = (f32[2,98336]{1,0:T(2,128)}, f32[2,98336]{1,0:T(2,128)}, f32[2,98336]{1,0:T(2,128)}, f32[2,98336]{1,0:T(2,128)}) fusion(f32[2,98336]{1,0:T(2,128)} %param.13, f32[2,98336]{1,0:T(2,128)S(1)} %copy-done, f32[2,98336]{1,0:T(2,128)} %param.12, f32[2,98336]{1,0:T(2,128)} %param.11, s32[]{:T(128)S(6)} %select_n.103, ...), kind=kLoop, calls=%fused_computation.19 | loop fusion | flops 3736768 | bytes 7088132 | tf_op jit(solution)/shard_map/add | solution.py:865
  (294 shorter events, 106.2 us)
Async XLA Ops:
  7.2 144.1 %all-gather.2.cloned.1.call-start = ((), (), s32[]{:S(2)}) async-start(), calls=%async_computation.1 | async-start | bytes 6488064 | tf_op jit(solution)/shard_map/all_gather | solution.py:735
  9.4 14.7 %collective-permute-start.2 = (bf16[32,512]{1,0:T(8,128)(2,1)S(1)}, bf16[32,512]{1,0:T(8,128)(2,1)S(1)}, u32[]{:S(2)}, u32[]{:S(2)}) collective-permute-start(bf16[32,512]{1,0:T(8,128)(2,1)S(1)} %broadcast_select_fusion.1), channel_id=1, source_target_pairs={{0,8}} | collective-permute-start | bytes 98312 | tf_op jit(solution)/shard_map/ppermute | solution.py:592
  10.1 16.3 %collective-permute-start.3 = (bf16[32,512]{1,0:T(8,128)(2,1)S(1)}, bf16[32,512]{1,0:T(8,128)(2,1)S(1)}, u32[]{:S(2)}, u32[]{:S(2)}) collective-permute-start(bf16[32,512]{1,0:T(8,128)(2,1)S(1)} %broadcast_select_fusion.1), channel_id=1, source_target_pairs={{0,16}} | collective-permute-start | bytes 98312 | tf_op jit(solution)/shard_map/ppermute | solution.py:592
  10.7 15.6 %collective-permute-start.4 = (bf16[32,512]{1,0:T(8,128)(2,1)S(1)}, bf16[32,512]{1,0:T(8,128)(2,1)S(1)}, u32[]{:S(2)}, u32[]{:S(2)}) collective-permute-start(bf16[32,512]{1,0:T(8,128)(2,1)S(1)} %broadcast_select_fusion.1), channel_id=1, source_target_pairs={{0,24}} | collective-permute-start | bytes 98312 | tf_op jit(solution)/shard_map/ppermute | solution.py:592
  24.0 13.0 %collective-permute-start.12 = (bf16[36,16,128]{2,1,0:T(8,128)(2,1)S(1)}, bf16[36,16,128]{2,1,0:T(8,128)(2,1)S(1)}, u32[]{:S(2)}, u32[]{:S(2)}) collective-permute-start(bf16[36,16,128]{2,1,0:T(8,128)(2,1)S(1)} %get-tuple-element.140), channel_id=1, source_target_pairs={{0,16},{1,17},{2,18},{3,19},{4,20},{5,21},{6,22},{7,23},{8,24},{9,... | collective-permute-start | bytes 442376 | tf_op jit(solution)/shard_map/ppermute | solution.py:657
  46.2 313.4 %reduce-scatter.2.cloned.1.call-start = ((), (), s32[]{:S(2)}) async-start(), calls=%async_computation.2 | async-start | bytes 6488064 | tf_op jit(solution)/shard_map/reduce_scatter | solution.py:817
  46.4 14.5 %collective-permute-start.1 = (bf16[16,512]{1,0:T(8,128)(2,1)S(1)}, bf16[16,512]{1,0:T(8,128)(2,1)S(1)}, u32[]{:S(2)}, u32[]{:S(2)}) collective-permute-start(bf16[16,512]{1,0:T(8,128)(2,1)S(1)} %slice.120), channel_id=1, source_target_pairs={{1,0},{2,1},{3,2},{4,3},{5,4},{6,5},{7,6},{8,7},{9,8},{10,9},{11,1... | collective-permute-start | bytes 49160 | tf_op jit(solution)/shard_map/ppermute | solution.py:578
  51.9 37.0 %collective-permute-start.15 = (bf16[4,36,16,128]{3,2,1,0:T(8,128)(2,1)S(1)}, bf16[4,36,16,128]{3,2,1,0:T(8,128)(2,1)S(1)}, u32[]{:S(2)}, u32[]{:S(2)}) collective-permute-start(bf16[4,36,16,128]{3,2,1,0:T(8,128)(2,1)S(1)} %pad_maximum_fusion.rest_0_), channel_id=1, source_target_pairs={{0,4},{1,3},{2,6},{3,1},{4,0},{5,7},{6,2},{7,5},{8,12},{9,11},{10,... | collective-permute-start | bytes 1769480 | tf_op jit(solution)/shard_map/ppermute | solution.py:657
  53.3 36.0 %collective-permute-start.16 = (bf16[4,36,16,128]{3,2,1,0:T(8,128)(2,1)S(1)}, bf16[4,36,16,128]{3,2,1,0:T(8,128)(2,1)}, u32[]{:S(2)}, u32[]{:S(2)}) collective-permute-start(bf16[4,36,16,128]{3,2,1,0:T(8,128)(2,1)S(1)} %collective-permute-done.14.rest_1_), channel_id=1, source_target_pairs={{0,4},{1,3},{2,6},{3,1},{4,0},{5,7},{6,2},{7,5},{8,12},{9,11},{10,... | collective-permute-start | bytes 1769480 | tf_op jit(solution)/shard_map/ppermute | solution.py:657
  54.9 25.2 %collective-permute-start.24 = (bf16[4,13,16,128]{3,2,1,0:T(8,128)(2,1)S(1)}, bf16[4,13,16,128]{3,2,1,0:T(8,128)(2,1)S(1)}, u32[]{:S(2)}, u32[]{:S(2)}) collective-permute-start(bf16[4,13,16,128]{3,2,1,0:T(8,128)(2,1)S(1)} %pad_maximum_fusion.2.rest_8_), channel_id=1, source_target_pairs={{0,8},{1,9},{2,10},{3,11},{4,12},{5,13},{6,14},{7,15},{8,16},{9,17... | collective-permute-start | bytes 638984 | tf_op jit(solution)/shard_map/ppermute | solution.py:657
  55.7 14.3 %collective-permute-start.9 = (bf16[32,512]{1,0:T(8,128)(2,1)S(1)}, bf16[32,512]{1,0:T(8,128)(2,1)S(1)}, u32[]{:S(2)}, u32[]{:S(2)}) collective-permute-start(bf16[32,512]{1,0:T(8,128)(2,1)S(1)} %copy-done.5), channel_id=1, source_target_pairs={{0,2},{1,3},{2,4},{3,5},{4,6},{5,7},{6,8},{7,9},{8,10},{9,11},{10,... | collective-permute-start | bytes 98312 | tf_op jit(solution)/shard_map/ppermute | solution.py:578
  60.9 19.5 %collective-permute-start.25 = (bf16[4,13,16,128]{3,2,1,0:T(8,128)(2,1)S(1)}, bf16[4,13,16,128]{3,2,1,0:T(8,128)(2,1)}, u32[]{:S(2)}, u32[]{:S(2)}) collective-permute-start(bf16[4,13,16,128]{3,2,1,0:T(8,128)(2,1)S(1)} %pad_maximum_fusion.2.rest_8_), channel_id=1, source_target_pairs={{0,16},{1,17},{2,18},{3,19},{4,20},{5,21},{6,22},{7,23},{8,24},{9,... | collective-permute-start | bytes 638984 | tf_op jit(solution)/shard_map/ppermute | solution.py:657
  123.1 17.3 %collective-permute-start.36 = (bf16[32,512]{1,0:T(8,128)(2,1)S(1)}, bf16[32,512]{1,0:T(8,128)(2,1)S(1)}, u32[]{:S(2)}, u32[]{:S(2)}) collective-permute-start(bf16[32,512]{1,0:T(8,128)(2,1)S(1)} %add_add_fusion.5), channel_id=1, source_target_pairs={{0,2},{8,10},{16,18},{24,26}} | collective-permute-start | bytes 98312 | tf_op jit(solution)/shard_map/ppermute | solution.py:592
  123.8 16.6 %collective-permute-start.37 = (bf16[32,512]{1,0:T(8,128)(2,1)S(1)}, bf16[32,512]{1,0:T(8,128)(2,1)S(1)}, u32[]{:S(2)}, u32[]{:S(2)}) collective-permute-start(bf16[32,512]{1,0:T(8,128)(2,1)S(1)} %add_add_fusion.5), channel_id=1, source_target_pairs={{0,4},{8,12},{16,20},{24,28}} | collective-permute-start | bytes 98312 | tf_op jit(solution)/shard_map/ppermute | solution.py:592
  124.5 16.0 %collective-permute-start.38 = (bf16[32,512]{1,0:T(8,128)(2,1)S(1)}, bf16[32,512]{1,0:T(8,128)(2,1)S(1)}, u32[]{:S(2)}, u32[]{:S(2)}) collective-permute-start(bf16[32,512]{1,0:T(8,128)(2,1)S(1)} %add_add_fusion.5), channel_id=1, source_target_pairs={{0,6},{8,14},{16,22},{24,30}} | collective-permute-start | bytes 98312 | tf_op jit(solution)/shard_map/ppermute | solution.py:592
  125.9 25.4 %collective-permute-start.31 = (bf16[64,512]{1,0:T(8,128)(2,1)S(1)}, bf16[64,512]{1,0:T(8,128)(2,1)S(1)}, u32[]{:S(2)}, u32[]{:S(2)}) collective-permute-start(bf16[64,512]{1,0:T(8,128)(2,1)S(1)} %pad_maximum_fusion.6), channel_id=1, source_target_pairs={{0,1},{1,2},{2,3},{3,4},{4,5},{5,6},{6,7},{7,8},{8,9},{9,10},{10,1... | collective-permute-start | bytes 196616 | tf_op jit(solution)/shard_map/ppermute | solution.py:578
  199.9 11.5 %collective-permute-start.42 = (f32[16,512]{1,0:T(8,128)S(1)}, f32[16,512]{1,0:T(8,128)S(1)}, u32[]{:S(2)}, u32[]{:S(2)}) collective-permute-start(f32[16,512]{1,0:T(8,128)S(1)} %slice.130), channel_id=1, source_target_pairs={{0,1},{1,2},{2,3},{3,4},{4,5},{5,6},{6,7},{7,8},{8,9},{9,10},{10,1... | collective-permute-start | bytes 98312 | tf_op jit(solution)/shard_map/ppermute | solution.py:578
  256.1 12.1 %collective-permute-start.53 = (f32[32,512]{1,0:T(8,128)S(1)}, f32[32,512]{1,0:T(8,128)S(1)}, u32[]{:S(2)}, u32[]{:S(2)}) collective-permute-start(f32[32,512]{1,0:T(8,128)S(1)} %slice.136), channel_id=1, source_target_pairs={{1,0},{3,2},{5,4},{7,6},{9,8},{11,10},{13,12},{15,14},{17,16},{19,... | collective-permute-start | bytes 196616 | tf_op jit(solution)/shard_map/ppermute | solution.py:600
  258.4 60.1 %collective-permute-start.52 = (f32[16,512]{1,0:T(8,128)S(1)}, f32[16,512]{1,0:T(8,128)S(1)}, u32[]{:S(2)}, u32[]{:S(2)}) collective-permute-start(f32[16,512]{1,0:T(8,128)S(1)} %slice.135), channel_id=1, source_target_pairs={{0,1},{1,2},{2,3},{3,4},{4,5},{5,6},{6,7},{7,8},{8,9},{9,10},{10,1... | collective-permute-start | bytes 98312 | tf_op jit(solution)/shard_map/ppermute | solution.py:578
  262.9 38.5 %collective-permute-start.59 = (bf16[2,4,36,16,128]{4,3,2,1,0:T(8,128)(2,1)S(1)}, bf16[2,4,36,16,128]{4,3,2,1,0:T(8,128)(2,1)S(1)}, u32[]{:S(2)}, u32[]{:S(2)}) collective-permute-start(bf16[2,4,36,16,128]{4,3,2,1,0:T(8,128)(2,1)S(1)} %fusion.1), channel_id=1, source_target_pairs={{0,4},{1,3},{2,6},{3,1},{4,0},{5,7},{6,2},{7,5},{8,12},{9,11},{10,... | collective-permute-start | bytes 3538952 | tf_op jit(solution)/shard_map/ppermute | solution.py:657
  264.2 23.7 %collective-permute-start.60 = (bf16[2,2,12,16,128]{4,3,2,1,0:T(8,128)(2,1)S(1)}, bf16[2,2,12,16,128]{4,3,2,1,0:T(8,128)(2,1)S(1)}, u32[]{:S(2)}, u32[]{:S(2)}) collective-permute-start(bf16[2,2,12,16,128]{4,3,2,1,0:T(8,128)(2,1)S(1)} %get-tuple-element.127), channel_id=1, source_target_pairs={{0,8},{1,9},{2,10},{3,11},{4,12},{5,13},{6,14},{7,15},{8,16},{9,17... | collective-permute-start | bytes 589832 | tf_op jit(solution)/shard_map/ppermute | solution.py:657
  268.2 31.5 %collective-permute-start.61 = (bf16[2,2,12,16,128]{4,3,2,1,0:T(8,128)(2,1)S(1)}, bf16[2,2,12,16,128]{4,3,2,1,0:T(8,128)(2,1)S(1)}, u32[]{:S(2)}, u32[]{:S(2)}) collective-permute-start(bf16[2,2,12,16,128]{4,3,2,1,0:T(8,128)(2,1)S(1)} %get-tuple-element.129), channel_id=1, source_target_pairs={{0,16},{1,17},{2,18},{3,19},{4,20},{5,21},{6,22},{7,23},{8,24},{9,... | collective-permute-start | bytes 589832 | tf_op jit(solution)/shard_map/ppermute | solution.py:657
  268.2 31.5 %collective-permute-start.62 = (bf16[2,2,12,16,128]{4,3,2,1,0:T(8,128)(2,1)S(1)}, bf16[2,2,12,16,128]{4,3,2,1,0:T(8,128)(2,1)S(1)}, u32[]{:S(2)}, u32[]{:S(2)}) collective-permute-start(bf16[2,2,12,16,128]{4,3,2,1,0:T(8,128)(2,1)S(1)} %get-tuple-element.128), channel_id=1, source_target_pairs={{0,24},{1,25},{2,26},{3,27},{4,28},{5,29},{6,30},{7,31},{8,0},{9,1... | collective-permute-start | bytes 589832 | tf_op jit(solution)/shard_map/ppermute | solution.py:657
  302.4 15.9 %collective-permute-start.67 = (bf16[4,36,16,128]{3,2,1,0:T(8,128)(2,1)S(1)}, bf16[4,36,16,128]{3,2,1,0:T(8,128)(2,1)S(1)}, u32[]{:S(2)}, u32[]{:S(2)}) collective-permute-start(bf16[4,36,16,128]{3,2,1,0:T(8,128)(2,1)S(1)} %fusion.8), channel_id=1, source_target_pairs={{0,2},{1,5},{2,0},{3,7},{4,6},{5,1},{6,4},{7,3},{8,10},{9,13},{10,... | collective-permute-start | bytes 1769480 | tf_op jit(solution)/shard_map/ppermute | solution.py:657
  307.7 10.0 %collective-permute-start.65 = (f32[32,512]{1,0:T(8,128)S(1)}, f32[32,512]{1,0:T(8,128)S(1)}, u32[]{:S(2)}, u32[]{:S(2)}) collective-permute-start(f32[32,512]{1,0:T(8,128)S(1)} %add_add_fusion.1), channel_id=1, source_target_pairs={{24,0}} | collective-permute-start | bytes 196616 | tf_op jit(solution)/shard_map/ppermute | solution.py:600
  308.4 16.1 %collective-permute-start.51 = (f32[64,512]{1,0:T(8,128)S(1)}, f32[64,512]{1,0:T(8,128)S(1)}, u32[]{:S(2)}, u32[]{:S(2)}) collective-permute-start(f32[64,512]{1,0:T(8,128)S(1)} %pad_maximum_fusion.4), channel_id=1, source_target_pairs={{1,0},{2,1},{3,2},{4,3},{5,4},{6,5},{7,6},{8,7},{9,8},{10,9},{11,1... | collective-permute-start | bytes 393224 | tf_op jit(solution)/shard_map/ppermute | solution.py:578
  333.0 12.1 %collective-permute-start.77 = (bf16[12,16,128]{2,1,0:T(8,128)(2,1)S(1)}, bf16[12,16,128]{2,1,0:T(8,128)(2,1)S(1)}, u32[]{:S(2)}, u32[]{:S(2)}) collective-permute-start(bf16[12,16,128]{2,1,0:T(8,128)(2,1)S(1)} %fusion.20), channel_id=1, source_target_pairs={{0,2},{1,5},{2,0},{3,7},{4,6},{5,1},{6,4},{7,3},{8,10},{9,13},{10,... | collective-permute-start | bytes 147464 | tf_op jit(solution)/shard_map/ppermute | solution.py:657
  337.9 17.2 %collective-permute-start.74 = (bf16[36,16,128]{2,1,0:T(8,128)(2,1)S(1)}, bf16[36,16,128]{2,1,0:T(8,128)(2,1)S(1)}, u32[]{:S(2)}, u32[]{:S(2)}) collective-permute-start(bf16[36,16,128]{2,1,0:T(8,128)(2,1)S(1)} %get-tuple-element.130), channel_id=1, source_target_pairs={{0,8},{1,9},{2,10},{3,11},{4,12},{5,13},{6,14},{7,15},{8,16},{9,17... | collective-permute-start | bytes 442376 | tf_op jit(solution)/shard_map/ppermute | solution.py:657
  338.0 17.1 %collective-permute-start.75 = (bf16[36,16,128]{2,1,0:T(8,128)(2,1)S(1)}, bf16[36,16,128]{2,1,0:T(8,128)(2,1)S(1)}, u32[]{:S(2)}, u32[]{:S(2)}) collective-permute-start(bf16[36,16,128]{2,1,0:T(8,128)(2,1)S(1)} %get-tuple-element.132), channel_id=1, source_target_pairs={{0,16},{1,17},{2,18},{3,19},{4,20},{5,21},{6,22},{7,23},{8,24},{9,... | collective-permute-start | bytes 442376 | tf_op jit(solution)/shard_map/ppermute | solution.py:657
  343.8 14.9 %collective-permute-start.76 = (bf16[36,16,128]{2,1,0:T(8,128)(2,1)S(1)}, bf16[36,16,128]{2,1,0:T(8,128)(2,1)S(1)}, u32[]{:S(2)}, u32[]{:S(2)}) collective-permute-start(bf16[36,16,128]{2,1,0:T(8,128)(2,1)S(1)} %get-tuple-element.131), channel_id=1, source_target_pairs={{0,24},{1,25},{2,26},{3,27},{4,28},{5,29},{6,30},{7,31},{8,0},{9,1... | collective-permute-start | bytes 442376 | tf_op jit(solution)/shard_map/ppermute | solution.py:657
  343.9 10.7 %collective-permute-start.72 = (f32[2,1024]{1,0:T(2,128)S(1)}, f32[2,1024]{1,0:T(2,128)S(1)}, u32[]{:S(2)}, u32[]{:S(2)}) collective-permute-start(f32[2,1024]{1,0:T(2,128)S(1)} %add.254), channel_id=1, source_target_pairs={{0,8},{1,9},{2,10},{3,11},{4,12},{5,13},{6,14},{7,15},{8,0},{9,1},... | collective-permute-start | bytes 24584 | tf_op jit(solution)/shard_map/ppermute | solution.py:616
  354.5 12.7 %collective-permute-start.73 = (f32[2,1024]{1,0:T(2,128)S(1)}, f32[2,1024]{1,0:T(2,128)}, u32[]{:S(2)}, u32[]{:S(2)}) collective-permute-start(f32[2,1024]{1,0:T(2,128)S(1)} %add.255), channel_id=1, source_target_pairs={{0,16},{1,17},{2,18},{3,19},{4,20},{5,21},{6,22},{7,23},{8,24},{9,... | collective-permute-start | bytes 24584 | tf_op jit(solution)/shard_map/ppermute | solution.py:616
  (80 other events, 779.2 us)
Sparse Core Ops, SparseCore 0:
  46.4 79.8 all-gather.1
  220.5 128.9 reduce-scatter.1

commit v3 on v2

v3 whole, which is shorter than its diff:
```python
import functools

import jax
import jax.numpy as jnp
from jax import lax
from jax.experimental import pallas as pl
from jax.experimental.pallas import tpu as pltpu
from jax.sharding import PartitionSpec as P

D = 512
HEADS = 8
FF = 2048
SEG = 16
LEFT = 30
RIGHT = 4
MEM = 4
STEP = 10
UN = 4
NEG = -1e30

TOK = 512
NSEG = TOK // SEG
LH = 32
RH = 16
EXT = LH + TOK + 2 * RH
ROWS = EXT + NSEG * MEM
BLK = 4
NBLK = NSEG // BLK
QB = BLK * SEG
KB = 128
WB = KB - BLK * MEM

TILES = 1536
QKV0, WO0, WU0, WD0 = 0, 384, 512, 1024
MATS = TILES * 16 * 128
GROUPS = 32
BT = TILES // GROUPS

F32 = jnp.float32
BF16 = jnp.bfloat16
VM = pl.BlockSpec(memory_space=pltpu.VMEM)
SM = pl.BlockSpec(memory_space=pltpu.SMEM)
ANYS = pl.BlockSpec(memory_space=pl.ANY)


def mm(a, b):
    return lax.dot_general(a, b, (((1,), (0,)), ((), ())), preferred_element_type=F32)


def mm_nt(a, b):
    return lax.dot_general(a, b, (((1,), (1,)), ((), ())), preferred_element_type=F32)


def mm_tn(a, b):
    return lax.dot_general(a, b, (((0,), (0,)), ((), ())), preferred_element_type=F32)


def wblk(w, base, nj, i0, ni, j0, nj_take):
    cols = [
        jnp.concatenate([w[base + (i0 + i) * nj + j0 + j] for i in range(ni)], axis=0)
        for j in range(nj_take)
    ]
    return cols[0] if nj_take == 1 else jnp.concatenate(cols, axis=1)


def place(me, rc, ra, rb, k):
    core = (me % 2) ^ rc
    x = ((me // 2) % 2) ^ jnp.where(core == 0, ra, rb)
    y = ((me // 4) % 2) ^ jnp.where(core == 0, rb, ra)
    z = (me // 8 + k) % 4
    return ((z * 2 + y) * 2 + x) * 2 + core


def load_weights(me, pieces, w_ref, sems, lo, hi, gt_ref=None):
    if len(pieces) < 8:
        if gt_ref is not None:
            pltpu.make_async_copy(pieces[1], gt_ref, sems.at[GROUPS]).start()
        for d in range(lo, hi):
            t = pl.ds(BT * d, BT)
            pltpu.make_async_copy(pieces[0].at[t], w_ref.at[t], sems.at[d]).start()
        return
    for rc in range(2):
        for m in range(4):
            for k in range(4):
                d = place(me, rc, m % 2, m // 2, -k % 4)
                piece = pieces[4 * rc + m].at[k]

                @pl.when((d >= lo) & (d < hi))
                def _():
                    pltpu.make_async_copy(
                        piece.at[pl.ds(0, BT)], w_ref.at[pl.ds(d * BT, BT)], sems.at[d]
                    ).start()

                if gt_ref is not None:

                    @pl.when(d == GROUPS - 1)
                    def _():
                        pltpu.make_async_copy(piece.at[BT], gt_ref, sems.at[GROUPS]).start()


def await_weights(w_ref, sems, lo, hi):
    for d in range(lo, hi):
        part = w_ref.at[pl.ds(d * BT, BT)]
        pltpu.make_async_copy(part, part, sems.at[d]).wait()


def gain_row(g_ref, layer, which):
    g = g_ref[...].astype(F32)
    r = 8 * layer + 4 * which
    return jnp.concatenate([g[r + k : r + k + 1] for k in range(4)], axis=1)


def norm_parts(v):
    mean = jnp.mean(v, axis=-1, keepdims=True)
    cen = v - mean
    rstd = lax.rsqrt(jnp.mean(cen * cen, axis=-1, keepdims=True) + 1e-05)
    return cen * rstd, rstd


def norm_back(dh, xhat, rstd, gain):
    dx = dh * gain
    return rstd * (
        dx
        - jnp.mean(dx, axis=-1, keepdims=True)
        - xhat * jnp.mean(dx * xhat, axis=-1, keepdims=True)
    )


def seg_mean(h):
    return (jnp.sum(h.astype(F32).reshape(NSEG, SEG, D), axis=1) * (1.0 / SEG)).astype(BF16)


def head_of_layer(x, gain):
    xhat, _ = norm_parts(x)
    h1 = (xhat * gain).astype(BF16)
    return h1, seg_mean(h1)


def send_on(me, rows_ref, means, ahead_ref, back_ref, root_ref, sum_ref):
    sum_ref[...] = means
    ahead_ref[0:LH] = rows_ref[TOK - LH : TOK]
    ahead_ref[LH:] = means
    back_ref[...] = rows_ref[0:RH]
    root_ref[...] = jnp.where(me == 0, means, jnp.zeros_like(means))


def first_kernel(me_ref, x_ref, ahead_ref, back_ref, root_ref, sum_ref):
    xhat, _ = norm_parts(x_ref[...].astype(F32))
    send_on(me_ref[0], x_ref, seg_mean(xhat), ahead_ref, back_ref, root_ref, sum_ref)


def lane_lo(rows):
    return lax.broadcasted_iota(jnp.int32, (rows, 128), 1) < 64


def split_heads(m, lo):
    z = jnp.zeros_like(m)
    return jnp.concatenate([jnp.where(lo, m, z), jnp.where(lo, z, m)], axis=0)


def onehot_of(loc_ref):
    ids = lax.broadcasted_iota(jnp.int32, (NSEG * MEM, 128), 1)
    return jnp.where(loc_ref[...] == ids, 1.0, 0.0).astype(BF16)


def block_keys(kv_ref, b, col):
    r0 = pl.multiple_of(b * QB, QB)
    m0 = pl.multiple_of(EXT + b * (BLK * MEM), BLK * MEM)
    return jnp.concatenate(
        [kv_ref[pl.ds(r0, WB), col : col + 128], kv_ref[pl.ds(m0, BLK * MEM), col : col + 128]], axis=0
    )


def attend(me, n, q_ref, kv_ref, vis_ref, p_ref, o_ref, s_ref):
    ki = lax.broadcasted_iota(jnp.int32, (KB, 128), 0)
    qi = (lax.broadcasted_iota(jnp.int32, (KB, 128), 1) % QB) // SEG
    off = ki - SEG * qi - (LH - LEFT)
    near = jnp.where((off >= 0) & (off < LEFT + SEG + RIGHT) & (ki < WB), 1.0, 0.0)
    memb = jnp.where((ki >= WB) & ((ki - WB) // MEM == qi), 1.0, 0.0)
    first = jnp.where(me == 0, LH, 0)
    end = jnp.where(me == n - 1, LH + TOK, EXT)
    lo = lane_lo(QB)

    def scores(b, carry):
        r0 = pl.multiple_of(b * QB, QB)
        m0 = pl.multiple_of(b * (BLK * MEM), BLK * MEM)
        inside = (ki + r0 >= first) & (ki + r0 < end)
        memv = jnp.concatenate(
            [jnp.zeros((WB, 128), F32), vis_ref[pl.ds(m0, BLK * MEM), :]], axis=0
        )
        seen = jnp.where(inside, near, 0.0) + memb * memv > 0.5
        for p in range(4):
            kc = block_keys(kv_ref, b, 128 * p)
            s = mm_nt(kc, split_heads(q_ref[pl.ds(r0, QB), 128 * p : 128 * p + 128], lo))
            s_ref[b * 4 + p] = jnp.where(seen, s, NEG)
        return carry

    def softmax(i, carry):
        s = s_ref[i]
        e = jnp.exp(s - jnp.max(s, axis=0, keepdims=True))
        p_ref[i] = (e * (1.0 / jnp.sum(e, axis=0, keepdims=True))).astype(BF16)
        return carry

    def mix(b, carry):
        r0 = pl.multiple_of(b * QB, QB)
        for p in range(4):
            o2 = mm_tn(p_ref[b * 4 + p], block_keys(kv_ref, b, D + 128 * p))
            o_ref[pl.ds(r0, QB), 128 * p : 128 * p + 128] = jnp.where(lo, o2[:QB], o2[QB:]).astype(BF16)
        return carry

    lax.fori_loop(0, NBLK, scores, 0, unroll=UN)
    lax.fori_loop(0, 4 * NBLK, softmax, 0, unroll=4)
    lax.fori_loop(0, NBLK, mix, 0, unroll=UN)


def attend_back(q_ref, kv_ref, p_ref, do_ref, dq_ref, dkv_ref, s_ref):
    dkv_ref[...] = jnp.zeros_like(dkv_ref)
    lo = lane_lo(QB)

    def weights(b, carry):
        r0 = pl.multiple_of(b * QB, QB)
        m0 = pl.multiple_of(EXT + b * (BLK * MEM), BLK * MEM)
        for p in range(4):
            vc0 = D + 128 * p
            dd = split_heads(do_ref[pl.ds(r0, QB), 128 * p : 128 * p + 128], lo)
            s_ref[b * 4 + p] = mm_nt(block_keys(kv_ref, b, vc0), dd)
            dv = mm(p_ref[b * 4 + p], dd)
            dkv_ref[pl.ds(r0, WB), vc0 : vc0 + 128] += dv[:WB]
            dkv_ref[pl.ds(m0, BLK * MEM), vc0 : vc0 + 128] = dv[WB:]
        return carry

    def softmax(i, carry):
        pf = p_ref[i].astype(F32)
        pd = pf * s_ref[i]
        p_ref[i] = (pd - pf * jnp.sum(pd, axis=0, keepdims=True)).astype(BF16)
        return carry

    def queries(b, carry):
        r0 = pl.multiple_of(b * QB, QB)
        m0 = pl.multiple_of(EXT + b * (BLK * MEM), BLK * MEM)
        for p in range(4):
            kc0 = 128 * p
            ds = p_ref[b * 4 + p]
            dk = mm(ds, split_heads(q_ref[pl.ds(r0, QB), kc0 : kc0 + 128], lo))
            dq2 = mm_tn(ds, block_keys(kv_ref, b, kc0))
            dq_ref[pl.ds(r0, QB), kc0 : kc0 + 128] = (jnp.where(lo, dq2[:QB], dq2[QB:]) * 0.125).astype(BF16)
            dkv_ref[pl.ds(r0, WB), kc0 : kc0 + 128] += dk[:WB]
            dkv_ref[pl.ds(m0, BLK * MEM), kc0 : kc0 + 128] = dk[WB:]
        return carry

    lax.fori_loop(0, NBLK, weights, 0, unroll=UN)
    lax.fori_loop(0, 4 * NBLK, softmax, 0, unroll=4)
    lax.fori_loop(0, NBLK, queries, 0, unroll=UN)


class Copies:
    def __init__(self, sems):
        self.sems, self.used, self.open = sems, 0, []

    def start(self, src, dst):
        copy = pltpu.make_async_copy(src, dst, self.sems.at[self.used])
        self.used += 1
        copy.start()
        return copy

    def out(self, src, dst):
        self.open.append(self.start(src, dst))

    def finish(self):
        for copy in self.open:
            copy.wait()


def project(hx_ref, w_ref, q_ref, kv_ref):
    q = mm(hx_ref[LH : LH + TOK], wblk(w_ref, QKV0, 12, 0, 32, 0, 4)).astype(BF16)
    q_ref[...] = q * jnp.asarray(0.125, BF16)
    for j in range(2):
        kv_ref[:, 512 * j : 512 * j + 512] = mm(hx_ref[...], wblk(w_ref, QKV0, 12, 0, 32, 4 + 4 * j, 4)).astype(BF16)


def feed_forward(h2_ref, w_ref, act_ref, gp_ref, out_ref, step):
    for c in range(4):
        u = mm(h2_ref[...], wblk(w_ref, WU0, 16, 0, 32, 4 * c, 4))
        cc, c3 = 0.7978845608028654, 0.7978845608028654 * 0.044715
        u2 = u * u
        t = jnp.tanh(u * (cc + c3 * u2))
        hu = 0.5 * u
        act = (hu + hu * t).astype(BF16)
        gp = 0.5 + 0.5 * t + hu * (1.0 - t * t) * (cc + 3 * c3 * u2)
        act_ref[:, 512 * c : 512 * c + 512] = act
        gp_ref[:, 512 * c : 512 * c + 512] = gp.astype(BF16)
        out_ref[...] += mm(act, wblk(w_ref, WD0, 4, 32 * c, 32, 0, 4))
        step(c)


def back_ffn(dx_ref, w_ref, gains, a_ref, gp_ref, da_ref, dxb_ref, dub_ref, dab_ref, dgb_ref, step):
    dxb_ref[...] = dx_ref[...].astype(BF16)
    step("dxb")
    for c in range(4):
        dact = mm_nt(dxb_ref[...], wblk(w_ref, WD0, 4, 32 * c, 32, 0, 4))
        du = (dact * gp_ref[:, 512 * c : 512 * c + 512].astype(F32)).astype(BF16)
        dub_ref[:, 512 * c : 512 * c + 512] = du
        dh2 = mm_nt(du, wblk(w_ref, WU0, 16, 0, 32, 4 * c, 4))
        if c:
            da_ref[...] += dh2
        else:
            da_ref[...] = dh2
    step("dub")
    xhat, rstd = norm_parts(a_ref[...])
    dh2 = da_ref[...]
    dgb_ref[...] = jnp.sum(dh2 * xhat, axis=0, keepdims=True)
    da = dx_ref[...] + norm_back(dh2, xhat, rstd, gains)
    da_ref[...] = da
    dab_ref[...] = da.astype(BF16)
    step("dab")


def back_attn(dab_ref, w_ref, q_ref, kv_ref, p_ref, dq_ref, dkvb_ref, dh_ref, dkv_ref, dob_ref, s_ref, step):
    dob_ref[...] = mm_nt(dab_ref[...], wblk(w_ref, WO0, 4, 0, 32, 0, 4)).astype(BF16)
    step("attend")
    attend_back(q_ref, kv_ref, p_ref, dob_ref, dq_ref, dkv_ref, s_ref)
    dkvb_ref[...] = dkv_ref[...].astype(BF16)
    step("dkvb")
    dh_ref[...] = mm_nt(dkvb_ref[...], wblk(w_ref, QKV0, 12, 0, 32, 4, 8))
    dh_ref[LH : LH + TOK] += mm_nt(dq_ref[...], wblk(w_ref, QKV0, 12, 0, 32, 0, 4))


def table_grad(loc_ref, dh_ref, hal_ref, har_ref, root_ref, b2_ref, mine_ref):
    dch = dh_ref[EXT:ROWS]
    hi = dch.astype(BF16)
    oh = onehot_of(loc_ref)
    dtab = mm_tn(oh, hi) + mm_tn(oh, (dch - hi.astype(F32)).astype(BF16))
    hal_ref[0:LH] = dh_ref[0:LH]
    hal_ref[LH:] = dtab[64:96]
    har_ref[...] = dh_ref[LH + TOK : LH + TOK + RH]
    root_ref[...] = dtab[0:32]
    b2_ref[...] = dtab[32:64]
    mine_ref[...] = dtab[96:128]
    return dtab


def low_attn_kernel(me_ref, x_ref, hl_ref, hr_ref, root_ref, b2_ref, summ_ref, loc_ref, vis_ref, *rest, np_, n):
    pieces, rest = rest[:np_], rest[np_:]
    gt_ref, hx_o, q_o, kv_o, p_o, o_o, w_ref, sems, hx_ref, q_ref, kv_ref, p_ref, o_ref, s_ref, osem = rest
    me = me_ref[0]
    load_weights(me, pieces, w_ref, sems, 0, 8, gt_ref)
    copies = Copies(osem)
    pltpu.make_async_copy(gt_ref, gt_ref, sems.at[GROUPS]).wait()
    ga = gain_row(gt_ref, 0, 0)
    for ref, rows, at in ((hl_ref, LH, 0), (x_ref, TOK, LH), (hr_ref, RH, LH + TOK)):
        xhat, _ = norm_parts(ref[0:rows].astype(F32))
        hx_ref[at : at + rows] = (xhat * ga).astype(BF16)
    means = jnp.concatenate([root_ref[...], b2_ref[...], hl_ref[LH:], summ_ref[...]], axis=0)
    hx_ref[LH + TOK + RH : EXT] = jnp.zeros((RH, D), BF16)
    hx_ref[EXT:ROWS] = mm(onehot_of(loc_ref), (means.astype(F32) * ga).astype(BF16)).astype(BF16)
    copies.out(hx_ref, hx_o)
    await_weights(w_ref, sems, 0, 8)
    project(hx_ref, w_ref, q_ref, kv_ref)
    copies.out(q_ref, q_o)
    copies.out(kv_ref, kv_o)
    attend(me, n, q_ref, kv_ref, vis_ref, p_ref, o_ref, s_ref)
    copies.out(p_ref, p_o)
    copies.out(o_ref, o_o)
    copies.finish()


def low_ffn_kernel(me_ref, x_ref, o_ref, gt_ref, *rest, np_):
    pieces, rest = rest[:np_], rest[np_:]
    (out_ref, h1n_ref, ahead_ref, back_ref, root_ref, sumn_ref, a_o, h2_o, gp_o, act_o,
     w_ref, sems, a_ref, h2_ref, gp_ref, act_ref, osem) = rest
    load_weights(me_ref[0], pieces, w_ref, sems, 8, 32)
    copies = Copies(osem)
    await_weights(w_ref, sems, 8, 11)
    a = x_ref[...].astype(F32) + mm(o_ref[...], wblk(w_ref, WO0, 4, 0, 32, 0, 4))
    a_ref[...] = a
    copies.out(a_ref, a_o)
    xhat, _ = norm_parts(a)
    h2_ref[...] = (xhat * gain_row(gt_ref, 0, 1)).astype(BF16)
    copies.out(h2_ref, h2_o)
    out_ref[...] = a
    await_weights(w_ref, sems, 11, 32)
    feed_forward(h2_ref, w_ref, act_ref, gp_ref, out_ref, lambda c: None)
    copies.out(act_ref, act_o)
    copies.out(gp_ref, gp_o)
    h1n, sumn = head_of_layer(out_ref[...], gain_row(gt_ref, 1, 0))
    h1n_ref[...] = h1n
    send_on(me_ref[0], h1n_ref, sumn, ahead_ref, back_ref, root_ref, sumn_ref)
    copies.finish()


def top_kernel(me_ref, x_ref, h1_ref, hl_ref, hr_ref, root_ref, b2_ref, summ_ref, loc_ref, vis_ref, gt_ref, cot_any,
               *rest, np_, n):
    pieces, rest = rest[:np_], rest[np_:]
    (out_o, da_ref, dhown_ref, hal_ref, har_ref, rootg_ref, b2g_ref, mine_ref, dgb_ref, hx_o, o_o, h2_o, act_o, dxb_o, dub_o, dab_o, dq_o, dkvb_o,
     w_ref, sems, hx_ref, q_ref, kv_ref, p_ref, o_ref, a_ref, h2_ref, gp_ref, act_ref,
     out_ref, dx_ref, dxb_ref, dub_ref, dab_ref, dq_ref, dkvb_ref, dkv_ref, dob_ref, dh_ref, s_ref, osem) = rest
    me = me_ref[0]
    load_weights(me, pieces, w_ref, sems, 0, 32)
    copies = Copies(osem)
    cot = copies.start(cot_any, dx_ref)
    hx_ref[0:LH] = hl_ref[0:LH]
    hx_ref[LH : LH + TOK] = h1_ref[...]
    hx_ref[LH + TOK : LH + TOK + RH] = hr_ref[...]
    hx_ref[LH + TOK + RH : EXT] = jnp.zeros((RH, D), BF16)
    table = jnp.concatenate([root_ref[...], b2_ref[...], hl_ref[LH:], summ_ref[...]], axis=0)
    hx_ref[EXT:ROWS] = mm(onehot_of(loc_ref), table).astype(BF16)
    copies.out(hx_ref, hx_o)
    await_weights(w_ref, sems, 0, 8)
    project(hx_ref, w_ref, q_ref, kv_ref)
    attend(me, n, q_ref, kv_ref, vis_ref, p_ref, o_ref, s_ref)
    copies.out(o_ref, o_o)
    await_weights(w_ref, sems, 8, 32)
    a = x_ref[...] + mm(o_ref[...], wblk(w_ref, WO0, 4, 0, 32, 0, 4))
    a_ref[...] = a
    xhat, _ = norm_parts(a)
    h2_ref[...] = (xhat * gain_row(gt_ref, 1, 1)).astype(BF16)
    copies.out(h2_ref, h2_o)
    out_ref[...] = a
    feed_forward(h2_ref, w_ref, act_ref, gp_ref, out_ref, lambda c: None)
    copies.out(act_ref, act_o)
    copies.out(out_ref, out_o)
    cot.wait()
    done = {"dxb": ((dxb_ref, dxb_o),), "dub": ((dub_ref, dub_o),), "dab": ((dab_ref, dab_o),),
            "dkvb": ((dkvb_ref, dkvb_o), (dq_ref, dq_o))}

    def step(name):
        for pair in done.get(name, ()):
            copies.out(*pair)

    back_ffn(dx_ref, w_ref, gain_row(gt_ref, 1, 1), a_ref, gp_ref, da_ref, dxb_ref, dub_ref, dab_ref, dgb_ref, step)
    back_attn(dab_ref, w_ref, q_ref, kv_ref, p_ref, dq_ref, dkvb_ref, dh_ref, dkv_ref, dob_ref, s_ref, step)
    dhown_ref[...] = dh_ref[LH : LH + TOK]
    table_grad(loc_ref, dh_ref, hal_ref, har_ref, rootg_ref, b2g_ref, mine_ref)
    copies.finish()


def norm_one_back(dh_ref, hal_ref, har_ref, dsum, x, gain, da_ref, acc_ref):
    acc_ref[...] = dh_ref[...]
    acc_ref[TOK - LH : TOK] += hal_ref[0:LH]
    acc_ref[0:RH] += har_ref[...]
    for s in range(NSEG):
        acc_ref[SEG * s : SEG * s + SEG] += dsum[s : s + 1, :] * (1.0 / SEG)
    xhat, rstd = norm_parts(x)
    dh = acc_ref[...]
    return da_ref[...] + norm_back(dh, xhat, rstd, gain), jnp.sum(dh * xhat, axis=0, keepdims=True)


def summed(me_ref, hal_ref, root_ref, b2_ref, mine_ref):
    return mine_ref[...] + hal_ref[LH:] + b2_ref[...] + jnp.where(me_ref[0] == 0, root_ref[...], 0.0)


def bottom_ffn_kernel(me_ref, hal_ref, har_ref, root_ref, b2_ref, dtabp_ref, dhp_ref, x_ref, dap_ref, gt_ref, *rest, np_):
    pieces, rest = rest[:np_], rest[np_:]
    (a_any, gp_any, dga_ref, da_ref, dgb_ref, dxb_o, dub_o, dab_o,
     w_ref, sems, a_ref, gp_ref, dx_ref, dxb_ref, dub_ref, dab_ref, osem) = rest
    load_weights(me_ref[0], pieces, w_ref, sems, 10, 32)
    copies = Copies(osem)
    loads = [copies.start(*pair) for pair in ((gp_any, gp_ref), (a_any, a_ref))]
    dx, dga = norm_one_back(
        dhp_ref, hal_ref, har_ref, summed(me_ref, hal_ref, root_ref, b2_ref, dtabp_ref), x_ref[...],
        gain_row(gt_ref, 1, 0), dap_ref, dx_ref,
    )
    dx_ref[...] = dx
    dga_ref[...] = dga
    await_weights(w_ref, sems, 10, 32)
    loads[0].wait()
    done = {"dxb": (dxb_ref, dxb_o), "dub": (dub_ref, dub_o), "dab": (dab_ref, dab_o)}

    def step(name):
        if name == "dub":
            loads[1].wait()
        copies.out(*done[name])

    back_ffn(dx_ref, w_ref, gain_row(gt_ref, 0, 1), a_ref, gp_ref, da_ref, dxb_ref, dub_ref, dab_ref, dgb_ref, step)
    copies.finish()


def bottom_attn_kernel(me_ref, dab_ref, loc_ref, frames_ref, ahead0_ref, hr0_ref, root0_ref, b20_ref, summ0_ref, *rest, np_):
    pieces, rest = rest[:np_], rest[np_:]
    (q_any, kv_any, p_any, dga_ref, dhown_ref, hal_ref, har_ref, rootg_ref, b2g_ref, mine_ref, dq_o, dkvb_o,
     w_ref, sems, q_ref, kv_ref, p_ref, dq_ref, dkvb_ref, dkv_ref, dob_ref, dh_ref, s_ref, osem) = rest
    load_weights(me_ref[0], pieces, w_ref, sems, 0, 11)
    copies = Copies(osem)
    loads = [copies.start(*pair) for pair in ((q_any, q_ref), (kv_any, kv_ref), (p_any, p_ref))]
    await_weights(w_ref, sems, 0, 11)

    def step(name):
        if name == "attend":
            for load in loads:
                load.wait()
        else:
            copies.out(dkvb_ref, dkvb_o)
            copies.out(dq_ref, dq_o)

    back_attn(dab_ref, w_ref, q_ref, kv_ref, p_ref, dq_ref, dkvb_ref, dh_ref, dkv_ref, dob_ref, s_ref, step)
    dhown_ref[...] = dh_ref[LH : LH + TOK]
    dtab = table_grad(loc_ref, dh_ref, hal_ref, har_ref, rootg_ref, b2g_ref, mine_ref)
    means = jnp.concatenate([root0_ref[...], b20_ref[...], ahead0_ref[LH:], summ0_ref[...]], axis=0)
    total = jnp.sum(dtab * means.astype(F32), axis=0, keepdims=True)
    for ref, rows, at in ((ahead0_ref, LH, 0), (frames_ref, TOK, LH), (hr0_ref, RH, LH + TOK)):
        xhat, _ = norm_parts(ref[0:rows].astype(F32))
        total += jnp.sum(dh_ref[at : at + rows] * xhat, axis=0, keepdims=True)
    dga_ref[...] = total
    copies.finish()


def last_kernel(me_ref, hal_ref, har_ref, root_ref, b2_ref, dtab_ref, dh_ref, x_ref, da_ref, gt_ref, dx_ref, acc_ref):
    dx, _ = norm_one_back(
        dh_ref, hal_ref, har_ref, summed(me_ref, hal_ref, root_ref, b2_ref, dtab_ref), x_ref[...].astype(F32),
        gain_row(gt_ref, 0, 0), da_ref, acc_ref,
    )
    dx_ref[...] = dx


def dw_kernel(me_ref, *rest, part, nouts, gains=False):
    srcs, rest = rest[:9], rest[9:]
    if gains:
        gain_ref, rest = rest[0], rest[1:]
    outs, rest = rest[-12 - nouts : -12], rest[-12:]
    hx_ref, dq_ref, dkv_ref, o_ref, dab_ref, h2_ref, dub_ref, act_ref, dxb_ref, g_ref, sem, isem = rest
    copies = Copies(isem)
    loads = {}
    for i in {0: (7, 8), 1: (5, 6), 2: (3, 4, 0, 1, 2)}[part]:
        loads[i] = copies.start(srcs[i], rest[i])

    def put(val, base, nj, i0, j0):
        v = val.astype(BF16)
        for i in range(val.shape[0] // 16):
            for j in range(val.shape[1] // 128):
                g_ref[base + (i0 + i) * nj + j0 + j] = v[16 * i : 16 * i + 16, 128 * j : 128 * j + 128]

    def send(lo, hi):
        if nouts == 1:
            tiles = pl.ds(lo * 16, (hi - lo) * 16)
            pltpu.make_async_copy(g_ref.at[tiles], outs[0].at[tiles], sem).start()
            return
        me = me_ref[0]
        units = {}
        for u in range(lo, hi):
            units.setdefault(u // 3, []).append(u % 3)
        for d, thirds in units.items():
            core = d % 2
            rx, ry = ((me // 2) % 2) ^ (d // 2 % 2), ((me // 4) % 2) ^ (d // 4 % 2)
            ra, rb = (rx, ry) if core == 0 else (ry, rx)
            k = (d // 8 - me // 8 + 4) % 4
            t0, t1 = 16 * thirds[0], 16 * thirds[-1] + 16
            for rc in range(2):

                @pl.when((me % 2) ^ core == rc)
                def _():
                    pltpu.make_async_copy(
                        g_ref.at[pl.ds(d * BT + t0, t1 - t0)], outs[rc].at[rb, ra, k, pl.ds(t0, t1 - t0)], sem
                    ).start()

    if part == 0:
        loads[7].wait()
        loads[8].wait()

        def down(c, carry):
            c0 = pl.multiple_of(c * 256, 256)
            put(mm_tn(act_ref[:, pl.ds(c0, 256)], dxb_ref[...]), WD0, 4, 16 * c, 0)
            return carry

        lax.fori_loop(0, FF // 256, down, 0)
        send(64, 96)
    if part == 1:
        loads[5].wait()
        loads[6].wait()

        def up(c, carry):
            c0 = pl.multiple_of(c * 256, 256)
            put(mm_tn(h2_ref[...], dub_ref[:, pl.ds(c0, 256)]), WU0, 16, 0, 2 * c)
            return carry

        lax.fori_loop(0, FF // 256, up, 0)
        send(32, 64)
    if part == 2:
        for i in (3, 4, 0, 1, 2):
            loads[i].wait()
        for j in range(2):
            put(mm_tn(o_ref[...], dab_ref[:, 256 * j : 256 * j + 256]), WO0, 4, 0, 2 * j)
        send(24, 32)
        for j in range(2):
            put(mm_tn(hx_ref[LH : LH + TOK], dq_ref[:, 256 * j : 256 * j + 256]), QKV0, 12, 0, 2 * j)
        for j in range(4):
            put(mm_tn(hx_ref[...], dkv_ref[:, 256 * j : 256 * j + 256]), QKV0, 12, 0, 4 + 2 * j)
        send(0, 24)
        if gains:
            for i in range(GROUPS):
                pltpu.make_async_copy(
                    gain_ref, outs[i // 16].at[i % 2, i // 2 % 2, i // 4 % 4, BT], sem
                ).start()
            for i in range(GROUPS):
                pltpu.make_async_copy(gain_ref, gain_ref, sem).wait()
    first, count = {0: (WD0, 512), 1: (WU0, 512), 2: (0, 512)}[part]
    all_of = g_ref.at[pl.ds(first, count)]
    pltpu.make_async_copy(all_of, all_of, sem).wait()


def sds(shape, dtype):
    return jax.ShapeDtypeStruct(shape, dtype)


PARAMS = dict(vmem_limit_bytes=56 * 1024 * 1024)


def run(kernel, outs, ins, specs=None, scratch=(), flops=0, nbytes=0, aliases=None, **kw):
    return pl.pallas_call(
        kernel,
        out_shape=outs,
        input_output_aliases=aliases or {},
        in_specs=specs or [VM] * len(ins),
        out_specs=jax.tree.map(lambda _: VM, outs) if "out_specs" not in kw else kw["out_specs"],
        scratch_shapes=list(scratch),
        compiler_params=pltpu.CompilerParams(**PARAMS),
        cost_estimate=pl.CostEstimate(flops=flops, bytes_accessed=nbytes, transcendentals=0),
    )(*ins)


def shift(value, by, n):
    return lax.ppermute(value, "ta", [(i, i + by) for i in range(n) if 0 <= i + by < n])


def strides(n):
    return [(1 << k, 2) for k in reversed(range(n.bit_length() - 1))]


def spread_round(value, digit, done, n):
    stride, radix = digit
    keep = [i for i in range(n) if all(i // s % r == 0 for s, r in strides(n) if (s, r) not in done)]
    parts = [lax.ppermute(value, "ta", [(i, i + j * stride) for i in keep]) for j in range(1, radix)]
    return functools.reduce(jnp.add, parts, value)


def collect_round(value, digit, done, n):
    stride, radix = digit
    keep = [i for i in range(n) if all(i // s % r == 0 for s, r in [digit] + done)]
    parts = [lax.ppermute(value, "ta", [(i + j * stride, i) for i in keep]) for j in range(1, radix)]
    return functools.reduce(jnp.add, parts, value)


def from_first(value, me, n, root=0):
    value = jnp.where(me == root, value, jnp.zeros_like(value))
    if root:
        value = shift(value, -root, n)
    digits = strides(n)
    for i in range(len(digits)):
        value = spread_round(value, digits[i], digits[:i], n)
    return value


def sum_all(value, n):
    step = 1
    while step < n:
        value = value + lax.ppermute(value, "ta", [(i, i ^ step) for i in range(n)])
        step *= 2
    return value


def tiles_of(rows, ni, nj):
    return rows.reshape(ni, 16, nj, 128).transpose(0, 2, 1, 3).reshape(ni * nj, 16, 128)


def rows_of(tiles, ni, nj):
    return tiles.reshape(ni, nj, 16, 128).transpose(0, 2, 1, 3).reshape(ni * nj * 16, 128)


PIECES = ((QKV0, 32, 12), (WO0, 32, 4), (WU0, 32, 16), (WD0, 128, 4))


def gather_plain(aligned):
    full = lax.all_gather(aligned.reshape(-1, 128), "ta", axis=0, tiled=True)
    return jnp.concatenate(
        [tiles_of(full[16 * b : 16 * (b + ni * nj)], ni, nj) for b, ni, nj in PIECES], axis=0
    )


def reduce_plain(tiles):
    full = jnp.concatenate([rows_of(tiles[b : b + ni * nj], ni, nj) for b, ni, nj in PIECES], axis=0)
    return lax.psum_scatter(full, "ta", scatter_dimension=0, tiled=True).astype(F32).reshape(-1)


def links(n, kind, by=1):
    pairs = []
    for i in range(n):
        if kind == "core":
            pairs.append((i, i ^ 1))
        elif kind == "z":
            pairs.append((i, (i + 8 * by) % n))
        else:
            pairs.append((i, i ^ (2 if (kind == "a") == (i % 2 == 0) else 4)))
    return pairs


def move(value, kind, by=1):
    return lax.ppermute(value, "ta", links(32, kind, by))


def after(value, *others):
    return lax.optimization_barrier((value,) + others)[0]


def to_tiles(rows, me):
    third = 3 * me + jnp.arange(3).reshape(3, 1, 1, 1)
    qkv = tiles_of(rows, 4, 12).reshape(3, 16, 16, 128)
    four = rows.reshape(3, 4, 16, 4, 128).transpose(0, 1, 3, 2, 4).reshape(3, 16, 16, 128)
    wide = rows.reshape(3, 16, 16, 128).transpose(0, 2, 1, 3)
    out = jnp.where(third < 24, qkv, jnp.where((third >= 32) & (third < 64), wide, four))
    return out.reshape(48, 16, 128)


def to_rows(tiles, me):
    third = 3 * me + jnp.arange(3).reshape(3, 1, 1)
    qkv = rows_of(tiles, 4, 12).reshape(3, 256, 128)
    four = tiles.reshape(3, 4, 4, 16, 128).transpose(0, 1, 3, 2, 4).reshape(3, 256, 128)
    wide = tiles.reshape(3, 16, 16, 128).transpose(0, 2, 1, 3).reshape(3, 256, 128)
    out = jnp.where(third < 24, qkv, jnp.where((third >= 32) & (third < 64), wide, four))
    return out.reshape(-1)


def head_rows(tiles, me):
    third = 3 * me
    four = ((third >= 24) & (third < 32)) | (third >= 64)
    return jnp.where(four, jnp.concatenate([tiles[:4, 0], tiles[:4, 1]], axis=0), tiles[:8, 0]).reshape(-1)


def per_device(frames, cotangent, mem_index, master, moment, second, average):
    n = lax.axis_size("ta")
    me = lax.axis_index("ta")
    mev = me.astype(jnp.int32).reshape(1)
    layers, share = master.shape
    step = 2 * D // n
    fast = n == GROUPS
    digits = strides(n)

    def vmem(*shape_types):
        return [pltpu.VMEM(shape, dtype) for shape, dtype in shape_types]

    def sems(count):
        return [pltpu.SemaphoreType.DMA((count,))]

    def call(kernel, ins, specs, outs, scratch, aliases=None, flops=3 * 10**9):
        return run(
            kernel, tuple(sds(*o) for o, _ in outs), tuple(ins), specs=specs,
            out_specs=tuple(VM if keep else ANYS for _, keep in outs), scratch=scratch,
            aliases=aliases, flops=flops, nbytes=10**7,
        )

    tf, tb = ((TOK, D), F32), ((TOK, D), BF16)
    wide, rows16, kv16 = ((TOK, FF), BF16), ((ROWS, D), BF16), ((ROWS, 2 * D), BF16)
    prob, rows32, kv32 = ((NBLK * 4, KB, 128), BF16), ((ROWS, D), F32), ((ROWS, 2 * D), F32)
    drow, dtab_t, sums = ((1, D), F32), ((128, D), F32), ((NSEG, D), BF16)
    tiles_t = ((TILES, 16, 128), BF16)
    score = ((NBLK * 4, KB, 128), F32)
    wscr = vmem(tiles_t) + sems(GROUPS + 1)

    msgs = [(((LH + NSEG, D), BF16), True), (((RH, D), BF16), True), (sums, True), (sums, True)]

    def forward_moves(ahead, back, summ):
        return shift(ahead, 1, n), shift(back, -1, n), shift(summ, 2, n)

    tail = shift(master[:, share - 2 * D :], 1, n)
    ahead, back, root, summ = call(first_kernel, (mev, frames), [SM, VM], msgs, [], flops=10**7)
    hl, hr, behind2 = forward_moves(ahead, back, summ)

    ext = jnp.concatenate([tail, master], axis=1)
    aligned = lax.dynamic_slice(ext, (0, 2 * D - step * me), (layers, MATS // n)).astype(BF16)
    gains = master[:, share - 2 * D :].astype(BF16).reshape(1, 16, 128)
    if fast:
        tiles = [to_tiles(aligned[l].reshape(-1, 128), me) for l in range(layers)]
        zd = 2
        for i in range(zd):
            root = spread_round(root, digits[i], digits[:i], n)
        b0 = after(jnp.concatenate([tiles[0], gains]), root, hl, hr, behind2)
        own0 = jnp.stack([b0] + [move(b0, "z", k) for k in range(1, 4)])
        for i in range(zd, len(digits)):
            root = spread_round(root, digits[i], digits[:i], n)
        own0 = after(own0, root)
        a0, s0 = move(own0, "a"), move(own0, "b")
        b1 = after(tiles[1], own0)
        own1 = jnp.stack([b1] + [move(b1, "z", k) for k in range(1, 4)])
        a0 = after(a0, s0, own1)
        as0 = move(a0, "b")
        w0 = [own0, a0, s0, as0]
        w0 += [move(after(v, own1), "core") for v in w0]
        own1 = after(own1, as0)
        a1, s1 = move(own1, "a"), move(own1, "b")
        w0 = tuple(w0)
    else:
        w0 = (gather_plain(aligned[0]), from_first(gains[0], me, n, n - 1))
        root = from_first(root, me, n)
    low_parts = (hl, hr, root, behind2, summ)

    first_seg = me * NSEG
    seg_ids = first_seg + jnp.arange(NSEG, dtype=jnp.int32)
    slot = jnp.arange(MEM, dtype=jnp.int32)
    loc = jnp.where(slot[None, :] == 0, mem_index, mem_index - first_seg + 96).reshape(-1, 1)
    loc = jnp.broadcast_to(loc, (NSEG * MEM, 128))
    vis = (mem_index < seg_ids[:, None]).astype(F32).reshape(-1, 1)
    vis = jnp.broadcast_to(vis, (NSEG * MEM, 128))

    hid = (rows16, tb, kv16, prob, tb)
    gt, hx0, q0, kv0, p0, o0 = call(
        functools.partial(low_attn_kernel, np_=len(w0), n=n), (mev, frames, *low_parts, loc, vis) + w0,
        [SM] + [VM] * 8 + [ANYS] * len(w0), [(((16, 128), BF16), True)] + [(t, False) for t in hid],
        wscr + vmem(*hid, score) + sems(5),
    )
    if fast:
        a1 = after(a1, o0)
        as1 = move(a1, "b")
        w1 = [own1, a1, s1]
        w1 = w1 + [as1] + [move(after(v, o0), "core") for v in w1]
    hid = (tf, tb, wide, wide)
    x1, h1, ahead, back, root, summ, a0, h20, gp0, act0 = call(
        functools.partial(low_ffn_kernel, np_=len(w0)), (mev, frames, o0, gt) + w0,
        [SM] + [VM] * 3 + [ANYS] * len(w0), [(tf, True), (tb, True)] + msgs + [(t, False) for t in hid],
        wscr + vmem(*hid) + sems(4),
    )
    if fast:
        ahead, back, root, summ, as1, *_ = lax.optimization_barrier((ahead, back, root, summ, as1, *w1[4:]))
        w1[3] = as1
    hl, hr, behind2 = forward_moves(ahead, back, summ)
    for i in range(len(digits)):
        root = spread_round(root, digits[i], digits[:i], n)
    if fast:
        w1 = tuple(w1 + [move(as1, "core")])
    else:
        w1 = (gather_plain(aligned[1]),)

    grads_out = [(tf, True), (((LH + NSEG, D), F32), True), (((RH, D), F32), True)] + [(((NSEG, D), F32), True)] * 3
    kept = (rows16, tb, tb, wide, tb, wide, tb, tb, kv16)
    output, da, dh, hal, har, root, b2, mine, dgb1, hx1, o1, h21, act1, dxb, dub, dab, dq, dkvb = call(
        functools.partial(top_kernel, np_=len(w1), n=n),
        (mev, x1, h1, hl, hr, root, behind2, summ, loc, vis, gt, cotangent) + w1,
        [SM] + [VM] * 10 + [ANYS] * (1 + len(w1)),
        [(tf, False), (tf, True)] + grads_out + [(drow, True)] + [(t, False) for t in kept],
        wscr + vmem(rows16, tb, kv16, prob, tb, tf, tb, wide, wide, tf, tf, tb, wide, tb, tb, kv16, kv32, tb, rows32, score) + sems(11),
        flops=8 * 10**9,
    )

    def backward_moves(hal, har, b2):
        return shift(hal, -1, n), shift(har, 1, n), shift(b2, -2, n)

    tree = digits[-1:] + digits[:-1]

    def collect(root, i):
        return collect_round(root, tree[i], tree[:i], n)

    dws = vmem(rows16, tb, kv16, tb, tb, tb, wide, wide, tb, tiles_t)
    dws += [pltpu.SemaphoreType.DMA] + sems(9)

    def weight_grads(part, ins, partial, gains=None):
        extra = BT + (1 if fast and gains_in else 0)
        outs = [(((2, 2, 4, extra, 16, 128), BF16), False)] * 2 if fast else [(tiles_t, False)]
        count = len(outs)
        ins = [mev] + list(ins) + ([] if gains is None else [gains])
        specs = [SM] + [ANYS] * 9 + [VM] * (len(ins) - 10)
        return call(
            functools.partial(dw_kernel, part=part, nouts=count, gains=gains is not None),
            ins + list(partial), specs + [ANYS] * len(partial), outs, dws,
            aliases={len(ins) + i: i for i in range(len(partial))}, flops=10**9,
        )

    gains_in = False
    hal, har, b2 = backward_moves(hal, har, b2)
    root = collect(root, 0)
    ins = [hx1, dq, dkvb, o1, dab, h21, dub, act1, after(dxb, root, hal, har, b2)]
    part = ()
    for i in range(2):
        part = weight_grads(i, ins, part)
        root = collect(root, i + 1)
        ins[6], ins[4] = after(dub, root), after(dab, root)
        root = after(root, part[0])
    for i in range(3, len(tree)):
        root = collect(root, i)
    grads = weight_grads(2, ins, part)

    def add(a, b):
        return (a.astype(F32) + b.astype(F32)).astype(BF16)

    if fast:
        v1 = after(add(grads[0], move(grads[1], "core")), root)
        got = move(v1[1], "b")
        x1 = after(x1, v1)
    else:
        reduced1 = reduce_plain(grads[0])

    dga1, da, dgb0, dxb, dub, dab = call(
        functools.partial(bottom_ffn_kernel, np_=len(w0)), (mev, hal, har, root, b2, mine, dh, x1, da, gt) + w0 + (a0, gp0),
        [SM] + [VM] * 9 + [ANYS] * (len(w0) + 2),
        [(drow, True), (tf, True), (drow, True), (tb, False), (wide, False), (tb, False)],
        wscr + vmem(tf, wide, tf, tb, wide, tb) + sems(5),
    )
    dga0, dh, hal, har, root, b2, mine, dq, dkvb = call(
        functools.partial(bottom_attn_kernel, np_=len(w0)),
        (mev, dab, loc, frames) + low_parts + w0 + (q0, kv0, p0), [SM] + [VM] * 8 + [ANYS] * (len(w0) + 3),
        [(drow, True)] + grads_out + [(tb, False), (kv16, False)],
        wscr + vmem(tb, kv16, prob, tb, kv16, kv32, tb, rows32, score) + sems(5),
    )
    gains = jnp.concatenate([dga0, dgb0, dga1, dgb1], axis=1)
    ins = [hx0, dq, dkvb, o0, dab, h20, dub, act0, dxb]
    if fast:
        v1 = add(after(v1[0], dh), got)
        got = move(v1[1], "a")
        ins[8] = after(dxb, v1)
        gains_in = True
    part = ()
    for i in range(2):
        part = weight_grads(i, ins, part)
    if fast:
        v1 = add(after(v1[0], part[0]), got)
        z1 = [move(v1[k], "z", k) for k in range(1, 4)]
        ins[4] = after(dab, v1)
    grads = weight_grads(2, ins, part, gains.astype(BF16).reshape(16, 128) if fast else None)
    if fast:
        v = add(grads[0], move(grads[1], "core"))
        root = collect(after(root, v), 0)
        got = move(v[1], "b")
        v = add(v[0], got)
        total1 = functools.reduce(jnp.add, [z.astype(F32) for z in z1], after(v1[0], v).astype(F32))
        got = move(v[1], "a")
        root = collect(collect(after(root, v, total1), 1), 2)
        reduced1, head1 = to_rows(total1, me), shift(head_rows(total1, me), -1, n)
        v = add(v[0], got)
        root = after(root, v, head1)
        zs = [move(v[k], "z", k) for k in range(1, 4)]
        for i in range(3, len(tree)):
            root = collect(root, i)
        hal, har, b2 = backward_moves(hal, har, after(b2, v))
        total0 = functools.reduce(jnp.add, [z.astype(F32) for z in zs], v[0].astype(F32))
        gsum = total0[BT].reshape(layers, 2 * D)
        total0 = total0[:BT]
        reduced = [to_rows(total0, me), reduced1]
        heads = [shift(head_rows(total0, me), -1, n), head1]
    else:
        hal, har, b2 = backward_moves(hal, har, b2)
        for i in range(len(tree)):
            root = collect(root, i)
        gsum = sum_all(gains.reshape(layers, 2 * D), n)
        reduced = [reduce_plain(grads[0]), reduced1]
        heads = [shift(r[: 2 * D], -1, n) for r in reduced]
    dx = call(
        last_kernel, (mev, hal, har, root, b2, mine, dh, frames, da, gt),
        [SM] + [VM] * 9, [(tf, True)], vmem(tf), flops=10**7,
    )[0]

    own = jnp.stack(reduced)
    head = jnp.where(me == n - 1, gsum, jnp.stack(heads))
    grad = lax.dynamic_slice(jnp.concatenate([own, head], axis=1), (0, step * me), (layers, share))
    gain_out = lax.dynamic_slice(gsum, (0, step * me), (layers, step))
    new_moment = 0.5 * moment + 0.5 * grad
    new_second = 0.5 * second + 0.5 * grad * grad
    correction = 1.0 - 0.5**STEP
    update = new_moment / correction / (jnp.sqrt(new_second / correction) + 1e-08) + 0.1 * master
    new_master = master - 0.08 * update
    new_average = 0.9 * average + 0.1 * new_master
    return (output, dx, gain_out, new_moment, new_second, new_master, new_average)


def solution(mesh):
    rows, flat = P("ta", None), P(None, "ta")
    return jax.shard_map(
        per_device,
        mesh=mesh,
        in_specs=(rows, rows, rows, flat, flat, flat, flat),
        out_specs=(rows, rows, flat, flat, flat, flat, flat),
        check_vma=False,
    )
```

time: 394 us -> 357 us (0.906)
  the two profiles are of different devices: /device:TPU:15 before, /device:TPU:20 now
where the time goes in v3:
time: 357 us; the launch traced here: 350 us
  starting transfers between devices  114 us (32%)
  Pallas kernels  103 us (29%)
  waiting for transfers between devices  89.4 us (25%)
  other arithmetic  26.5 us (7%)
  local copies, waits for them, and re-layouts  14.6 us (4%)
    pallas_call x13, Pallas kernels, run(): pl.pallas_call(kernel, out_shape=outs, input_output_aliases=aliases or {}...  103 us
    ppermute x32, waiting for transfers between devices, move(): return lax.ppermute(value, 'ta', links(32, kind, by))  53.4 us
    ppermute x15, starting transfers between devices, shift(): lax.ppermute(value, 'ta', [(i, i + by) for i in range(n) if 0 <= i + by <...  47.9 us
    ppermute x32, starting transfers between devices, move(): return lax.ppermute(value, 'ta', links(32, kind, by))  39.1 us
    ppermute x10, waiting for transfers between devices, spread_round(): lax.ppermute(value, 'ta', [(i, i + j * stride) for i in keep])  21.9 us
    ppermute x10, starting transfers between devices, collect_round(): lax.ppermute(value, 'ta', [(i + j * stride, i) for i in keep])  17.1 us
    ppermute x15, waiting for transfers between devices, shift(): lax.ppermute(value, 'ta', [(i, i + by) for i in range(n) if 0 <= i + by <...  12.2 us
    ppermute x10, starting transfers between devices, spread_round(): lax.ppermute(value, 'ta', [(i, i + j * stride) for i in keep])  10.4 us
  transfers between devices with their start and end apart: 67, of which 19 were waited for; matrix products, arithmetic and copies ran while one was open for 7% of the time, Pallas kernels for 18%

profile of v3, /device:TPU:20, one launch (start us, length us, event | category | flops | bytes accessed | tf_op | source)
XLA Modules:
  0.0 350.3 jit_solution(17835275514848705849)
XLA Ops:
  4.8 4.5 %collective-permute-start.1 = (bf16[16,512]{1,0:T(8,128)(2,1)}, bf16[16,512]{1,0:T(8,128)(2,1)S(1)}, u32[]{:S(2)}, u32[]{:S(2)}) collective-permute-start(bf16[16,512]{1,0:T(8,128)(2,1)} %get-tuple-element.109), channel_id=1, source_target_pairs={{1,0},{2,1},{3,2},{4,3},{5,4},{6,5},{7,6},{8,7},{9,8},{10,9},{11,1... | collective-permute-start | bytes 49160 | tf_op jit(solution)/shard_map/ppermute | solution.py:621
  15.2 3.8 %collective-permute-done.8 = bf16[2,1024]{1,0:T(2,128)(2,1)S(1)} collective-permute-done((bf16[2,1024]{1,0:T(2,128)(2,1)S(1)}, bf16[2,1024]{1,0:T(2,128)(2,1)S(1)}, u32[]{:S(2)}, u32[]{:S(2)}) %collective-permute-start.8) | collective-permute-done | bytes 4128 | tf_op jit(solution)/shard_map/ppermute | solution.py:621
  25.0 3.5 collective-permute-start.10
  29.7 9.5 %collective-permute-done.4 = bf16[32,512]{1,0:T(8,128)(2,1)S(1)} collective-permute-done((bf16[32,512]{1,0:T(8,128)(2,1)S(1)}, bf16[32,512]{1,0:T(8,128)(2,1)S(1)}, u32[]{:S(2)}, u32[]{:S(2)}) %collective-permute-start.4) | collective-permute-done | bytes 32800 | tf_op jit(solution)/shard_map/ppermute | solution.py:631
  51.5 11.6 %collective-permute-done.16 = bf16[48,16,128]{2,1,0:T(8,128)(2,1)S(1)} collective-permute-done((bf16[48,16,128]{2,1,0:T(8,128)(2,1)S(1)}, bf16[48,16,128]{2,1,0:T(8,128)(2,1)S(1)}, u32[]{:S(2)}, u32[]{:S(2)}) %collective-permute-start.16) | collective-permute-done | bytes 196640 | tf_op jit(solution)/shard_map/ppermute | solution.py:696
  63.2 3.4 collective-permute-done.15
  71.5 10.0 %collective-permute-done.17.rest_3_ = bf16[4,49,16,128]{3,2,1,0:T(8,128)(2,1)S(1)} collective-permute-done((bf16[4,49,16,128]{3,2,1,0:T(8,128)(2,1)S(1)}, bf16[4,49,16,128]{3,2,1,0:T(8,128)(2,1)S(1)}, u32[]{:S(2)}, u32[]{:S(2)}) %collective-permute-start.17) | collective-permute-done | bytes 802848 | tf_op jit(solution)/shard_map/ppermute | solution.py:696
  86.5 8.2 %shard_map.127 = (bf16[16,128]{1,0:T(8,128)(2,1)}, bf16[704,512]{1,0:T(8,128)(2,1)}, bf16[512,512]{1,0:T(8,128)(2,1)}, bf16[704,1024]{1,0:T(8,128)(2,1)}, bf16[3...) custom-call(s32[1]{0:T(128)} %bitcast.me_ref, bf16[512,512]{1,0:T(8,128)(2,1)} %x_ref.7, bf16[64,512]{1,0:T(8,128)(2,1)} %copy-done.26, ...), custom_call_target="tpu_custom_call" | custom-call | flops 3000000000 | bytes 10000000 | tf_op jit(solution)/shard_map/pallas_call | solution.py:608
  94.7 5.8 %collective-permute-done.22.rest_1_ = bf16[4,48,16,128]{3,2,1,0:T(8,128)(2,1)} collective-permute-done((bf16[4,48,16,128]{3,2,1,0:T(8,128)(2,1)}, bf16[4,48,16,128]{3,2,1,0:T(8,128)(2,1)}, u32[]{:S(2)}, u32[]{:S(2)}) %collective-permute-start.22) | collective-permute-done | bytes 786464 | tf_op jit(solution)/shard_map/ppermute | solution.py:696
  104.1 11.1 %shard_map.128 = (f32[512,512]{1,0:T(8,128)}, bf16[512,512]{1,0:T(8,128)(2,1)}, bf16[64,512]{1,0:T(8,128)(2,1)}, bf16[16,512]{1,0:T(8,128)(2,1)}, bf16[32,512]{1...) custom-call(s32[1]{0:T(128)} %bitcast.me_ref, ...), custom_call_target="tpu_custom_call" | custom-call | flops 3000000000 | bytes 10000000 | tf_op jit(solution)/shard_map/pallas_call | solution.py:608
  119.7 9.9 %collective-permute-done.32 = bf16[32,512]{1,0:T(8,128)(2,1)S(1)} collective-permute-done((bf16[32,512]{1,0:T(8,128)(2,1)S(1)}, bf16[32,512]{1,0:T(8,128)(2,1)S(1)}, u32[]{:S(2)}, u32[]{:S(2)}) %collective-permute-start.32) | collective-permute-done | bytes 32800 | tf_op jit(solution)/shard_map/ppermute | solution.py:631
  134.2 5.6 %collective-permute-start.35 = (bf16[32,512]{1,0:T(8,128)(2,1)}, bf16[32,512]{1,0:T(8,128)(2,1)S(1)}, u32[]{:S(2)}, u32[]{:S(2)}) collective-permute-start(bf16[32,512]{1,0:T(8,128)(2,1)} %get-tuple-element.136.summ_ref), channel_id=1, source_target_pairs={{0,2},{1,3},{2,4},{3,5},{4,6},{5,7},{6,8},{7,9},{8,10},{9,11},{10,... | collective-permute-start | bytes 98312 | tf_op jit(solution)/shard_map/ppermute | solution.py:621
  144.2 22.6 %shard_map.129 = (f32[512,512]{1,0:T(8,128)}, f32[512,512]{1,0:T(8,128)}, f32[512,512]{1,0:T(8,128)}, f32[64,512]{1,0:T(8,128)}, f32[16,512]{1,0:T(8,128)}, /*in...) custom-call(s32[1]{0:T(128)} %bitcast.me_ref, ...), custom_call_target="tpu_custom_call" | custom-call | flops 8000000000 | bytes 10000000 | tf_op jit(solution)/shard_map/pallas_call | solution.py:608
  166.9 4.5 %collective-permute-start.37 = (f32[64,512]{1,0:T(8,128)}, f32[64,512]{1,0:T(8,128)S(1)}, u32[]{:S(2)}, u32[]{:S(2)}) collective-permute-start(f32[64,512]{1,0:T(8,128)} %get-tuple-element.139), channel_id=1, source_target_pairs={{1,0},{2,1},{3,2},{4,3},{5,4},{6,5},{7,6},{8,7},{9,8},{10,9},{11,1... | collective-permute-start | bytes 393224 | tf_op jit(solution)/shard_map/ppermute | solution.py:621
  179.2 4.4 %collective-permute-done.38.har_ref = f32[16,512]{1,0:T(8,128)S(1)} collective-permute-done((f32[16,512]{1,0:T(8,128)}, f32[16,512]{1,0:T(8,128)S(1)}, u32[]{:S(2)}, u32[]{:S(2)}) %collective-permute-start.38) | collective-permute-done | bytes 32800 | tf_op jit(solution)/shard_map/ppermute | solution.py:621
  183.6 5.8 %shard_map.130 = (bf16[2,2,4,48,16,128]{5,4,3,2,1,0:T(8,128)(2,1)}, bf16[2,2,4,48,16,128]{5,4,3,2,1,0:T(8,128)(2,1)}) custom-call(s32[1]{0:T(128)} %bitcast.me_ref, bf16[704,512]{1,0:T(8,128)(2,1)} %get-tuple-element.142.rest_0_, bf16[512,512]{1,0:T(8,128)(2,1)} %get-tuple-element.143.rest_1_, bf16[704,1024]{1,0:T(8,128)(2,1)} %get-tuple-element.144.rest_2_, ...), custom_call_target="tpu_custom_call" | custom-call | flops 1000000000 | bytes 10000000 | tf_op jit(solution)/shard_map/pallas_call | solution.py:608
  190.7 6.1 %shard_map.131 = (bf16[2,2,4,48,16,128]{5,4,3,2,1,0:T(8,128)(2,1)}, bf16[2,2,4,48,16,128]{5,4,3,2,1,0:T(8,128)(2,1)}) custom-call(s32[1]{0:T(128)} %bitcast.me_ref, bf16[704,512]{1,0:T(8,128)(2,1)} %get-tuple-element.142.rest_0_, bf16[512,512]{1,0:T(8,128)(2,1)} %get-tuple-element.143.rest_1_, ...), custom_call_target="tpu_custom_call", output_to_operand_aliasing={{0}: (10, {}), {1}: (11, {})} | custom-call | flops 1000000000 | bytes 10000000 | tf_op jit(solution)/shard_map/pallas_call | solution.py:608
  196.8 5.0 %shard_map.132 = (bf16[2,2,4,48,16,128]{5,4,3,2,1,0:T(8,128)(2,1)}, bf16[2,2,4,48,16,128]{5,4,3,2,1,0:T(8,128)(2,1)}) custom-call(s32[1]{0:T(128)} %bitcast.me_ref, bf16[704,512]{1,0:T(8,128)(2,1)} %get-tuple-element.142.rest_0_, bf16[512,512]{1,0:T(8,128)(2,1)} %get-tuple-element.143.rest_1_, ...), custom_call_target="tpu_custom_call", output_to_operand_aliasing={{0}: (10, {}), {1}: (11, {})} | custom-call | flops 1000000000 | bytes 10000000 | tf_op jit(solution)/shard_map/pallas_call | solution.py:608
  203.9 3.8 %collective-permute-done.45 = bf16[2,2,4,48,16,128]{5,4,3,2,1,0:T(8,128)(2,1)S(1)} collective-permute-done((bf16[2,2,4,48,16,128]{5,4,3,2,1,0:T(8,128)(2,1)}, bf16[2,2,4,48,16,128]{5,4,3,2,1,0:T(8,128)(2,1)S(1)}, u32[]{:S(2)}, u32[]{:S(2)}) %collective-permute-start.45) | collective-permute-done | bytes 3145760 | tf_op jit(solution)/shard_map/ppermute | solution.py:696
  213.1 10.6 %shard_map.133 = (f32[1,512]{1,0:T(1,128)}, f32[512,512]{1,0:T(8,128)}, f32[1,512]{1,0:T(1,128)}, bf16[512,512]{1,0:T(8,128)(2,1)}, bf16[512,2048]{1,0:T(8,128)(2,1)}, /*index=5*/bf16[512,512]{1,0:T(8,128)(2,1)}) custom-call(s32[1]{0:T(128)} %bitcast.me_ref, f32[64,512]{1,0:T(8,128)} %copy-done.9, f32[16,512]{1,0:T(8,128)} %copy-done.13, ...), custom_call_target="tpu_custom_call" | custom-call | flops 3000000000 | bytes 10000000 | tf_op jit(solution)/shard_map/pallas_call | solution.py:608
  223.7 10.3 %shard_map.134 = (f32[1,512]{1,0:T(1,128)}, f32[512,512]{1,0:T(8,128)}, f32[64,512]{1,0:T(8,128)}, f32[16,512]{1,0:T(8,128)}, f32[32,512]{1,0:T(8,128)}, /*index...) custom-call(s32[1]{0:T(128)} %bitcast.me_ref, ...), custom_call_target="tpu_custom_call" | custom-call | flops 3000000000 | bytes 10000000 | tf_op jit(solution)/shard_map/pallas_call | solution.py:608
  235.6 5.8 %shard_map.135 = (bf16[2,2,4,49,16,128]{5,4,3,2,1,0:T(8,128)(2,1)}, bf16[2,2,4,49,16,128]{5,4,3,2,1,0:T(8,128)(2,1)}) custom-call(s32[1]{0:T(128)} %bitcast.me_ref, bf16[704,512]{1,0:T(8,128)(2,1)} %get-tuple-element.179.rest_0_, bf16[512,512]{1,0:T(8,128)(2,1)} %get-tuple-element.180.rest_1_, bf16[704,1024]{1,0:T(8,128)(2,1)} %get-tuple-element.181.rest_2_, ...), custom_call_target="tpu_custom_call" | custom-call | flops 1000000000 | bytes 10000000 | tf_op jit(solution)/shard_map/pallas_call | solution.py:608
  241.4 6.1 %shard_map.136 = (bf16[2,2,4,49,16,128]{5,4,3,2,1,0:T(8,128)(2,1)}, bf16[2,2,4,49,16,128]{5,4,3,2,1,0:T(8,128)(2,1)}) custom-call(s32[1]{0:T(128)} %bitcast.me_ref, bf16[704,512]{1,0:T(8,128)(2,1)} %get-tuple-element.179.rest_0_, bf16[512,512]{1,0:T(8,128)(2,1)} %get-tuple-element.180.rest_1_, ...), custom_call_target="tpu_custom_call", output_to_operand_aliasing={{0}: (10, {}), {1}: (11, {})} | custom-call | flops 1000000000 | bytes 10000000 | tf_op jit(solution)/shard_map/pallas_call | solution.py:608
  247.8 5.6 %shard_map.137 = (bf16[2,2,4,49,16,128]{5,4,3,2,1,0:T(8,128)(2,1)}, bf16[2,2,4,49,16,128]{5,4,3,2,1,0:T(8,128)(2,1)}) custom-call(s32[1]{0:T(128)} %bitcast.me_ref, bf16[704,512]{1,0:T(8,128)(2,1)} %get-tuple-element.179.rest_0_, bf16[512,512]{1,0:T(8,128)(2,1)} %get-tuple-element.180.rest_1_, ...), custom_call_target="tpu_custom_call", output_to_operand_aliasing={{0}: (11, {}), {1}: (12, {})} | custom-call | flops 1000000000 | bytes 10000000 | tf_op jit(solution)/shard_map/pallas_call | solution.py:608
  253.5 6.0 %collective-permute-done.50 = bf16[2,2,4,49,16,128]{5,4,3,2,1,0:T(8,128)(2,1)S(1)} collective-permute-done((bf16[2,2,4,49,16,128]{5,4,3,2,1,0:T(8,128)(2,1)}, bf16[2,2,4,49,16,128]{5,4,3,2,1,0:T(8,128)(2,1)S(1)}, u32[]{:S(2)}, u32[]{:S(2)}) %collective-permute-start.50) | collective-permute-done | bytes 3211296 | tf_op jit(solution)/shard_map/ppermute | solution.py:696
  265.8 4.6 %collective-permute-start.54 = (bf16[48,16,128]{2,1,0:T(8,128)(2,1)S(1)}, bf16[48,16,128]{2,1,0:T(8,128)(2,1)S(1)}, u32[]{:S(2)}, u32[]{:S(2)}) collective-permute-start(bf16[48,16,128]{2,1,0:T(8,128)(2,1)S(1)} %get-tuple-element.228), channel_id=1, source_target_pairs={{0,16},{1,17},{2,18},{3,19},{4,20},{5,21},{6,22},{7,23},{8,24},{9,... | collective-permute-start | bytes 589832 | tf_op jit(solution)/shard_map/ppermute | solution.py:696
  272.4 11.0 %collective-permute-done.52 = bf16[2,4,49,16,128]{4,3,2,1,0:T(8,128)(2,1)S(1)} collective-permute-done((bf16[2,4,49,16,128]{4,3,2,1,0:T(8,128)(2,1)S(1)}, bf16[2,4,49,16,128]{4,3,2,1,0:T(8,128)(2,1)S(1)}, u32[]{:S(2)}, u32[]{:S(2)}) %collective-permute-start.52) | collective-permute-done | bytes 1605664 | tf_op jit(solution)/shard_map/ppermute | solution.py:696
  290.1 7.8 %collective-permute-start.56 = (f32[32,512]{1,0:T(8,128)S(1)}, f32[32,512]{1,0:T(8,128)S(1)}, u32[]{:S(2)}, u32[]{:S(2)}) collective-permute-start(f32[32,512]{1,0:T(8,128)S(1)} %add.194), channel_id=1, source_target_pairs={{16,0},{18,2},{20,4},{22,6},{24,8},{26,10},{28,12},{30,14}} | collective-permute-start | bytes 196616 | tf_op jit(solution)/shard_map/ppermute | solution.py:638
  302.7 5.0 %collective-permute-start.65 = (bf16[49,16,128]{2,1,0:T(8,128)(2,1)}, bf16[49,16,128]{2,1,0:T(8,128)(2,1)S(1)}, u32[]{:S(2)}, u32[]{:S(2)}) collective-permute-start(bf16[49,16,128]{2,1,0:T(8,128)(2,1)} %get-tuple-element.220), channel_id=1, source_target_pairs={{0,24},{1,25},{2,26},{3,27},{4,28},{5,29},{6,30},{7,31},{8,0},{9,1... | collective-permute-start | bytes 602120 | tf_op jit(solution)/shard_map/ppermute | solution.py:696
  325.2 3.5 %shard_map.138 = f32[512,512]{1,0:T(8,128)} custom-call(s32[1]{0:T(128)} %bitcast.me_ref, f32[64,512]{1,0:T(8,128)} %collective-permute-done.46.hal_ref, f32[16,512]{1,0:T(8,128)} %copy-done.14, f32[32,512]{1,0:T(8,128)} %add.203.root_ref, f32[32,512]{1,0:T(8,128)} %copy-done.11, f32[32,512]{1,0:T(8,128)} %get-tuple-element.207.dtab_ref, ...), custom_call_target="tpu_custom_call" | custom-call | flops 10000000 | bytes 10000000 | tf_op jit(solution)/shard_map/pallas_call | solution.py:608
  328.9 11.2 %collective-permute-start.66 = (f32[1024]{0:T(1024)S(1)}, f32[1024]{0:T(1024)S(1)}, u32[]{:S(2)}, u32[]{:S(2)}) collective-permute-start(f32[1024]{0:T(1024)S(1)} %fusion.12), channel_id=1, source_target_pairs={{1,0},{2,1},{3,2},{4,3},{5,4},{6,5},{7,6},{8,7},{9,8},{10,9},{11,1... | collective-permute-start | bytes 12296 | tf_op jit(solution)/shard_map/ppermute | solution.py:621
  344.9 5.3 %multiply_add_fusion.1 = (f32[2,98336]{1,0:T(2,128)}, f32[2,98336]{1,0:T(2,128)}, f32[2,98336]{1,0:T(2,128)}, f32[2,98336]{1,0:T(2,128)}) fusion(f32[2,98336]{1,0:T(2,128)S(1)} %copy-done.6, f32[2,98336]{1,0:T(2,128)S(1)} %copy-done.1, f32[2,98336]{1,0:T(2,128)S(1)} %copy-done.7, f32[2,98336]{1,0:T(2,128)S(1)} %copy-done.8, s32[]{:T(128)S(6)} %select_n.105, ...), kind=kLoop, calls=%fused_computation.25 | loop fusion | flops 3736768 | bytes 7088132 | tf_op jit(solution)/shard_map/add | solution.py:956
  (270 shorter events, 115.9 us)
Async XLA Ops:
  2.8 21.6 %collective-permute-start = (bf16[64,512]{1,0:T(8,128)(2,1)}, bf16[64,512]{1,0:T(8,128)(2,1)S(1)}, u32[]{:S(2)}, u32[]{:S(2)}) collective-permute-start(bf16[64,512]{1,0:T(8,128)(2,1)} %get-tuple-element.108), channel_id=1, source_target_pairs={{0,1},{1,2},{2,3},{3,4},{4,5},{5,6},{6,7},{7,8},{8,9},{9,10},{10,1... | collective-permute-start | bytes 196616 | tf_op jit(solution)/shard_map/ppermute | solution.py:621
  4.8 19.6 %collective-permute-start.1 = (bf16[16,512]{1,0:T(8,128)(2,1)}, bf16[16,512]{1,0:T(8,128)(2,1)S(1)}, u32[]{:S(2)}, u32[]{:S(2)}) collective-permute-start(bf16[16,512]{1,0:T(8,128)(2,1)} %get-tuple-element.109), channel_id=1, source_target_pairs={{1,0},{2,1},{3,2},{4,3},{5,4},{6,5},{7,6},{8,7},{9,8},{10,9},{11,1... | collective-permute-start | bytes 49160 | tf_op jit(solution)/shard_map/ppermute | solution.py:621
  9.3 14.3 %collective-permute-start.2 = (bf16[32,512]{1,0:T(8,128)(2,1)}, bf16[32,512]{1,0:T(8,128)(2,1)S(1)}, u32[]{:S(2)}, u32[]{:S(2)}) collective-permute-start(bf16[32,512]{1,0:T(8,128)(2,1)} %get-tuple-element.110), channel_id=1, source_target_pairs={{0,16}} | collective-permute-start | bytes 98312 | tf_op jit(solution)/shard_map/ppermute | solution.py:631
  10.0 14.4 %collective-permute-start.7 = (bf16[32,512]{1,0:T(8,128)(2,1)}, bf16[32,512]{1,0:T(8,128)(2,1)S(1)}, u32[]{:S(2)}, u32[]{:S(2)}) collective-permute-start(bf16[32,512]{1,0:T(8,128)(2,1)} %get-tuple-element.111.summ_ref.summ0_ref), channel_id=1, source_target_pairs={{0,2},{1,3},{2,4},{3,5},{4,6},{5,7},{6,8},{7,9},{8,10},{9,11},{10,... | collective-permute-start | bytes 98312 | tf_op jit(solution)/shard_map/ppermute | solution.py:621
  24.5 20.5 %collective-permute-start.11 = (bf16[49,16,128]{2,1,0:T(8,128)(2,1)S(1)}, bf16[49,16,128]{2,1,0:T(8,128)(2,1)S(1)}, u32[]{:S(2)}, u32[]{:S(2)}) collective-permute-start(bf16[49,16,128]{2,1,0:T(8,128)(2,1)S(1)} %pad_maximum_fusion.2), channel_id=1, source_target_pairs={{0,24},{1,25},{2,26},{3,27},{4,28},{5,29},{6,30},{7,31},{8,0},{9,1... | collective-permute-start | bytes 602120 | tf_op jit(solution)/shard_map/ppermute | solution.py:696
  25.0 20.0 %collective-permute-start.10 = (bf16[49,16,128]{2,1,0:T(8,128)(2,1)S(1)}, bf16[49,16,128]{2,1,0:T(8,128)(2,1)S(1)}, u32[]{:S(2)}, u32[]{:S(2)}) collective-permute-start(bf16[49,16,128]{2,1,0:T(8,128)(2,1)S(1)} %pad_maximum_fusion.2), channel_id=1, source_target_pairs={{0,16},{1,17},{2,18},{3,19},{4,20},{5,21},{6,22},{7,23},{8,24},{9,... | collective-permute-start | bytes 602120 | tf_op jit(solution)/shard_map/ppermute | solution.py:696
  28.4 16.5 %collective-permute-start.9 = (bf16[49,16,128]{2,1,0:T(8,128)(2,1)S(1)}, bf16[49,16,128]{2,1,0:T(8,128)(2,1)S(1)}, u32[]{:S(2)}, u32[]{:S(2)}) collective-permute-start(bf16[49,16,128]{2,1,0:T(8,128)(2,1)S(1)} %pad_maximum_fusion.2), channel_id=1, source_target_pairs={{0,8},{1,9},{2,10},{3,11},{4,12},{5,13},{6,14},{7,15},{8,16},{9,17... | collective-permute-start | bytes 602120 | tf_op jit(solution)/shard_map/ppermute | solution.py:696
  45.1 24.2 %collective-permute-start.12 = (bf16[4,49,16,128]{3,2,1,0:T(8,128)(2,1)S(1)}, bf16[4,49,16,128]{3,2,1,0:T(8,128)(2,1)S(1)}, u32[]{:S(2)}, u32[]{:S(2)}) collective-permute-start(bf16[4,49,16,128]{3,2,1,0:T(8,128)(2,1)S(1)} %pad_maximum_fusion.rest_0_), channel_id=1, source_target_pairs={{0,2},{1,5},{2,0},{3,7},{4,6},{5,1},{6,4},{7,3},{8,10},{9,13},{10,... | collective-permute-start | bytes 2408456 | tf_op jit(solution)/shard_map/ppermute | solution.py:696
  47.5 21.8 %collective-permute-start.13 = (bf16[4,49,16,128]{3,2,1,0:T(8,128)(2,1)S(1)}, bf16[4,49,16,128]{3,2,1,0:T(8,128)(2,1)S(1)}, u32[]{:S(2)}, u32[]{:S(2)}) collective-permute-start(bf16[4,49,16,128]{3,2,1,0:T(8,128)(2,1)S(1)} %pad_maximum_fusion.rest_0_), channel_id=1, source_target_pairs={{0,4},{1,3},{2,6},{3,1},{4,0},{5,7},{6,2},{7,5},{8,12},{9,11},{10,... | collective-permute-start | bytes 2408456 | tf_op jit(solution)/shard_map/ppermute | solution.py:696
  47.5 15.7 %collective-permute-start.16 = (bf16[48,16,128]{2,1,0:T(8,128)(2,1)S(1)}, bf16[48,16,128]{2,1,0:T(8,128)(2,1)S(1)}, u32[]{:S(2)}, u32[]{:S(2)}) collective-permute-start(bf16[48,16,128]{2,1,0:T(8,128)(2,1)S(1)} %bitcast.138), channel_id=1, source_target_pairs={{0,24},{1,25},{2,26},{3,27},{4,28},{5,29},{6,30},{7,31},{8,0},{9,1... | collective-permute-start | bytes 589832 | tf_op jit(solution)/shard_map/ppermute | solution.py:696
  49.5 17.1 %collective-permute-start.15 = (bf16[48,16,128]{2,1,0:T(8,128)(2,1)S(1)}, bf16[48,16,128]{2,1,0:T(8,128)(2,1)S(1)}, u32[]{:S(2)}, u32[]{:S(2)}) collective-permute-start(bf16[48,16,128]{2,1,0:T(8,128)(2,1)S(1)} %bitcast.139), channel_id=1, source_target_pairs={{0,16},{1,17},{2,18},{3,19},{4,20},{5,21},{6,22},{7,23},{8,24},{9,... | collective-permute-start | bytes 589832 | tf_op jit(solution)/shard_map/ppermute | solution.py:696
  51.3 17.0 %collective-permute-start.14 = (bf16[48,16,128]{2,1,0:T(8,128)(2,1)S(1)}, bf16[48,16,128]{2,1,0:T(8,128)(2,1)S(1)}, u32[]{:S(2)}, u32[]{:S(2)}) collective-permute-start(bf16[48,16,128]{2,1,0:T(8,128)(2,1)S(1)} %bitcast.140), channel_id=1, source_target_pairs={{0,8},{1,9},{2,10},{3,11},{4,12},{5,13},{6,14},{7,15},{8,16},{9,17... | collective-permute-start | bytes 589832 | tf_op jit(solution)/shard_map/ppermute | solution.py:696
  69.3 12.2 %collective-permute-start.17 = (bf16[4,49,16,128]{3,2,1,0:T(8,128)(2,1)S(1)}, bf16[4,49,16,128]{3,2,1,0:T(8,128)(2,1)S(1)}, u32[]{:S(2)}, u32[]{:S(2)}) collective-permute-start(bf16[4,49,16,128]{3,2,1,0:T(8,128)(2,1)S(1)} %collective-permute-done.12.rest_1_), channel_id=1, source_target_pairs={{0,4},{1,3},{2,6},{3,1},{4,0},{5,7},{6,2},{7,5},{8,12},{9,11},{10,... | collective-permute-start | bytes 2408456 | tf_op jit(solution)/shard_map/ppermute | solution.py:696
  71.0 14.0 %collective-permute-start.19 = (bf16[4,49,16,128]{3,2,1,0:T(8,128)(2,1)S(1)}, bf16[4,49,16,128]{3,2,1,0:T(8,128)(2,1)}, u32[]{:S(2)}, u32[]{:S(2)}) collective-permute-start(bf16[4,49,16,128]{3,2,1,0:T(8,128)(2,1)S(1)} %collective-permute-done.12.rest_1_), channel_id=1, source_target_pairs={{0,1},{1,0},{2,3},{3,2},{4,5},{5,4},{6,7},{7,6},{8,9},{9,8},{10,11... | collective-permute-start | bytes 2408456 | tf_op jit(solution)/shard_map/ppermute | solution.py:696
  71.5 13.5 %collective-permute-start.20 = (bf16[4,49,16,128]{3,2,1,0:T(8,128)(2,1)S(1)}, bf16[4,49,16,128]{3,2,1,0:T(8,128)(2,1)}, u32[]{:S(2)}, u32[]{:S(2)}) collective-permute-start(bf16[4,49,16,128]{3,2,1,0:T(8,128)(2,1)S(1)} %collective-permute-done.13.rest_2_), channel_id=1, source_target_pairs={{0,1},{1,0},{2,3},{3,2},{4,5},{5,4},{6,7},{7,6},{8,9},{9,8},{10,11... | collective-permute-start | bytes 2408456 | tf_op jit(solution)/shard_map/ppermute | solution.py:696
  81.5 18.9 %collective-permute-start.22 = (bf16[4,48,16,128]{3,2,1,0:T(8,128)(2,1)}, bf16[4,48,16,128]{3,2,1,0:T(8,128)(2,1)}, u32[]{:S(2)}, u32[]{:S(2)}) collective-permute-start(bf16[4,48,16,128]{3,2,1,0:T(8,128)(2,1)} %pad_maximum_fusion.1.rest_0_), channel_id=1, source_target_pairs={{0,2},{1,5},{2,0},{3,7},{4,6},{5,1},{6,4},{7,3},{8,10},{9,13},{10,... | collective-permute-start | bytes 2359304 | tf_op jit(solution)/shard_map/ppermute | solution.py:696
  82.9 21.2 %collective-permute-start.26 = (bf16[4,48,16,128]{3,2,1,0:T(8,128)(2,1)}, bf16[4,48,16,128]{3,2,1,0:T(8,128)(2,1)}, u32[]{:S(2)}, u32[]{:S(2)}) collective-permute-start(bf16[4,48,16,128]{3,2,1,0:T(8,128)(2,1)} %pad_maximum_fusion.1.rest_0_), channel_id=1, source_target_pairs={{0,4},{1,3},{2,6},{3,1},{4,0},{5,7},{6,2},{7,5},{8,12},{9,11},{10,... | collective-permute-start | bytes 2359304 | tf_op jit(solution)/shard_map/ppermute | solution.py:696
  100.5 14.7 %collective-permute-start.23 = (bf16[4,48,16,128]{3,2,1,0:T(8,128)(2,1)}, bf16[4,48,16,128]{3,2,1,0:T(8,128)(2,1)S(1)}, u32[]{:S(2)}, u32[]{:S(2)}) collective-permute-start(bf16[4,48,16,128]{3,2,1,0:T(8,128)(2,1)} %collective-permute-done.22.rest_1_), channel_id=1, source_target_pairs={{0,4},{1,3},{2,6},{3,1},{4,0},{5,7},{6,2},{7,5},{8,12},{9,11},{10,... | collective-permute-start | bytes 2359304 | tf_op jit(solution)/shard_map/ppermute | solution.py:696
  115.3 28.0 %collective-permute-start.36 = (bf16[4,48,16,128]{3,2,1,0:T(8,128)(2,1)S(1)}, bf16[4,48,16,128]{3,2,1,0:T(8,128)(2,1)S(1)}, u32[]{:S(2)}, u32[]{:S(2)}) collective-permute-start(bf16[4,48,16,128]{3,2,1,0:T(8,128)(2,1)S(1)} %collective-permute-done.23.rest_3_), channel_id=1, source_target_pairs={{0,1},{1,0},{2,3},{3,2},{4,5},{5,4},{6,7},{7,6},{8,9},{9,8},{10,11... | collective-permute-start | bytes 2359304 | tf_op jit(solution)/shard_map/ppermute | solution.py:696
  130.9 12.4 %collective-permute-start.28 = (bf16[64,512]{1,0:T(8,128)(2,1)}, bf16[64,512]{1,0:T(8,128)(2,1)S(1)}, u32[]{:S(2)}, u32[]{:S(2)}) collective-permute-start(bf16[64,512]{1,0:T(8,128)(2,1)} %get-tuple-element.133), channel_id=1, source_target_pairs={{0,1},{1,2},{2,3},{3,4},{4,5},{5,6},{6,7},{7,8},{8,9},{9,10},{10,1... | collective-permute-start | bytes 196616 | tf_op jit(solution)/shard_map/ppermute | solution.py:621
  166.9 16.7 %collective-permute-start.37 = (f32[64,512]{1,0:T(8,128)}, f32[64,512]{1,0:T(8,128)S(1)}, u32[]{:S(2)}, u32[]{:S(2)}) collective-permute-start(f32[64,512]{1,0:T(8,128)} %get-tuple-element.139), channel_id=1, source_target_pairs={{1,0},{2,1},{3,2},{4,3},{5,4},{6,5},{7,6},{8,7},{9,8},{10,9},{11,1... | collective-permute-start | bytes 393224 | tf_op jit(solution)/shard_map/ppermute | solution.py:621
  211.0 23.1 %collective-permute-start.48 = (bf16[2,4,48,16,128]{4,3,2,1,0:T(8,128)(2,1)S(1)}, bf16[2,4,48,16,128]{4,3,2,1,0:T(8,128)(2,1)S(1)}, u32[]{:S(2)}, u32[]{:S(2)}) collective-permute-start(bf16[2,4,48,16,128]{4,3,2,1,0:T(8,128)(2,1)S(1)} %get-tuple-element.216), channel_id=1, source_target_pairs={{0,4},{1,3},{2,6},{3,1},{4,0},{5,7},{6,2},{7,5},{8,12},{9,11},{10,... | collective-permute-start | bytes 4718600 | tf_op jit(solution)/shard_map/ppermute | solution.py:696
  234.8 12.8 %collective-permute-start.49 = (bf16[4,48,16,128]{3,2,1,0:T(8,128)(2,1)S(1)}, bf16[4,48,16,128]{3,2,1,0:T(8,128)(2,1)S(1)}, u32[]{:S(2)}, u32[]{:S(2)}) collective-permute-start(bf16[4,48,16,128]{3,2,1,0:T(8,128)(2,1)S(1)} %get-tuple-element.218), channel_id=1, source_target_pairs={{0,2},{1,5},{2,0},{3,7},{4,6},{5,1},{6,4},{7,3},{8,10},{9,13},{10,... | collective-permute-start | bytes 2359304 | tf_op jit(solution)/shard_map/ppermute | solution.py:696
  262.5 20.8 %collective-permute-start.52 = (bf16[2,4,49,16,128]{4,3,2,1,0:T(8,128)(2,1)S(1)}, bf16[2,4,49,16,128]{4,3,2,1,0:T(8,128)(2,1)S(1)}, u32[]{:S(2)}, u32[]{:S(2)}) collective-permute-start(bf16[2,4,49,16,128]{4,3,2,1,0:T(8,128)(2,1)S(1)} %slice_bitcast_fusion), channel_id=1, source_target_pairs={{0,4},{1,3},{2,6},{3,1},{4,0},{5,7},{6,2},{7,5},{8,12},{9,11},{10,... | collective-permute-start | bytes 4816904 | tf_op jit(solution)/shard_map/ppermute | solution.py:696
  264.6 24.4 %collective-permute-start.55 = (bf16[48,16,128]{2,1,0:T(8,128)(2,1)}, bf16[48,16,128]{2,1,0:T(8,128)(2,1)S(1)}, u32[]{:S(2)}, u32[]{:S(2)}) collective-permute-start(bf16[48,16,128]{2,1,0:T(8,128)(2,1)} %get-tuple-element.227), channel_id=1, source_target_pairs={{0,24},{1,25},{2,26},{3,27},{4,28},{5,29},{6,30},{7,31},{8,0},{9,1... | collective-permute-start | bytes 589832 | tf_op jit(solution)/shard_map/ppermute | solution.py:696
  265.8 23.3 %collective-permute-start.54 = (bf16[48,16,128]{2,1,0:T(8,128)(2,1)S(1)}, bf16[48,16,128]{2,1,0:T(8,128)(2,1)S(1)}, u32[]{:S(2)}, u32[]{:S(2)}) collective-permute-start(bf16[48,16,128]{2,1,0:T(8,128)(2,1)S(1)} %get-tuple-element.228), channel_id=1, source_target_pairs={{0,16},{1,17},{2,18},{3,19},{4,20},{5,21},{6,22},{7,23},{8,24},{9,... | collective-permute-start | bytes 589832 | tf_op jit(solution)/shard_map/ppermute | solution.py:696
  270.3 18.8 %collective-permute-start.53 = (bf16[48,16,128]{2,1,0:T(8,128)(2,1)S(1)}, bf16[48,16,128]{2,1,0:T(8,128)(2,1)}, u32[]{:S(2)}, u32[]{:S(2)}) collective-permute-start(bf16[48,16,128]{2,1,0:T(8,128)(2,1)S(1)} %get-tuple-element.229), channel_id=1, source_target_pairs={{0,8},{1,9},{2,10},{3,11},{4,12},{5,13},{6,14},{7,15},{8,16},{9,17... | collective-permute-start | bytes 589832 | tf_op jit(solution)/shard_map/ppermute | solution.py:696
  283.9 16.7 %collective-permute-start.58 = (bf16[4,49,16,128]{3,2,1,0:T(8,128)(2,1)S(1)}, bf16[4,49,16,128]{3,2,1,0:T(8,128)(2,1)}, u32[]{:S(2)}, u32[]{:S(2)}) collective-permute-start(bf16[4,49,16,128]{3,2,1,0:T(8,128)(2,1)S(1)} %slice_bitcast_fusion.4), channel_id=1, source_target_pairs={{0,2},{1,5},{2,0},{3,7},{4,6},{5,1},{6,4},{7,3},{8,10},{9,13},{10,... | collective-permute-start | bytes 2408456 | tf_op jit(solution)/shard_map/ppermute | solution.py:696
  302.7 26.0 %collective-permute-start.65 = (bf16[49,16,128]{2,1,0:T(8,128)(2,1)}, bf16[49,16,128]{2,1,0:T(8,128)(2,1)S(1)}, u32[]{:S(2)}, u32[]{:S(2)}) collective-permute-start(bf16[49,16,128]{2,1,0:T(8,128)(2,1)} %get-tuple-element.220), channel_id=1, source_target_pairs={{0,24},{1,25},{2,26},{3,27},{4,28},{5,29},{6,30},{7,31},{8,0},{9,1... | collective-permute-start | bytes 602120 | tf_op jit(solution)/shard_map/ppermute | solution.py:696
  307.7 21.0 %collective-permute-start.64 = (bf16[49,16,128]{2,1,0:T(8,128)(2,1)S(1)}, bf16[49,16,128]{2,1,0:T(8,128)(2,1)S(1)}, u32[]{:S(2)}, u32[]{:S(2)}) collective-permute-start(bf16[49,16,128]{2,1,0:T(8,128)(2,1)S(1)} %get-tuple-element.221), channel_id=1, source_target_pairs={{0,16},{1,17},{2,18},{3,19},{4,20},{5,21},{6,22},{7,23},{8,24},{9,... | collective-permute-start | bytes 602120 | tf_op jit(solution)/shard_map/ppermute | solution.py:696
  307.7 21.0 %collective-permute-start.63 = (bf16[49,16,128]{2,1,0:T(8,128)(2,1)S(1)}, bf16[49,16,128]{2,1,0:T(8,128)(2,1)S(1)}, u32[]{:S(2)}, u32[]{:S(2)}) collective-permute-start(bf16[49,16,128]{2,1,0:T(8,128)(2,1)S(1)} %get-tuple-element.219), channel_id=1, source_target_pairs={{0,8},{1,9},{2,10},{3,11},{4,12},{5,13},{6,14},{7,15},{8,16},{9,17... | collective-permute-start | bytes 602120 | tf_op jit(solution)/shard_map/ppermute | solution.py:696
  328.9 15.9 %collective-permute-start.66 = (f32[1024]{0:T(1024)S(1)}, f32[1024]{0:T(1024)S(1)}, u32[]{:S(2)}, u32[]{:S(2)}) collective-permute-start(f32[1024]{0:T(1024)S(1)} %fusion.12), channel_id=1, source_target_pairs={{1,0},{2,1},{3,2},{4,3},{5,4},{6,5},{7,6},{8,7},{9,8},{10,9},{11,1... | collective-permute-start | bytes 12296 | tf_op jit(solution)/shard_map/ppermute | solution.py:621
  (68 other events, 759.1 us)

commit v4 on v3

--- a/solution.py
+++ b/solution.py
@@ -278,7 +278,7 @@
         kv_ref[:, 512 * j : 512 * j + 512] = mm(hx_ref[...], wblk(w_ref, QKV0, 12, 0, 32, 4 + 4 * j, 4)).astype(BF16)
 
 
-def feed_forward(h2_ref, w_ref, act_ref, gp_ref, out_ref, step):
+def feed_forward(h2_ref, w_ref, act_ref, gp_ref, out_ref, ready):
     for c in range(4):
         u = mm(h2_ref[...], wblk(w_ref, WU0, 16, 0, 32, 4 * c, 4))
         cc, c3 = 0.7978845608028654, 0.7978845608028654 * 0.044715
@@ -289,8 +289,9 @@
         gp = 0.5 + 0.5 * t + hu * (1.0 - t * t) * (cc + 3 * c3 * u2)
         act_ref[:, 512 * c : 512 * c + 512] = act
         gp_ref[:, 512 * c : 512 * c + 512] = gp.astype(BF16)
+        if c == 0:
+            ready()
         out_ref[...] += mm(act, wblk(w_ref, WD0, 4, 32 * c, 32, 0, 4))
-        step(c)
 
 
 def back_ffn(dx_ref, w_ref, gains, a_ref, gp_ref, da_ref, dxb_ref, dub_ref, dab_ref, dgb_ref, step):
@@ -330,11 +331,12 @@
     hi = dch.astype(BF16)
     oh = onehot_of(loc_ref)
     dtab = mm_tn(oh, hi) + mm_tn(oh, (dch - hi.astype(F32)).astype(BF16))
-    hal_ref[0:LH] = dh_ref[0:LH]
-    hal_ref[LH:] = dtab[64:96]
-    har_ref[...] = dh_ref[LH + TOK : LH + TOK + RH]
-    root_ref[...] = dtab[0:32]
-    b2_ref[...] = dtab[32:64]
+    kind = hal_ref.dtype
+    hal_ref[0:LH] = dh_ref[0:LH].astype(kind)
+    hal_ref[LH:] = dtab[64:96].astype(kind)
+    har_ref[...] = dh_ref[LH + TOK : LH + TOK + RH].astype(kind)
+    root_ref[...] = dtab[0:32].astype(kind)
+    b2_ref[...] = dtab[32:64].astype(kind)
     mine_ref[...] = dtab[96:128]
     return dtab
 
@@ -378,8 +380,8 @@
     h2_ref[...] = (xhat * gain_row(gt_ref, 0, 1)).astype(BF16)
     copies.out(h2_ref, h2_o)
     out_ref[...] = a
-    await_weights(w_ref, sems, 11, 32)
-    feed_forward(h2_ref, w_ref, act_ref, gp_ref, out_ref, lambda c: None)
+    await_weights(w_ref, sems, 11, 22)
+    feed_forward(h2_ref, w_ref, act_ref, gp_ref, out_ref, lambda: await_weights(w_ref, sems, 22, 32))
     copies.out(act_ref, act_o)
     copies.out(gp_ref, gp_o)
     h1n, sumn = head_of_layer(out_ref[...], gain_row(gt_ref, 1, 0))
@@ -416,7 +418,7 @@
     h2_ref[...] = (xhat * gain_row(gt_ref, 1, 1)).astype(BF16)
     copies.out(h2_ref, h2_o)
     out_ref[...] = a
-    feed_forward(h2_ref, w_ref, act_ref, gp_ref, out_ref, lambda c: None)
+    feed_forward(h2_ref, w_ref, act_ref, gp_ref, out_ref, lambda: None)
     copies.out(act_ref, act_o)
     copies.out(out_ref, out_o)
     cot.wait()
@@ -436,8 +438,8 @@
 
 def norm_one_back(dh_ref, hal_ref, har_ref, dsum, x, gain, da_ref, acc_ref):
     acc_ref[...] = dh_ref[...]
-    acc_ref[TOK - LH : TOK] += hal_ref[0:LH]
-    acc_ref[0:RH] += har_ref[...]
+    acc_ref[TOK - LH : TOK] += hal_ref[0:LH].astype(F32)
+    acc_ref[0:RH] += har_ref[...].astype(F32)
     for s in range(NSEG):
         acc_ref[SEG * s : SEG * s + SEG] += dsum[s : s + 1, :] * (1.0 / SEG)
     xhat, rstd = norm_parts(x)
@@ -446,7 +448,8 @@
 
 
 def summed(me_ref, hal_ref, root_ref, b2_ref, mine_ref):
-    return mine_ref[...] + hal_ref[LH:] + b2_ref[...] + jnp.where(me_ref[0] == 0, root_ref[...], 0.0)
+    near = mine_ref[...] + hal_ref[LH:].astype(F32) + b2_ref[...].astype(F32)
+    return near + jnp.where(me_ref[0] == 0, root_ref[...].astype(F32), 0.0)
 
 
 def bottom_ffn_kernel(me_ref, hal_ref, har_ref, root_ref, b2_ref, dtabp_ref, dhp_ref, x_ref, dap_ref, gt_ref, *rest, np_):
@@ -561,7 +564,7 @@
             put(mm_tn(act_ref[:, pl.ds(c0, 256)], dxb_ref[...]), WD0, 4, 16 * c, 0)
             return carry
 
-        lax.fori_loop(0, FF // 256, down, 0)
+        lax.fori_loop(0, FF // 256, down, 0, unroll=4)
         send(64, 96)
     if part == 1:
         loads[5].wait()
@@ -572,7 +575,7 @@
             put(mm_tn(h2_ref[...], dub_ref[:, pl.ds(c0, 256)]), WU0, 16, 0, 2 * c)
             return carry
 
-        lax.fori_loop(0, FF // 256, up, 0)
+        lax.fori_loop(0, FF // 256, up, 0, unroll=4)
         send(32, 64)
     if part == 2:
         for i in (3, 4, 0, 1, 2):
@@ -636,7 +639,7 @@
     stride, radix = digit
     keep = [i for i in range(n) if all(i // s % r == 0 for s, r in [digit] + done)]
     parts = [lax.ppermute(value, "ta", [(i + j * stride, i) for i in keep]) for j in range(1, radix)]
-    return functools.reduce(jnp.add, parts, value)
+    return sum((part.astype(F32) for part in parts), value.astype(F32)).astype(value.dtype)
 
 
 def from_first(value, me, n, root=0):
@@ -761,6 +764,7 @@
 
     tail = shift(master[:, share - 2 * D :], 1, n)
     ahead, back, root, summ = call(first_kernel, (mev, frames), [SM, VM], msgs, [], flops=10**7)
+    ahead, back, root, summ, tail = lax.optimization_barrier((ahead, back, root, summ, tail))
     hl, hr, behind2 = forward_moves(ahead, back, summ)
 
     ext = jnp.concatenate([tail, master], axis=1)
@@ -783,7 +787,6 @@
         as0 = move(a0, "b")
         w0 = [own0, a0, s0, as0]
         w0 += [move(after(v, own1), "core") for v in w0]
-        own1 = after(own1, as0)
         a1, s1 = move(own1, "a"), move(own1, "b")
         w0 = tuple(w0)
     else:
@@ -822,18 +825,23 @@
     hl, hr, behind2 = forward_moves(ahead, back, summ)
     for i in range(len(digits)):
         root = spread_round(root, digits[i], digits[:i], n)
+        if i == 1:
+            root = after(root, hl, hr, behind2)
     if fast:
         w1 = tuple(w1 + [move(as1, "core")])
     else:
         w1 = (gather_plain(aligned[1]),)
 
-    grads_out = [(tf, True), (((LH + NSEG, D), F32), True), (((RH, D), F32), True)] + [(((NSEG, D), F32), True)] * 3
+    def grads_out(kind):
+        shapes = ((LH + NSEG, D), kind), ((RH, D), kind), ((NSEG, D), kind), ((NSEG, D), kind), ((NSEG, D), F32)
+        return [(tf, True)] + [(shape, True) for shape in shapes]
+
     kept = (rows16, tb, tb, wide, tb, wide, tb, tb, kv16)
     output, da, dh, hal, har, root, b2, mine, dgb1, hx1, o1, h21, act1, dxb, dub, dab, dq, dkvb = call(
         functools.partial(top_kernel, np_=len(w1), n=n),
         (mev, x1, h1, hl, hr, root, behind2, summ, loc, vis, gt, cotangent) + w1,
         [SM] + [VM] * 10 + [ANYS] * (1 + len(w1)),
-        [(tf, False), (tf, True)] + grads_out + [(drow, True)] + [(t, False) for t in kept],
+        [(tf, False), (tf, True)] + grads_out(BF16) + [(drow, True)] + [(t, False) for t in kept],
         wscr + vmem(rows16, tb, kv16, prob, tb, tf, tb, wide, wide, tf, tf, tb, wide, tb, tb, kv16, kv32, tb, rows32, score) + sems(11),
         flops=8 * 10**9,
     )
@@ -894,7 +902,7 @@
     dga0, dh, hal, har, root, b2, mine, dq, dkvb = call(
         functools.partial(bottom_attn_kernel, np_=len(w0)),
         (mev, dab, loc, frames) + low_parts + w0 + (q0, kv0, p0), [SM] + [VM] * 8 + [ANYS] * (len(w0) + 3),
-        [(drow, True)] + grads_out + [(tb, False), (kv16, False)],
+        [(drow, True)] + grads_out(F32) + [(tb, False), (kv16, False)],
         wscr + vmem(tb, kv16, prob, tb, kv16, kv32, tb, rows32, score) + sems(5),
     )
     gains = jnp.concatenate([dga0, dgb0, dga1, dgb1], axis=1)

time: 357 us -> 348 us (0.975)
  Pallas kernels: 103 us -> 98 us
    pallas_call x13, Pallas kernels: 103 us -> 98 us  [run(): pl.pallas_call(kernel, out_shape=outs, input_output_aliases=aliases or {}...]
  transfers between devices with their start and end apart: 67 -> 67, of which waited for: 19 -> 21; matrix products, arithmetic and copies ran while one was open for 7% -> 7% of each run, Pallas kernels for 18% -> 18%
where the time goes in v4:
time: 348 us; the launch traced here: 342 us
  starting transfers between devices  114 us (33%)
  Pallas kernels  98 us (28%)
  waiting for transfers between devices  86.5 us (25%)
  other arithmetic  26.4 us (8%)
  local copies, waits for them, and re-layouts  14.6 us (4%)
    pallas_call x13, Pallas kernels, run(): pl.pallas_call(kernel, out_shape=outs, input_output_aliases=aliases or {}...  98 us
    ppermute x32, waiting for transfers between devices, move(): return lax.ppermute(value, 'ta', links(32, kind, by))  53.5 us
    ppermute x15, starting transfers between devices, shift(): lax.ppermute(value, 'ta', [(i, i + by) for i in range(n) if 0 <= i + by <...  46.7 us
    ppermute x32, starting transfers between devices, move(): return lax.ppermute(value, 'ta', links(32, kind, by))  39.2 us
    ppermute x10, waiting for transfers between devices, spread_round(): lax.ppermute(value, 'ta', [(i, i + j * stride) for i in keep])  20.7 us
    ppermute x10, starting transfers between devices, collect_round(): lax.ppermute(value, 'ta', [(i + j * stride, i) for i in keep])  16.9 us
    ppermute x10, starting transfers between devices, spread_round(): lax.ppermute(value, 'ta', [(i, i + j * stride) for i in keep])  10.9 us
    ppermute x15, waiting for transfers between devices, shift(): lax.ppermute(value, 'ta', [(i, i + by) for i in range(n) if 0 <= i + by <...  10.4 us
  transfers between devices with their start and end apart: 67, of which 21 were waited for; matrix products, arithmetic and copies ran while one was open for 7% of the time, Pallas kernels for 18%

profile of v4, /device:TPU:20, one launch (start us, length us, event | category | flops | bytes accessed | tf_op | source)
XLA Modules:
  0.0 341.7 jit_solution(18393376341667824935)
XLA Ops:
  9.3 4.5 %collective-permute-start.2 = (bf16[16,512]{1,0:T(8,128)(2,1)}, bf16[16,512]{1,0:T(8,128)(2,1)S(1)}, u32[]{:S(2)}, u32[]{:S(2)}) collective-permute-start(bf16[16,512]{1,0:T(8,128)(2,1)} %get-tuple-element.118), channel_id=1, source_target_pairs={{1,0},{2,1},{3,2},{4,3},{5,4},{6,5},{7,6},{8,7},{9,8},{10,9},{11,1... | collective-permute-start | bytes 49160 | tf_op jit(solution)/shard_map/ppermute | solution.py:624
  22.3 3.5 %collective-permute-start.10 = (bf16[49,16,128]{2,1,0:T(8,128)(2,1)S(1)}, bf16[49,16,128]{2,1,0:T(8,128)(2,1)S(1)}, u32[]{:S(2)}, u32[]{:S(2)}) collective-permute-start(bf16[49,16,128]{2,1,0:T(8,128)(2,1)S(1)} %pad_maximum_fusion.2), channel_id=1, source_target_pairs={{0,16},{1,17},{2,18},{3,19},{4,20},{5,21},{6,22},{7,23},{8,24},{9,... | collective-permute-start | bytes 602120 | tf_op jit(solution)/shard_map/ppermute | solution.py:699
  27.1 10.3 %collective-permute-done.5 = bf16[32,512]{1,0:T(8,128)(2,1)S(1)} collective-permute-done((bf16[32,512]{1,0:T(8,128)(2,1)S(1)}, bf16[32,512]{1,0:T(8,128)(2,1)S(1)}, u32[]{:S(2)}, u32[]{:S(2)}) %collective-permute-start.5) | collective-permute-done | bytes 32800 | tf_op jit(solution)/shard_map/ppermute | solution.py:634
  49.7 11.6 %collective-permute-done.16 = bf16[48,16,128]{2,1,0:T(8,128)(2,1)S(1)} collective-permute-done((bf16[48,16,128]{2,1,0:T(8,128)(2,1)S(1)}, bf16[48,16,128]{2,1,0:T(8,128)(2,1)S(1)}, u32[]{:S(2)}, u32[]{:S(2)}) %collective-permute-start.16) | collective-permute-done | bytes 196640 | tf_op jit(solution)/shard_map/ppermute | solution.py:699
  61.3 3.4 %collective-permute-done.15 = bf16[48,16,128]{2,1,0:T(8,128)(2,1)S(1)} collective-permute-done((bf16[48,16,128]{2,1,0:T(8,128)(2,1)S(1)}, bf16[48,16,128]{2,1,0:T(8,128)(2,1)S(1)}, u32[]{:S(2)}, u32[]{:S(2)}) %collective-permute-start.15) | collective-permute-done | bytes 196640 | tf_op jit(solution)/shard_map/ppermute | solution.py:699
  69.6 10.0 %collective-permute-done.17.rest_3_ = bf16[4,49,16,128]{3,2,1,0:T(8,128)(2,1)S(1)} collective-permute-done((bf16[4,49,16,128]{3,2,1,0:T(8,128)(2,1)S(1)}, bf16[4,49,16,128]{3,2,1,0:T(8,128)(2,1)S(1)}, u32[]{:S(2)}, u32[]{:S(2)}) %collective-permute-start.17) | collective-permute-done | bytes 802848 | tf_op jit(solution)/shard_map/ppermute | solution.py:699
  84.6 8.2 %shard_map.127 = (bf16[16,128]{1,0:T(8,128)(2,1)}, bf16[704,512]{1,0:T(8,128)(2,1)}, bf16[512,512]{1,0:T(8,128)(2,1)}, bf16[704,1024]{1,0:T(8,128)(2,1)}, bf16[3...) custom-call(s32[1]{0:T(128)} %bitcast.me_ref, bf16[512,512]{1,0:T(8,128)(2,1)} %x_ref.7, bf16[64,512]{1,0:T(8,128)(2,1)} %copy-done.26, ...), custom_call_target="tpu_custom_call" | custom-call | flops 3000000000 | bytes 10000000 | tf_op jit(solution)/shard_map/pallas_call | solution.py:611
  92.8 5.8 %collective-permute-done.22.rest_1_ = bf16[4,48,16,128]{3,2,1,0:T(8,128)(2,1)} collective-permute-done((bf16[4,48,16,128]{3,2,1,0:T(8,128)(2,1)}, bf16[4,48,16,128]{3,2,1,0:T(8,128)(2,1)}, u32[]{:S(2)}, u32[]{:S(2)}) %collective-permute-start.22) | collective-permute-done | bytes 786464 | tf_op jit(solution)/shard_map/ppermute | solution.py:699
  102.2 11.5 %shard_map.128 = (f32[512,512]{1,0:T(8,128)}, bf16[512,512]{1,0:T(8,128)(2,1)}, bf16[64,512]{1,0:T(8,128)(2,1)}, bf16[16,512]{1,0:T(8,128)(2,1)}, bf16[32,512]{1...) custom-call(s32[1]{0:T(128)} %bitcast.me_ref, ...), custom_call_target="tpu_custom_call" | custom-call | flops 3000000000 | bytes 10000000 | tf_op jit(solution)/shard_map/pallas_call | solution.py:611
  120.9 4.3 %collective-permute-start.29 = (bf16[16,512]{1,0:T(8,128)(2,1)}, bf16[16,512]{1,0:T(8,128)(2,1)S(1)}, u32[]{:S(2)}, u32[]{:S(2)}) collective-permute-start(bf16[16,512]{1,0:T(8,128)(2,1)} %get-tuple-element.143), channel_id=1, source_target_pairs={{1,0},{2,1},{3,2},{4,3},{5,4},{6,5},{7,6},{8,7},{9,8},{10,9},{11,1... | collective-permute-start | bytes 49160 | tf_op jit(solution)/shard_map/ppermute | solution.py:624
  128.1 6.1 %collective-permute-done.33 = bf16[32,512]{1,0:T(8,128)(2,1)S(1)} collective-permute-done((bf16[32,512]{1,0:T(8,128)(2,1)S(1)}, bf16[32,512]{1,0:T(8,128)(2,1)S(1)}, u32[]{:S(2)}, u32[]{:S(2)}) %collective-permute-start.33) | collective-permute-done | bytes 32800 | tf_op jit(solution)/shard_map/ppermute | solution.py:634
  140.8 22.5 %shard_map.129 = (f32[512,512]{1,0:T(8,128)}, f32[512,512]{1,0:T(8,128)}, f32[512,512]{1,0:T(8,128)}, bf16[64,512]{1,0:T(8,128)(2,1)}, bf16[16,512]{1,0:T(8,128)...) custom-call(s32[1]{0:T(128)} %bitcast.me_ref, ...), custom_call_target="tpu_custom_call" | custom-call | flops 8000000000 | bytes 10000000 | tf_op jit(solution)/shard_map/pallas_call | solution.py:611
  164.7 4.1 %collective-permute-start.37 = (bf16[64,512]{1,0:T(8,128)(2,1)}, bf16[64,512]{1,0:T(8,128)(2,1)S(1)}, u32[]{:S(2)}, u32[]{:S(2)}) collective-permute-start(bf16[64,512]{1,0:T(8,128)(2,1)} %get-tuple-element.149), channel_id=1, source_target_pairs={{1,0},{2,1},{3,2},{4,3},{5,4},{6,5},{7,6},{8,7},{9,8},{10,9},{11,1... | collective-permute-start | bytes 196616 | tf_op jit(solution)/shard_map/ppermute | solution.py:624
  175.3 4.2 %collective-permute-done.38.har_ref = bf16[16,512]{1,0:T(8,128)(2,1)S(1)} collective-permute-done((bf16[16,512]{1,0:T(8,128)(2,1)}, bf16[16,512]{1,0:T(8,128)(2,1)S(1)}, u32[]{:S(2)}, u32[]{:S(2)}) %collective-permute-start.38) | collective-permute-done | bytes 16416 | tf_op jit(solution)/shard_map/ppermute | solution.py:624
  179.6 4.6 %shard_map.130 = (bf16[2,2,4,48,16,128]{5,4,3,2,1,0:T(8,128)(2,1)}, bf16[2,2,4,48,16,128]{5,4,3,2,1,0:T(8,128)(2,1)}) custom-call(s32[1]{0:T(128)} %bitcast.me_ref, bf16[704,512]{1,0:T(8,128)(2,1)} %get-tuple-element.152.rest_0_, bf16[512,512]{1,0:T(8,128)(2,1)} %get-tuple-element.153.rest_1_, bf16[704,1024]{1,0:T(8,128)(2,1)} %get-tuple-element.154.rest_2_, ...), custom_call_target="tpu_custom_call" | custom-call | flops 1000000000 | bytes 10000000 | tf_op jit(solution)/shard_map/pallas_call | solution.py:611
  185.1 4.7 %shard_map.131 = (bf16[2,2,4,48,16,128]{5,4,3,2,1,0:T(8,128)(2,1)}, bf16[2,2,4,48,16,128]{5,4,3,2,1,0:T(8,128)(2,1)}) custom-call(s32[1]{0:T(128)} %bitcast.me_ref, bf16[704,512]{1,0:T(8,128)(2,1)} %get-tuple-element.152.rest_0_, bf16[512,512]{1,0:T(8,128)(2,1)} %get-tuple-element.153.rest_1_, ...), custom_call_target="tpu_custom_call", output_to_operand_aliasing={{0}: (10, {}), {1}: (11, {})} | custom-call | flops 1000000000 | bytes 10000000 | tf_op jit(solution)/shard_map/pallas_call | solution.py:611
  189.9 5.0 %shard_map.132 = (bf16[2,2,4,48,16,128]{5,4,3,2,1,0:T(8,128)(2,1)}, bf16[2,2,4,48,16,128]{5,4,3,2,1,0:T(8,128)(2,1)}) custom-call(s32[1]{0:T(128)} %bitcast.me_ref, bf16[704,512]{1,0:T(8,128)(2,1)} %get-tuple-element.152.rest_0_, bf16[512,512]{1,0:T(8,128)(2,1)} %get-tuple-element.153.rest_1_, ...), custom_call_target="tpu_custom_call", output_to_operand_aliasing={{0}: (10, {}), {1}: (11, {})} | custom-call | flops 1000000000 | bytes 10000000 | tf_op jit(solution)/shard_map/pallas_call | solution.py:611
  197.0 3.8 %collective-permute-done.45 = bf16[2,2,4,48,16,128]{5,4,3,2,1,0:T(8,128)(2,1)S(1)} collective-permute-done((bf16[2,2,4,48,16,128]{5,4,3,2,1,0:T(8,128)(2,1)}, bf16[2,2,4,48,16,128]{5,4,3,2,1,0:T(8,128)(2,1)S(1)}, u32[]{:S(2)}, u32[]{:S(2)}) %collective-permute-start.45) | collective-permute-done | bytes 3145760 | tf_op jit(solution)/shard_map/ppermute | solution.py:699
  204.9 10.4 %shard_map.133 = (f32[1,512]{1,0:T(1,128)}, f32[512,512]{1,0:T(8,128)}, f32[1,512]{1,0:T(1,128)}, bf16[512,512]{1,0:T(8,128)(2,1)}, bf16[512,2048]{1,0:T(8,128)(2,1)}, /*index=5*/bf16[512,512]{1,0:T(8,128)(2,1)}) custom-call(s32[1]{0:T(128)} %bitcast.me_ref, bf16[64,512]{1,0:T(8,128)(2,1)} %copy-done.9, bf16[16,512]{1,0:T(8,128)(2,1)} %copy-done.15, ...), custom_call_target="tpu_custom_call" | custom-call | flops 3000000000 | bytes 10000000 | tf_op jit(solution)/shard_map/pallas_call | solution.py:611
  215.3 10.4 %shard_map.134 = (f32[1,512]{1,0:T(1,128)}, f32[512,512]{1,0:T(8,128)}, f32[64,512]{1,0:T(8,128)}, f32[16,512]{1,0:T(8,128)}, f32[32,512]{1,0:T(8,128)}, /*index...) custom-call(s32[1]{0:T(128)} %bitcast.me_ref, ...), custom_call_target="tpu_custom_call" | custom-call | flops 3000000000 | bytes 10000000 | tf_op jit(solution)/shard_map/pallas_call | solution.py:611
  227.8 4.6 %shard_map.135 = (bf16[2,2,4,49,16,128]{5,4,3,2,1,0:T(8,128)(2,1)}, bf16[2,2,4,49,16,128]{5,4,3,2,1,0:T(8,128)(2,1)}) custom-call(s32[1]{0:T(128)} %bitcast.me_ref, bf16[704,512]{1,0:T(8,128)(2,1)} %get-tuple-element.189.rest_0_, bf16[512,512]{1,0:T(8,128)(2,1)} %get-tuple-element.190.rest_1_, bf16[704,1024]{1,0:T(8,128)(2,1)} %get-tuple-element.191.rest_2_, ...), custom_call_target="tpu_custom_call" | custom-call | flops 1000000000 | bytes 10000000 | tf_op jit(solution)/shard_map/pallas_call | solution.py:611
  232.4 4.8 %shard_map.136 = (bf16[2,2,4,49,16,128]{5,4,3,2,1,0:T(8,128)(2,1)}, bf16[2,2,4,49,16,128]{5,4,3,2,1,0:T(8,128)(2,1)}) custom-call(s32[1]{0:T(128)} %bitcast.me_ref, bf16[704,512]{1,0:T(8,128)(2,1)} %get-tuple-element.189.rest_0_, bf16[512,512]{1,0:T(8,128)(2,1)} %get-tuple-element.190.rest_1_, ...), custom_call_target="tpu_custom_call", output_to_operand_aliasing={{0}: (10, {}), {1}: (11, {})} | custom-call | flops 1000000000 | bytes 10000000 | tf_op jit(solution)/shard_map/pallas_call | solution.py:611
  238.7 5.6 %shard_map.137 = (bf16[2,2,4,49,16,128]{5,4,3,2,1,0:T(8,128)(2,1)}, bf16[2,2,4,49,16,128]{5,4,3,2,1,0:T(8,128)(2,1)}) custom-call(s32[1]{0:T(128)} %bitcast.me_ref, bf16[704,512]{1,0:T(8,128)(2,1)} %get-tuple-element.189.rest_0_, bf16[512,512]{1,0:T(8,128)(2,1)} %get-tuple-element.190.rest_1_, ...), custom_call_target="tpu_custom_call", output_to_operand_aliasing={{0}: (11, {}), {1}: (12, {})} | custom-call | flops 1000000000 | bytes 10000000 | tf_op jit(solution)/shard_map/pallas_call | solution.py:611
  244.4 6.0 %collective-permute-done.50 = bf16[2,2,4,49,16,128]{5,4,3,2,1,0:T(8,128)(2,1)S(1)} collective-permute-done((bf16[2,2,4,49,16,128]{5,4,3,2,1,0:T(8,128)(2,1)}, bf16[2,2,4,49,16,128]{5,4,3,2,1,0:T(8,128)(2,1)S(1)}, u32[]{:S(2)}, u32[]{:S(2)}) %collective-permute-start.50) | collective-permute-done | bytes 3211296 | tf_op jit(solution)/shard_map/ppermute | solution.py:699
  256.9 6.7 %collective-permute-start.54 = (bf16[48,16,128]{2,1,0:T(8,128)(2,1)S(1)}, bf16[48,16,128]{2,1,0:T(8,128)(2,1)S(1)}, u32[]{:S(2)}, u32[]{:S(2)}) collective-permute-start(bf16[48,16,128]{2,1,0:T(8,128)(2,1)S(1)} %get-tuple-element.238), channel_id=1, source_target_pairs={{0,16},{1,17},{2,18},{3,19},{4,20},{5,21},{6,22},{7,23},{8,24},{9,... | collective-permute-start | bytes 589832 | tf_op jit(solution)/shard_map/ppermute | solution.py:699
  265.6 8.7 %collective-permute-done.52 = bf16[2,4,49,16,128]{4,3,2,1,0:T(8,128)(2,1)S(1)} collective-permute-done((bf16[2,4,49,16,128]{4,3,2,1,0:T(8,128)(2,1)S(1)}, bf16[2,4,49,16,128]{4,3,2,1,0:T(8,128)(2,1)S(1)}, u32[]{:S(2)}, u32[]{:S(2)}) %collective-permute-start.52) | collective-permute-done | bytes 1605664 | tf_op jit(solution)/shard_map/ppermute | solution.py:699
  280.8 7.6 %collective-permute-start.56 = (f32[32,512]{1,0:T(8,128)S(1)}, f32[32,512]{1,0:T(8,128)S(1)}, u32[]{:S(2)}, u32[]{:S(2)}) collective-permute-start(f32[32,512]{1,0:T(8,128)S(1)} %add.194), channel_id=1, source_target_pairs={{16,0},{18,2},{20,4},{22,6},{24,8},{26,10},{28,12},{30,14}} | collective-permute-start | bytes 196616 | tf_op jit(solution)/shard_map/ppermute | solution.py:641
  293.3 5.0 %collective-permute-start.65 = (bf16[49,16,128]{2,1,0:T(8,128)(2,1)}, bf16[49,16,128]{2,1,0:T(8,128)(2,1)S(1)}, u32[]{:S(2)}, u32[]{:S(2)}) collective-permute-start(bf16[49,16,128]{2,1,0:T(8,128)(2,1)} %get-tuple-element.230), channel_id=1, source_target_pairs={{0,24},{1,25},{2,26},{3,27},{4,28},{5,29},{6,30},{7,31},{8,0},{9,1... | collective-permute-start | bytes 602120 | tf_op jit(solution)/shard_map/ppermute | solution.py:699
  308.5 4.5 %collective-permute-start.62 = (f32[32,512]{1,0:T(8,128)}, f32[32,512]{1,0:T(8,128)S(1)}, u32[]{:S(2)}, u32[]{:S(2)}) collective-permute-start(f32[32,512]{1,0:T(8,128)} %get-tuple-element.216), channel_id=1, source_target_pairs={{2,0},{3,1},{4,2},{5,3},{6,4},{7,5},{8,6},{9,7},{10,8},{11,9},{12,... | collective-permute-start | bytes 196616 | tf_op jit(solution)/shard_map/ppermute | solution.py:624
  318.0 3.5 %shard_map.138 = f32[512,512]{1,0:T(8,128)} custom-call(s32[1]{0:T(128)} %bitcast.me_ref, f32[64,512]{1,0:T(8,128)} %collective-permute-done.46.hal_ref, f32[16,512]{1,0:T(8,128)} %copy-done.13, f32[32,512]{1,0:T(8,128)} %add.203.root_ref, f32[32,512]{1,0:T(8,128)} %copy-done.10, f32[32,512]{1,0:T(8,128)} %get-tuple-element.217.dtab_ref, ...), custom_call_target="tpu_custom_call" | custom-call | flops 10000000 | bytes 10000000 | tf_op jit(solution)/shard_map/pallas_call | solution.py:611
  321.7 9.8 %collective-permute-start.66 = (f32[1024]{0:T(1024)S(1)}, f32[1024]{0:T(1024)S(1)}, u32[]{:S(2)}, u32[]{:S(2)}) collective-permute-start(f32[1024]{0:T(1024)S(1)} %fusion.12), channel_id=1, source_target_pairs={{1,0},{2,1},{3,2},{4,3},{5,4},{6,5},{7,6},{8,7},{9,8},{10,9},{11,1... | collective-permute-start | bytes 12296 | tf_op jit(solution)/shard_map/ppermute | solution.py:624
  336.2 5.3 %multiply_add_fusion.1 = (f32[2,98336]{1,0:T(2,128)}, f32[2,98336]{1,0:T(2,128)}, f32[2,98336]{1,0:T(2,128)}, f32[2,98336]{1,0:T(2,128)}) fusion(f32[2,98336]{1,0:T(2,128)S(1)} %copy-done.6, f32[2,98336]{1,0:T(2,128)S(1)} %copy-done.1, f32[2,98336]{1,0:T(2,128)S(1)} %copy-done.7, f32[2,98336]{1,0:T(2,128)S(1)} %copy-done.8, s32[]{:T(128)S(6)} %select_n.105, ...), kind=kLoop, calls=%fused_computation.25 | loop fusion | flops 3736768 | bytes 7088132 | tf_op jit(solution)/shard_map/add | solution.py:964
  (270 shorter events, 118.4 us)
Async XLA Ops:
  7.2 14.6 %collective-permute-start.1 = (bf16[64,512]{1,0:T(8,128)(2,1)}, bf16[64,512]{1,0:T(8,128)(2,1)S(1)}, u32[]{:S(2)}, u32[]{:S(2)}) collective-permute-start(bf16[64,512]{1,0:T(8,128)(2,1)} %get-tuple-element.117), channel_id=1, source_target_pairs={{0,1},{1,2},{2,3},{3,4},{4,5},{5,6},{6,7},{7,8},{8,9},{9,10},{10,1... | collective-permute-start | bytes 196616 | tf_op jit(solution)/shard_map/ppermute | solution.py:624
  9.3 12.5 %collective-permute-start.2 = (bf16[16,512]{1,0:T(8,128)(2,1)}, bf16[16,512]{1,0:T(8,128)(2,1)S(1)}, u32[]{:S(2)}, u32[]{:S(2)}) collective-permute-start(bf16[16,512]{1,0:T(8,128)(2,1)} %get-tuple-element.118), channel_id=1, source_target_pairs={{1,0},{2,1},{3,2},{4,3},{5,4},{6,5},{7,6},{8,7},{9,8},{10,9},{11,1... | collective-permute-start | bytes 49160 | tf_op jit(solution)/shard_map/ppermute | solution.py:624
  21.8 21.2 %collective-permute-start.11 = (bf16[49,16,128]{2,1,0:T(8,128)(2,1)S(1)}, bf16[49,16,128]{2,1,0:T(8,128)(2,1)S(1)}, u32[]{:S(2)}, u32[]{:S(2)}) collective-permute-start(bf16[49,16,128]{2,1,0:T(8,128)(2,1)S(1)} %pad_maximum_fusion.2), channel_id=1, source_target_pairs={{0,24},{1,25},{2,26},{3,27},{4,28},{5,29},{6,30},{7,31},{8,0},{9,1... | collective-permute-start | bytes 602120 | tf_op jit(solution)/shard_map/ppermute | solution.py:699
  22.3 20.7 %collective-permute-start.10 = (bf16[49,16,128]{2,1,0:T(8,128)(2,1)S(1)}, bf16[49,16,128]{2,1,0:T(8,128)(2,1)S(1)}, u32[]{:S(2)}, u32[]{:S(2)}) collective-permute-start(bf16[49,16,128]{2,1,0:T(8,128)(2,1)S(1)} %pad_maximum_fusion.2), channel_id=1, source_target_pairs={{0,16},{1,17},{2,18},{3,19},{4,20},{5,21},{6,22},{7,23},{8,24},{9,... | collective-permute-start | bytes 602120 | tf_op jit(solution)/shard_map/ppermute | solution.py:699
  25.8 17.2 %collective-permute-start.9 = (bf16[49,16,128]{2,1,0:T(8,128)(2,1)S(1)}, bf16[49,16,128]{2,1,0:T(8,128)(2,1)S(1)}, u32[]{:S(2)}, u32[]{:S(2)}) collective-permute-start(bf16[49,16,128]{2,1,0:T(8,128)(2,1)S(1)} %pad_maximum_fusion.2), channel_id=1, source_target_pairs={{0,8},{1,9},{2,10},{3,11},{4,12},{5,13},{6,14},{7,15},{8,16},{9,17... | collective-permute-start | bytes 602120 | tf_op jit(solution)/shard_map/ppermute | solution.py:699
  43.2 24.2 %collective-permute-start.12 = (bf16[4,49,16,128]{3,2,1,0:T(8,128)(2,1)S(1)}, bf16[4,49,16,128]{3,2,1,0:T(8,128)(2,1)S(1)}, u32[]{:S(2)}, u32[]{:S(2)}) collective-permute-start(bf16[4,49,16,128]{3,2,1,0:T(8,128)(2,1)S(1)} %pad_maximum_fusion.rest_0_), channel_id=1, source_target_pairs={{0,2},{1,5},{2,0},{3,7},{4,6},{5,1},{6,4},{7,3},{8,10},{9,13},{10,... | collective-permute-start | bytes 2408456 | tf_op jit(solution)/shard_map/ppermute | solution.py:699
  45.6 21.8 %collective-permute-start.13 = (bf16[4,49,16,128]{3,2,1,0:T(8,128)(2,1)S(1)}, bf16[4,49,16,128]{3,2,1,0:T(8,128)(2,1)S(1)}, u32[]{:S(2)}, u32[]{:S(2)}) collective-permute-start(bf16[4,49,16,128]{3,2,1,0:T(8,128)(2,1)S(1)} %pad_maximum_fusion.rest_0_), channel_id=1, source_target_pairs={{0,4},{1,3},{2,6},{3,1},{4,0},{5,7},{6,2},{7,5},{8,12},{9,11},{10,... | collective-permute-start | bytes 2408456 | tf_op jit(solution)/shard_map/ppermute | solution.py:699
  45.6 15.7 %collective-permute-start.16 = (bf16[48,16,128]{2,1,0:T(8,128)(2,1)S(1)}, bf16[48,16,128]{2,1,0:T(8,128)(2,1)S(1)}, u32[]{:S(2)}, u32[]{:S(2)}) collective-permute-start(bf16[48,16,128]{2,1,0:T(8,128)(2,1)S(1)} %bitcast.138), channel_id=1, source_target_pairs={{0,24},{1,25},{2,26},{3,27},{4,28},{5,29},{6,30},{7,31},{8,0},{9,1... | collective-permute-start | bytes 589832 | tf_op jit(solution)/shard_map/ppermute | solution.py:699
  47.6 17.1 %collective-permute-start.15 = (bf16[48,16,128]{2,1,0:T(8,128)(2,1)S(1)}, bf16[48,16,128]{2,1,0:T(8,128)(2,1)S(1)}, u32[]{:S(2)}, u32[]{:S(2)}) collective-permute-start(bf16[48,16,128]{2,1,0:T(8,128)(2,1)S(1)} %bitcast.139), channel_id=1, source_target_pairs={{0,16},{1,17},{2,18},{3,19},{4,20},{5,21},{6,22},{7,23},{8,24},{9,... | collective-permute-start | bytes 589832 | tf_op jit(solution)/shard_map/ppermute | solution.py:699
  49.4 17.0 %collective-permute-start.14 = (bf16[48,16,128]{2,1,0:T(8,128)(2,1)S(1)}, bf16[48,16,128]{2,1,0:T(8,128)(2,1)S(1)}, u32[]{:S(2)}, u32[]{:S(2)}) collective-permute-start(bf16[48,16,128]{2,1,0:T(8,128)(2,1)S(1)} %bitcast.140), channel_id=1, source_target_pairs={{0,8},{1,9},{2,10},{3,11},{4,12},{5,13},{6,14},{7,15},{8,16},{9,17... | collective-permute-start | bytes 589832 | tf_op jit(solution)/shard_map/ppermute | solution.py:699
  67.4 12.2 %collective-permute-start.17 = (bf16[4,49,16,128]{3,2,1,0:T(8,128)(2,1)S(1)}, bf16[4,49,16,128]{3,2,1,0:T(8,128)(2,1)S(1)}, u32[]{:S(2)}, u32[]{:S(2)}) collective-permute-start(bf16[4,49,16,128]{3,2,1,0:T(8,128)(2,1)S(1)} %collective-permute-done.12.rest_1_), channel_id=1, source_target_pairs={{0,4},{1,3},{2,6},{3,1},{4,0},{5,7},{6,2},{7,5},{8,12},{9,11},{10,... | collective-permute-start | bytes 2408456 | tf_op jit(solution)/shard_map/ppermute | solution.py:699
  69.1 14.0 %collective-permute-start.19 = (bf16[4,49,16,128]{3,2,1,0:T(8,128)(2,1)S(1)}, bf16[4,49,16,128]{3,2,1,0:T(8,128)(2,1)}, u32[]{:S(2)}, u32[]{:S(2)}) collective-permute-start(bf16[4,49,16,128]{3,2,1,0:T(8,128)(2,1)S(1)} %collective-permute-done.12.rest_1_), channel_id=1, source_target_pairs={{0,1},{1,0},{2,3},{3,2},{4,5},{5,4},{6,7},{7,6},{8,9},{9,8},{10,11... | collective-permute-start | bytes 2408456 | tf_op jit(solution)/shard_map/ppermute | solution.py:699
  69.6 13.5 %collective-permute-start.20 = (bf16[4,49,16,128]{3,2,1,0:T(8,128)(2,1)S(1)}, bf16[4,49,16,128]{3,2,1,0:T(8,128)(2,1)}, u32[]{:S(2)}, u32[]{:S(2)}) collective-permute-start(bf16[4,49,16,128]{3,2,1,0:T(8,128)(2,1)S(1)} %collective-permute-done.13.rest_2_), channel_id=1, source_target_pairs={{0,1},{1,0},{2,3},{3,2},{4,5},{5,4},{6,7},{7,6},{8,9},{9,8},{10,11... | collective-permute-start | bytes 2408456 | tf_op jit(solution)/shard_map/ppermute | solution.py:699
  79.6 18.9 %collective-permute-start.22 = (bf16[4,48,16,128]{3,2,1,0:T(8,128)(2,1)}, bf16[4,48,16,128]{3,2,1,0:T(8,128)(2,1)}, u32[]{:S(2)}, u32[]{:S(2)}) collective-permute-start(bf16[4,48,16,128]{3,2,1,0:T(8,128)(2,1)} %pad_maximum_fusion.1.rest_0_), channel_id=1, source_target_pairs={{0,2},{1,5},{2,0},{3,7},{4,6},{5,1},{6,4},{7,3},{8,10},{9,13},{10,... | collective-permute-start | bytes 2359304 | tf_op jit(solution)/shard_map/ppermute | solution.py:699
  81.0 21.2 %collective-permute-start.26 = (bf16[4,48,16,128]{3,2,1,0:T(8,128)(2,1)}, bf16[4,48,16,128]{3,2,1,0:T(8,128)(2,1)}, u32[]{:S(2)}, u32[]{:S(2)}) collective-permute-start(bf16[4,48,16,128]{3,2,1,0:T(8,128)(2,1)} %pad_maximum_fusion.1.rest_0_), channel_id=1, source_target_pairs={{0,4},{1,3},{2,6},{3,1},{4,0},{5,7},{6,2},{7,5},{8,12},{9,11},{10,... | collective-permute-start | bytes 2359304 | tf_op jit(solution)/shard_map/ppermute | solution.py:699
  98.6 15.1 %collective-permute-start.23 = (bf16[4,48,16,128]{3,2,1,0:T(8,128)(2,1)}, bf16[4,48,16,128]{3,2,1,0:T(8,128)(2,1)S(1)}, u32[]{:S(2)}, u32[]{:S(2)}) collective-permute-start(bf16[4,48,16,128]{3,2,1,0:T(8,128)(2,1)} %collective-permute-done.22.rest_1_), channel_id=1, source_target_pairs={{0,4},{1,3},{2,6},{3,1},{4,0},{5,7},{6,2},{7,5},{8,12},{9,11},{10,... | collective-permute-start | bytes 2359304 | tf_op jit(solution)/shard_map/ppermute | solution.py:699
  101.6 12.0 %collective-permute-start.24 = (bf16[4,48,16,128]{3,2,1,0:T(8,128)(2,1)}, bf16[4,48,16,128]{3,2,1,0:T(8,128)(2,1)S(1)}, u32[]{:S(2)}, u32[]{:S(2)}) collective-permute-start(bf16[4,48,16,128]{3,2,1,0:T(8,128)(2,1)} %pad_maximum_fusion.1.rest_0_), channel_id=1, source_target_pairs={{0,1},{1,0},{2,3},{3,2},{4,5},{5,4},{6,7},{7,6},{8,9},{9,8},{10,11... | collective-permute-start | bytes 2359304 | tf_op jit(solution)/shard_map/ppermute | solution.py:699
  101.7 12.0 %collective-permute-start.25 = (bf16[4,48,16,128]{3,2,1,0:T(8,128)(2,1)}, bf16[4,48,16,128]{3,2,1,0:T(8,128)(2,1)S(1)}, u32[]{:S(2)}, u32[]{:S(2)}) collective-permute-start(bf16[4,48,16,128]{3,2,1,0:T(8,128)(2,1)} %collective-permute-done.22.rest_1_), channel_id=1, source_target_pairs={{0,1},{1,0},{2,3},{3,2},{4,5},{5,4},{6,7},{7,6},{8,9},{9,8},{10,11... | collective-permute-start | bytes 2359304 | tf_op jit(solution)/shard_map/ppermute | solution.py:699
  102.2 11.6 %collective-permute-start.27 = (bf16[4,48,16,128]{3,2,1,0:T(8,128)(2,1)}, bf16[4,48,16,128]{3,2,1,0:T(8,128)(2,1)S(1)}, u32[]{:S(2)}, u32[]{:S(2)}) collective-permute-start(bf16[4,48,16,128]{3,2,1,0:T(8,128)(2,1)} %collective-permute-done.26.rest_2_), channel_id=1, source_target_pairs={{0,1},{1,0},{2,3},{3,2},{4,5},{5,4},{6,7},{7,6},{8,9},{9,8},{10,11... | collective-permute-start | bytes 2359304 | tf_op jit(solution)/shard_map/ppermute | solution.py:699
  113.7 26.2 %collective-permute-start.36 = (bf16[4,48,16,128]{3,2,1,0:T(8,128)(2,1)S(1)}, bf16[4,48,16,128]{3,2,1,0:T(8,128)(2,1)S(1)}, u32[]{:S(2)}, u32[]{:S(2)}) collective-permute-start(bf16[4,48,16,128]{3,2,1,0:T(8,128)(2,1)S(1)} %collective-permute-done.23.rest_3_), channel_id=1, source_target_pairs={{0,1},{1,0},{2,3},{3,2},{4,5},{5,4},{6,7},{7,6},{8,9},{9,8},{10,11... | collective-permute-start | bytes 2359304 | tf_op jit(solution)/shard_map/ppermute | solution.py:699
  164.7 14.9 %collective-permute-start.37 = (bf16[64,512]{1,0:T(8,128)(2,1)}, bf16[64,512]{1,0:T(8,128)(2,1)S(1)}, u32[]{:S(2)}, u32[]{:S(2)}) collective-permute-start(bf16[64,512]{1,0:T(8,128)(2,1)} %get-tuple-element.149), channel_id=1, source_target_pairs={{1,0},{2,1},{3,2},{4,3},{5,4},{6,5},{7,6},{8,7},{9,8},{10,9},{11,1... | collective-permute-start | bytes 196616 | tf_op jit(solution)/shard_map/ppermute | solution.py:624
  204.1 21.6 %collective-permute-start.48 = (bf16[2,4,48,16,128]{4,3,2,1,0:T(8,128)(2,1)S(1)}, bf16[2,4,48,16,128]{4,3,2,1,0:T(8,128)(2,1)S(1)}, u32[]{:S(2)}, u32[]{:S(2)}) collective-permute-start(bf16[2,4,48,16,128]{4,3,2,1,0:T(8,128)(2,1)S(1)} %get-tuple-element.226), channel_id=1, source_target_pairs={{0,4},{1,3},{2,6},{3,1},{4,0},{5,7},{6,2},{7,5},{8,12},{9,11},{10,... | collective-permute-start | bytes 4718600 | tf_op jit(solution)/shard_map/ppermute | solution.py:699
  226.4 12.1 %collective-permute-start.49 = (bf16[4,48,16,128]{3,2,1,0:T(8,128)(2,1)S(1)}, bf16[4,48,16,128]{3,2,1,0:T(8,128)(2,1)S(1)}, u32[]{:S(2)}, u32[]{:S(2)}) collective-permute-start(bf16[4,48,16,128]{3,2,1,0:T(8,128)(2,1)S(1)} %get-tuple-element.228), channel_id=1, source_target_pairs={{0,2},{1,5},{2,0},{3,7},{4,6},{5,1},{6,4},{7,3},{8,10},{9,13},{10,... | collective-permute-start | bytes 2359304 | tf_op jit(solution)/shard_map/ppermute | solution.py:699
  253.4 20.8 %collective-permute-start.52 = (bf16[2,4,49,16,128]{4,3,2,1,0:T(8,128)(2,1)S(1)}, bf16[2,4,49,16,128]{4,3,2,1,0:T(8,128)(2,1)S(1)}, u32[]{:S(2)}, u32[]{:S(2)}) collective-permute-start(bf16[2,4,49,16,128]{4,3,2,1,0:T(8,128)(2,1)S(1)} %slice_bitcast_fusion), channel_id=1, source_target_pairs={{0,4},{1,3},{2,6},{3,1},{4,0},{5,7},{6,2},{7,5},{8,12},{9,11},{10,... | collective-permute-start | bytes 4816904 | tf_op jit(solution)/shard_map/ppermute | solution.py:699
  255.6 23.1 %collective-permute-start.55 = (bf16[48,16,128]{2,1,0:T(8,128)(2,1)}, bf16[48,16,128]{2,1,0:T(8,128)(2,1)S(1)}, u32[]{:S(2)}, u32[]{:S(2)}) collective-permute-start(bf16[48,16,128]{2,1,0:T(8,128)(2,1)} %get-tuple-element.237), channel_id=1, source_target_pairs={{0,24},{1,25},{2,26},{3,27},{4,28},{5,29},{6,30},{7,31},{8,0},{9,1... | collective-permute-start | bytes 589832 | tf_op jit(solution)/shard_map/ppermute | solution.py:699
  256.9 21.8 %collective-permute-start.54 = (bf16[48,16,128]{2,1,0:T(8,128)(2,1)S(1)}, bf16[48,16,128]{2,1,0:T(8,128)(2,1)S(1)}, u32[]{:S(2)}, u32[]{:S(2)}) collective-permute-start(bf16[48,16,128]{2,1,0:T(8,128)(2,1)S(1)} %get-tuple-element.238), channel_id=1, source_target_pairs={{0,16},{1,17},{2,18},{3,19},{4,20},{5,21},{6,22},{7,23},{8,24},{9,... | collective-permute-start | bytes 589832 | tf_op jit(solution)/shard_map/ppermute | solution.py:699
  263.5 16.3 %collective-permute-start.53 = (bf16[48,16,128]{2,1,0:T(8,128)(2,1)S(1)}, bf16[48,16,128]{2,1,0:T(8,128)(2,1)}, u32[]{:S(2)}, u32[]{:S(2)}) collective-permute-start(bf16[48,16,128]{2,1,0:T(8,128)(2,1)S(1)} %get-tuple-element.239), channel_id=1, source_target_pairs={{0,8},{1,9},{2,10},{3,11},{4,12},{5,13},{6,14},{7,15},{8,16},{9,17... | collective-permute-start | bytes 589832 | tf_op jit(solution)/shard_map/ppermute | solution.py:699
  274.8 16.3 %collective-permute-start.58 = (bf16[4,49,16,128]{3,2,1,0:T(8,128)(2,1)S(1)}, bf16[4,49,16,128]{3,2,1,0:T(8,128)(2,1)}, u32[]{:S(2)}, u32[]{:S(2)}) collective-permute-start(bf16[4,49,16,128]{3,2,1,0:T(8,128)(2,1)S(1)} %slice_bitcast_fusion.4), channel_id=1, source_target_pairs={{0,2},{1,5},{2,0},{3,7},{4,6},{5,1},{6,4},{7,3},{8,10},{9,13},{10,... | collective-permute-start | bytes 2408456 | tf_op jit(solution)/shard_map/ppermute | solution.py:699
  293.3 28.2 %collective-permute-start.65 = (bf16[49,16,128]{2,1,0:T(8,128)(2,1)}, bf16[49,16,128]{2,1,0:T(8,128)(2,1)S(1)}, u32[]{:S(2)}, u32[]{:S(2)}) collective-permute-start(bf16[49,16,128]{2,1,0:T(8,128)(2,1)} %get-tuple-element.230), channel_id=1, source_target_pairs={{0,24},{1,25},{2,26},{3,27},{4,28},{5,29},{6,30},{7,31},{8,0},{9,1... | collective-permute-start | bytes 602120 | tf_op jit(solution)/shard_map/ppermute | solution.py:699
  298.3 23.2 %collective-permute-start.64 = (bf16[49,16,128]{2,1,0:T(8,128)(2,1)S(1)}, bf16[49,16,128]{2,1,0:T(8,128)(2,1)S(1)}, u32[]{:S(2)}, u32[]{:S(2)}) collective-permute-start(bf16[49,16,128]{2,1,0:T(8,128)(2,1)S(1)} %get-tuple-element.231), channel_id=1, source_target_pairs={{0,16},{1,17},{2,18},{3,19},{4,20},{5,21},{6,22},{7,23},{8,24},{9,... | collective-permute-start | bytes 602120 | tf_op jit(solution)/shard_map/ppermute | solution.py:699
  298.3 23.2 %collective-permute-start.63 = (bf16[49,16,128]{2,1,0:T(8,128)(2,1)S(1)}, bf16[49,16,128]{2,1,0:T(8,128)(2,1)S(1)}, u32[]{:S(2)}, u32[]{:S(2)}) collective-permute-start(bf16[49,16,128]{2,1,0:T(8,128)(2,1)S(1)} %get-tuple-element.229), channel_id=1, source_target_pairs={{0,8},{1,9},{2,10},{3,11},{4,12},{5,13},{6,14},{7,15},{8,16},{9,17... | collective-permute-start | bytes 602120 | tf_op jit(solution)/shard_map/ppermute | solution.py:699
  321.7 14.4 %collective-permute-start.66 = (f32[1024]{0:T(1024)S(1)}, f32[1024]{0:T(1024)S(1)}, u32[]{:S(2)}, u32[]{:S(2)}) collective-permute-start(f32[1024]{0:T(1024)S(1)} %fusion.12), channel_id=1, source_target_pairs={{1,0},{2,1},{3,2},{4,3},{5,4},{6,5},{7,6},{8,7},{9,8},{10,9},{11,1... | collective-permute-start | bytes 12296 | tf_op jit(solution)/shard_map/ppermute | solution.py:624
  (68 other events, 793.2 us)

commit v5 on v4

--- a/solution.py
+++ b/solution.py
@@ -15,7 +15,7 @@
 RIGHT = 4
 MEM = 4
 STEP = 10
-UN = 4
+UN = 8
 NEG = -1e30
 
 TOK = 512
@@ -209,7 +209,7 @@
         return carry
 
     lax.fori_loop(0, NBLK, scores, 0, unroll=UN)
-    lax.fori_loop(0, 4 * NBLK, softmax, 0, unroll=4)
+    lax.fori_loop(0, 4 * NBLK, softmax, 0, unroll=8)
     lax.fori_loop(0, NBLK, mix, 0, unroll=UN)
 
 
@@ -249,7 +249,7 @@
         return carry
 
     lax.fori_loop(0, NBLK, weights, 0, unroll=UN)
-    lax.fori_loop(0, 4 * NBLK, softmax, 0, unroll=4)
+    lax.fori_loop(0, 4 * NBLK, softmax, 0, unroll=8)
     lax.fori_loop(0, NBLK, queries, 0, unroll=UN)
 
 
@@ -564,7 +564,7 @@
             put(mm_tn(act_ref[:, pl.ds(c0, 256)], dxb_ref[...]), WD0, 4, 16 * c, 0)
             return carry
 
-        lax.fori_loop(0, FF // 256, down, 0, unroll=4)
+        lax.fori_loop(0, FF // 256, down, 0, unroll=8)
         send(64, 96)
     if part == 1:
         loads[5].wait()
@@ -575,7 +575,7 @@
             put(mm_tn(h2_ref[...], dub_ref[:, pl.ds(c0, 256)]), WU0, 16, 0, 2 * c)
             return carry
 
-        lax.fori_loop(0, FF // 256, up, 0, unroll=4)
+        lax.fori_loop(0, FF // 256, up, 0, unroll=8)
         send(32, 64)
     if part == 2:
         for i in (3, 4, 0, 1, 2):

time: 348 us -> 347 us (level)
  transfers between devices with their start and end apart: 67 -> 67, of which waited for: 21 -> 21; matrix products, arithmetic and copies ran while one was open for 7% -> 7% of each run, Pallas kernels for 18% -> 17%
where the time goes in v5:
time: 347 us; the launch traced here: 340 us
  starting transfers between devices  115 us (33%)
  Pallas kernels  94.9 us (27%)
  waiting for transfers between devices  87.3 us (25%)
  other arithmetic  26.4 us (8%)
  local copies, waits for them, and re-layouts  14.6 us (4%)
    pallas_call x13, Pallas kernels, run(): pl.pallas_call(kernel, out_shape=outs, input_output_aliases=aliases or {}...  94.9 us
    ppermute x32, waiting for transfers between devices, move(): return lax.ppermute(value, 'ta', links(32, kind, by))  54.2 us
    ppermute x15, starting transfers between devices, shift(): lax.ppermute(value, 'ta', [(i, i + by) for i in range(n) if 0 <= i + by <...  47 us
    ppermute x32, starting transfers between devices, move(): return lax.ppermute(value, 'ta', links(32, kind, by))  40.3 us
    ppermute x10, waiting for transfers between devices, spread_round(): lax.ppermute(value, 'ta', [(i, i + j * stride) for i in keep])  21.1 us
    ppermute x10, starting transfers between devices, collect_round(): lax.ppermute(value, 'ta', [(i + j * stride, i) for i in keep])  16.9 us
    ppermute x10, starting transfers between devices, spread_round(): lax.ppermute(value, 'ta', [(i, i + j * stride) for i in keep])  10.6 us
    ppermute x15, waiting for transfers between devices, shift(): lax.ppermute(value, 'ta', [(i, i + by) for i in range(n) if 0 <= i + by <...  10.2 us
  transfers between devices with their start and end apart: 67, of which 21 were waited for; matrix products, arithmetic and copies ran while one was open for 7% of the time, Pallas kernels for 17%

profile of v5, /device:TPU:20, one launch (start us, length us, event | category | flops | bytes accessed | tf_op | source)
XLA Modules:
  0.0 340.3 jit_solution(14720306148074160314)
XLA Ops:
  9.3 4.5 %collective-permute-start.2 = (bf16[16,512]{1,0:T(8,128)(2,1)}, bf16[16,512]{1,0:T(8,128)(2,1)S(1)}, u32[]{:S(2)}, u32[]{:S(2)}) collective-permute-start(bf16[16,512]{1,0:T(8,128)(2,1)} %get-tuple-element.118), channel_id=1, source_target_pairs={{1,0},{2,1},{3,2},{4,3},{5,4},{6,5},{7,6},{8,7},{9,8},{10,9},{11,1... | collective-permute-start | bytes 49160 | tf_op jit(solution)/shard_map/ppermute | solution.py:624
  22.3 3.5 %collective-permute-start.10 = (bf16[49,16,128]{2,1,0:T(8,128)(2,1)S(1)}, bf16[49,16,128]{2,1,0:T(8,128)(2,1)S(1)}, u32[]{:S(2)}, u32[]{:S(2)}) collective-permute-start(bf16[49,16,128]{2,1,0:T(8,128)(2,1)S(1)} %pad_maximum_fusion.2), channel_id=1, source_target_pairs={{0,16},{1,17},{2,18},{3,19},{4,20},{5,21},{6,22},{7,23},{8,24},{9,... | collective-permute-start | bytes 602120 | tf_op jit(solution)/shard_map/ppermute | solution.py:699
  27.1 10.3 %collective-permute-done.5 = bf16[32,512]{1,0:T(8,128)(2,1)S(1)} collective-permute-done((bf16[32,512]{1,0:T(8,128)(2,1)S(1)}, bf16[32,512]{1,0:T(8,128)(2,1)S(1)}, u32[]{:S(2)}, u32[]{:S(2)}) %collective-permute-start.5) | collective-permute-done | bytes 32800 | tf_op jit(solution)/shard_map/ppermute | solution.py:634
  49.9 11.4 %collective-permute-done.16 = bf16[48,16,128]{2,1,0:T(8,128)(2,1)S(1)} collective-permute-done((bf16[48,16,128]{2,1,0:T(8,128)(2,1)S(1)}, bf16[48,16,128]{2,1,0:T(8,128)(2,1)S(1)}, u32[]{:S(2)}, u32[]{:S(2)}) %collective-permute-start.16) | collective-permute-done | bytes 196640 | tf_op jit(solution)/shard_map/ppermute | solution.py:699
  61.3 3.4 %collective-permute-done.15 = bf16[48,16,128]{2,1,0:T(8,128)(2,1)S(1)} collective-permute-done((bf16[48,16,128]{2,1,0:T(8,128)(2,1)S(1)}, bf16[48,16,128]{2,1,0:T(8,128)(2,1)S(1)}, u32[]{:S(2)}, u32[]{:S(2)}) %collective-permute-start.15) | collective-permute-done | bytes 196640 | tf_op jit(solution)/shard_map/ppermute | solution.py:699
  69.6 10.0 %collective-permute-done.17.rest_3_ = bf16[4,49,16,128]{3,2,1,0:T(8,128)(2,1)S(1)} collective-permute-done((bf16[4,49,16,128]{3,2,1,0:T(8,128)(2,1)S(1)}, bf16[4,49,16,128]{3,2,1,0:T(8,128)(2,1)S(1)}, u32[]{:S(2)}, u32[]{:S(2)}) %collective-permute-start.17) | collective-permute-done | bytes 802848 | tf_op jit(solution)/shard_map/ppermute | solution.py:699
  84.6 7.4 %shard_map.127 = (bf16[16,128]{1,0:T(8,128)(2,1)}, bf16[704,512]{1,0:T(8,128)(2,1)}, bf16[512,512]{1,0:T(8,128)(2,1)}, bf16[704,1024]{1,0:T(8,128)(2,1)}, bf16[3...) custom-call(s32[1]{0:T(128)} %bitcast.me_ref, bf16[512,512]{1,0:T(8,128)(2,1)} %x_ref.7, bf16[64,512]{1,0:T(8,128)(2,1)} %copy-done.26, ...), custom_call_target="tpu_custom_call" | custom-call | flops 3000000000 | bytes 10000000 | tf_op jit(solution)/shard_map/pallas_call | solution.py:611
  92.0 6.5 %collective-permute-done.22.rest_1_ = bf16[4,48,16,128]{3,2,1,0:T(8,128)(2,1)} collective-permute-done((bf16[4,48,16,128]{3,2,1,0:T(8,128)(2,1)}, bf16[4,48,16,128]{3,2,1,0:T(8,128)(2,1)}, u32[]{:S(2)}, u32[]{:S(2)}) %collective-permute-start.22) | collective-permute-done | bytes 786464 | tf_op jit(solution)/shard_map/ppermute | solution.py:699
  102.2 11.5 %shard_map.128 = (f32[512,512]{1,0:T(8,128)}, bf16[512,512]{1,0:T(8,128)(2,1)}, bf16[64,512]{1,0:T(8,128)(2,1)}, bf16[16,512]{1,0:T(8,128)(2,1)}, bf16[32,512]{1...) custom-call(s32[1]{0:T(128)} %bitcast.me_ref, ...), custom_call_target="tpu_custom_call" | custom-call | flops 3000000000 | bytes 10000000 | tf_op jit(solution)/shard_map/pallas_call | solution.py:611
  120.9 4.3 %collective-permute-start.29 = (bf16[16,512]{1,0:T(8,128)(2,1)}, bf16[16,512]{1,0:T(8,128)(2,1)S(1)}, u32[]{:S(2)}, u32[]{:S(2)}) collective-permute-start(bf16[16,512]{1,0:T(8,128)(2,1)} %get-tuple-element.143), channel_id=1, source_target_pairs={{1,0},{2,1},{3,2},{4,3},{5,4},{6,5},{7,6},{8,7},{9,8},{10,9},{11,1... | collective-permute-start | bytes 49160 | tf_op jit(solution)/shard_map/ppermute | solution.py:624
  128.1 6.1 %collective-permute-done.33 = bf16[32,512]{1,0:T(8,128)(2,1)S(1)} collective-permute-done((bf16[32,512]{1,0:T(8,128)(2,1)S(1)}, bf16[32,512]{1,0:T(8,128)(2,1)S(1)}, u32[]{:S(2)}, u32[]{:S(2)}) %collective-permute-start.33) | collective-permute-done | bytes 32800 | tf_op jit(solution)/shard_map/ppermute | solution.py:634
  140.8 21.4 %shard_map.129 = (f32[512,512]{1,0:T(8,128)}, f32[512,512]{1,0:T(8,128)}, f32[512,512]{1,0:T(8,128)}, bf16[64,512]{1,0:T(8,128)(2,1)}, bf16[16,512]{1,0:T(8,128)...) custom-call(s32[1]{0:T(128)} %bitcast.me_ref, ...), custom_call_target="tpu_custom_call" | custom-call | flops 8000000000 | bytes 10000000 | tf_op jit(solution)/shard_map/pallas_call | solution.py:611
  163.5 4.1 %collective-permute-start.37 = (bf16[64,512]{1,0:T(8,128)(2,1)}, bf16[64,512]{1,0:T(8,128)(2,1)S(1)}, u32[]{:S(2)}, u32[]{:S(2)}) collective-permute-start(bf16[64,512]{1,0:T(8,128)(2,1)} %get-tuple-element.149), channel_id=1, source_target_pairs={{1,0},{2,1},{3,2},{4,3},{5,4},{6,5},{7,6},{8,7},{9,8},{10,9},{11,1... | collective-permute-start | bytes 196616 | tf_op jit(solution)/shard_map/ppermute | solution.py:624
  174.4 4.0 %collective-permute-done.38.har_ref = bf16[16,512]{1,0:T(8,128)(2,1)S(1)} collective-permute-done((bf16[16,512]{1,0:T(8,128)(2,1)}, bf16[16,512]{1,0:T(8,128)(2,1)S(1)}, u32[]{:S(2)}, u32[]{:S(2)}) %collective-permute-start.38) | collective-permute-done | bytes 16416 | tf_op jit(solution)/shard_map/ppermute | solution.py:624
  178.5 4.4 %shard_map.130 = (bf16[2,2,4,48,16,128]{5,4,3,2,1,0:T(8,128)(2,1)}, bf16[2,2,4,48,16,128]{5,4,3,2,1,0:T(8,128)(2,1)}) custom-call(s32[1]{0:T(128)} %bitcast.me_ref, bf16[704,512]{1,0:T(8,128)(2,1)} %get-tuple-element.152.rest_0_, bf16[512,512]{1,0:T(8,128)(2,1)} %get-tuple-element.153.rest_1_, bf16[704,1024]{1,0:T(8,128)(2,1)} %get-tuple-element.154.rest_2_, ...), custom_call_target="tpu_custom_call" | custom-call | flops 1000000000 | bytes 10000000 | tf_op jit(solution)/shard_map/pallas_call | solution.py:611
  183.6 4.5 %shard_map.131 = (bf16[2,2,4,48,16,128]{5,4,3,2,1,0:T(8,128)(2,1)}, bf16[2,2,4,48,16,128]{5,4,3,2,1,0:T(8,128)(2,1)}) custom-call(s32[1]{0:T(128)} %bitcast.me_ref, bf16[704,512]{1,0:T(8,128)(2,1)} %get-tuple-element.152.rest_0_, bf16[512,512]{1,0:T(8,128)(2,1)} %get-tuple-element.153.rest_1_, ...), custom_call_target="tpu_custom_call", output_to_operand_aliasing={{0}: (10, {}), {1}: (11, {})} | custom-call | flops 1000000000 | bytes 10000000 | tf_op jit(solution)/shard_map/pallas_call | solution.py:611
  188.1 5.0 %shard_map.132 = (bf16[2,2,4,48,16,128]{5,4,3,2,1,0:T(8,128)(2,1)}, bf16[2,2,4,48,16,128]{5,4,3,2,1,0:T(8,128)(2,1)}) custom-call(s32[1]{0:T(128)} %bitcast.me_ref, bf16[704,512]{1,0:T(8,128)(2,1)} %get-tuple-element.152.rest_0_, bf16[512,512]{1,0:T(8,128)(2,1)} %get-tuple-element.153.rest_1_, ...), custom_call_target="tpu_custom_call", output_to_operand_aliasing={{0}: (10, {}), {1}: (11, {})} | custom-call | flops 1000000000 | bytes 10000000 | tf_op jit(solution)/shard_map/pallas_call | solution.py:611
  195.1 3.8 %collective-permute-done.45 = bf16[2,2,4,48,16,128]{5,4,3,2,1,0:T(8,128)(2,1)S(1)} collective-permute-done((bf16[2,2,4,48,16,128]{5,4,3,2,1,0:T(8,128)(2,1)}, bf16[2,2,4,48,16,128]{5,4,3,2,1,0:T(8,128)(2,1)S(1)}, u32[]{:S(2)}, u32[]{:S(2)}) %collective-permute-start.45) | collective-permute-done | bytes 3145760 | tf_op jit(solution)/shard_map/ppermute | solution.py:699
  203.1 10.4 %shard_map.133 = (f32[1,512]{1,0:T(1,128)}, f32[512,512]{1,0:T(8,128)}, f32[1,512]{1,0:T(1,128)}, bf16[512,512]{1,0:T(8,128)(2,1)}, bf16[512,2048]{1,0:T(8,128)(2,1)}, /*index=5*/bf16[512,512]{1,0:T(8,128)(2,1)}) custom-call(s32[1]{0:T(128)} %bitcast.me_ref, bf16[64,512]{1,0:T(8,128)(2,1)} %copy-done.9, bf16[16,512]{1,0:T(8,128)(2,1)} %copy-done.15, ...), custom_call_target="tpu_custom_call" | custom-call | flops 3000000000 | bytes 10000000 | tf_op jit(solution)/shard_map/pallas_call | solution.py:611
  213.5 10.2 %shard_map.134 = (f32[1,512]{1,0:T(1,128)}, f32[512,512]{1,0:T(8,128)}, f32[64,512]{1,0:T(8,128)}, f32[16,512]{1,0:T(8,128)}, f32[32,512]{1,0:T(8,128)}, /*index...) custom-call(s32[1]{0:T(128)} %bitcast.me_ref, ...), custom_call_target="tpu_custom_call" | custom-call | flops 3000000000 | bytes 10000000 | tf_op jit(solution)/shard_map/pallas_call | solution.py:611
  225.7 4.4 %shard_map.135 = (bf16[2,2,4,49,16,128]{5,4,3,2,1,0:T(8,128)(2,1)}, bf16[2,2,4,49,16,128]{5,4,3,2,1,0:T(8,128)(2,1)}) custom-call(s32[1]{0:T(128)} %bitcast.me_ref, bf16[704,512]{1,0:T(8,128)(2,1)} %get-tuple-element.189.rest_0_, bf16[512,512]{1,0:T(8,128)(2,1)} %get-tuple-element.190.rest_1_, bf16[704,1024]{1,0:T(8,128)(2,1)} %get-tuple-element.191.rest_2_, ...), custom_call_target="tpu_custom_call" | custom-call | flops 1000000000 | bytes 10000000 | tf_op jit(solution)/shard_map/pallas_call | solution.py:611
  230.1 4.5 %shard_map.136 = (bf16[2,2,4,49,16,128]{5,4,3,2,1,0:T(8,128)(2,1)}, bf16[2,2,4,49,16,128]{5,4,3,2,1,0:T(8,128)(2,1)}) custom-call(s32[1]{0:T(128)} %bitcast.me_ref, bf16[704,512]{1,0:T(8,128)(2,1)} %get-tuple-element.189.rest_0_, bf16[512,512]{1,0:T(8,128)(2,1)} %get-tuple-element.190.rest_1_, ...), custom_call_target="tpu_custom_call", output_to_operand_aliasing={{0}: (10, {}), {1}: (11, {})} | custom-call | flops 1000000000 | bytes 10000000 | tf_op jit(solution)/shard_map/pallas_call | solution.py:611
  236.7 5.6 %shard_map.137 = (bf16[2,2,4,49,16,128]{5,4,3,2,1,0:T(8,128)(2,1)}, bf16[2,2,4,49,16,128]{5,4,3,2,1,0:T(8,128)(2,1)}) custom-call(s32[1]{0:T(128)} %bitcast.me_ref, bf16[704,512]{1,0:T(8,128)(2,1)} %get-tuple-element.189.rest_0_, bf16[512,512]{1,0:T(8,128)(2,1)} %get-tuple-element.190.rest_1_, ...), custom_call_target="tpu_custom_call", output_to_operand_aliasing={{0}: (11, {}), {1}: (12, {})} | custom-call | flops 1000000000 | bytes 10000000 | tf_op jit(solution)/shard_map/pallas_call | solution.py:611
  242.4 6.0 %collective-permute-done.50 = bf16[2,2,4,49,16,128]{5,4,3,2,1,0:T(8,128)(2,1)S(1)} collective-permute-done((bf16[2,2,4,49,16,128]{5,4,3,2,1,0:T(8,128)(2,1)}, bf16[2,2,4,49,16,128]{5,4,3,2,1,0:T(8,128)(2,1)S(1)}, u32[]{:S(2)}, u32[]{:S(2)}) %collective-permute-start.50) | collective-permute-done | bytes 3211296 | tf_op jit(solution)/shard_map/ppermute | solution.py:699
  254.8 7.5 %collective-permute-start.54 = (bf16[48,16,128]{2,1,0:T(8,128)(2,1)S(1)}, bf16[48,16,128]{2,1,0:T(8,128)(2,1)S(1)}, u32[]{:S(2)}, u32[]{:S(2)}) collective-permute-start(bf16[48,16,128]{2,1,0:T(8,128)(2,1)S(1)} %get-tuple-element.238), channel_id=1, source_target_pairs={{0,16},{1,17},{2,18},{3,19},{4,20},{5,21},{6,22},{7,23},{8,24},{9,... | collective-permute-start | bytes 589832 | tf_op jit(solution)/shard_map/ppermute | solution.py:699
  264.4 7.8 %collective-permute-done.52 = bf16[2,4,49,16,128]{4,3,2,1,0:T(8,128)(2,1)S(1)} collective-permute-done((bf16[2,4,49,16,128]{4,3,2,1,0:T(8,128)(2,1)S(1)}, bf16[2,4,49,16,128]{4,3,2,1,0:T(8,128)(2,1)S(1)}, u32[]{:S(2)}, u32[]{:S(2)}) %collective-permute-start.52) | collective-permute-done | bytes 1605664 | tf_op jit(solution)/shard_map/ppermute | solution.py:699
  279.3 7.8 %collective-permute-start.56 = (f32[32,512]{1,0:T(8,128)S(1)}, f32[32,512]{1,0:T(8,128)S(1)}, u32[]{:S(2)}, u32[]{:S(2)}) collective-permute-start(f32[32,512]{1,0:T(8,128)S(1)} %add.194), channel_id=1, source_target_pairs={{16,0},{18,2},{20,4},{22,6},{24,8},{26,10},{28,12},{30,14}} | collective-permute-start | bytes 196616 | tf_op jit(solution)/shard_map/ppermute | solution.py:641
  291.9 5.0 %collective-permute-start.65 = (bf16[49,16,128]{2,1,0:T(8,128)(2,1)}, bf16[49,16,128]{2,1,0:T(8,128)(2,1)S(1)}, u32[]{:S(2)}, u32[]{:S(2)}) collective-permute-start(bf16[49,16,128]{2,1,0:T(8,128)(2,1)} %get-tuple-element.230), channel_id=1, source_target_pairs={{0,24},{1,25},{2,26},{3,27},{4,28},{5,29},{6,30},{7,31},{8,0},{9,1... | collective-permute-start | bytes 602120 | tf_op jit(solution)/shard_map/ppermute | solution.py:699
  307.1 4.6 %collective-permute-start.62 = (f32[32,512]{1,0:T(8,128)}, f32[32,512]{1,0:T(8,128)S(1)}, u32[]{:S(2)}, u32[]{:S(2)}) collective-permute-start(f32[32,512]{1,0:T(8,128)} %get-tuple-element.216), channel_id=1, source_target_pairs={{2,0},{3,1},{4,2},{5,3},{6,4},{7,5},{8,6},{9,7},{10,8},{11,9},{12,... | collective-permute-start | bytes 196616 | tf_op jit(solution)/shard_map/ppermute | solution.py:624
  316.7 3.5 %shard_map.138 = f32[512,512]{1,0:T(8,128)} custom-call(s32[1]{0:T(128)} %bitcast.me_ref, f32[64,512]{1,0:T(8,128)} %collective-permute-done.46.hal_ref, f32[16,512]{1,0:T(8,128)} %copy-done.13, f32[32,512]{1,0:T(8,128)} %add.203.root_ref, f32[32,512]{1,0:T(8,128)} %copy-done.10, f32[32,512]{1,0:T(8,128)} %get-tuple-element.217.dtab_ref, ...), custom_call_target="tpu_custom_call" | custom-call | flops 10000000 | bytes 10000000 | tf_op jit(solution)/shard_map/pallas_call | solution.py:611
  320.5 9.7 %collective-permute-start.66 = (f32[1024]{0:T(1024)S(1)}, f32[1024]{0:T(1024)S(1)}, u32[]{:S(2)}, u32[]{:S(2)}) collective-permute-start(f32[1024]{0:T(1024)S(1)} %fusion.12), channel_id=1, source_target_pairs={{1,0},{2,1},{3,2},{4,3},{5,4},{6,5},{7,6},{8,7},{9,8},{10,9},{11,1... | collective-permute-start | bytes 12296 | tf_op jit(solution)/shard_map/ppermute | solution.py:624
  334.8 5.3 %multiply_add_fusion.1 = (f32[2,98336]{1,0:T(2,128)}, f32[2,98336]{1,0:T(2,128)}, f32[2,98336]{1,0:T(2,128)}, f32[2,98336]{1,0:T(2,128)}) fusion(f32[2,98336]{1,0:T(2,128)S(1)} %copy-done.6, f32[2,98336]{1,0:T(2,128)S(1)} %copy-done.1, f32[2,98336]{1,0:T(2,128)S(1)} %copy-done.7, f32[2,98336]{1,0:T(2,128)S(1)} %copy-done.8, s32[]{:T(128)S(6)} %select_n.105, ...), kind=kLoop, calls=%fused_computation.25 | loop fusion | flops 3736768 | bytes 7088132 | tf_op jit(solution)/shard_map/add | solution.py:964
  (270 shorter events, 119.6 us)
Async XLA Ops:
  7.2 14.6 %collective-permute-start.1 = (bf16[64,512]{1,0:T(8,128)(2,1)}, bf16[64,512]{1,0:T(8,128)(2,1)S(1)}, u32[]{:S(2)}, u32[]{:S(2)}) collective-permute-start(bf16[64,512]{1,0:T(8,128)(2,1)} %get-tuple-element.117), channel_id=1, source_target_pairs={{0,1},{1,2},{2,3},{3,4},{4,5},{5,6},{6,7},{7,8},{8,9},{9,10},{10,1... | collective-permute-start | bytes 196616 | tf_op jit(solution)/shard_map/ppermute | solution.py:624
  9.3 12.5 %collective-permute-start.2 = (bf16[16,512]{1,0:T(8,128)(2,1)}, bf16[16,512]{1,0:T(8,128)(2,1)S(1)}, u32[]{:S(2)}, u32[]{:S(2)}) collective-permute-start(bf16[16,512]{1,0:T(8,128)(2,1)} %get-tuple-element.118), channel_id=1, source_target_pairs={{1,0},{2,1},{3,2},{4,3},{5,4},{6,5},{7,6},{8,7},{9,8},{10,9},{11,1... | collective-permute-start | bytes 49160 | tf_op jit(solution)/shard_map/ppermute | solution.py:624
  21.8 21.2 %collective-permute-start.11 = (bf16[49,16,128]{2,1,0:T(8,128)(2,1)S(1)}, bf16[49,16,128]{2,1,0:T(8,128)(2,1)S(1)}, u32[]{:S(2)}, u32[]{:S(2)}) collective-permute-start(bf16[49,16,128]{2,1,0:T(8,128)(2,1)S(1)} %pad_maximum_fusion.2), channel_id=1, source_target_pairs={{0,24},{1,25},{2,26},{3,27},{4,28},{5,29},{6,30},{7,31},{8,0},{9,1... | collective-permute-start | bytes 602120 | tf_op jit(solution)/shard_map/ppermute | solution.py:699
  22.3 20.7 %collective-permute-start.10 = (bf16[49,16,128]{2,1,0:T(8,128)(2,1)S(1)}, bf16[49,16,128]{2,1,0:T(8,128)(2,1)S(1)}, u32[]{:S(2)}, u32[]{:S(2)}) collective-permute-start(bf16[49,16,128]{2,1,0:T(8,128)(2,1)S(1)} %pad_maximum_fusion.2), channel_id=1, source_target_pairs={{0,16},{1,17},{2,18},{3,19},{4,20},{5,21},{6,22},{7,23},{8,24},{9,... | collective-permute-start | bytes 602120 | tf_op jit(solution)/shard_map/ppermute | solution.py:699
  25.8 17.2 %collective-permute-start.9 = (bf16[49,16,128]{2,1,0:T(8,128)(2,1)S(1)}, bf16[49,16,128]{2,1,0:T(8,128)(2,1)S(1)}, u32[]{:S(2)}, u32[]{:S(2)}) collective-permute-start(bf16[49,16,128]{2,1,0:T(8,128)(2,1)S(1)} %pad_maximum_fusion.2), channel_id=1, source_target_pairs={{0,8},{1,9},{2,10},{3,11},{4,12},{5,13},{6,14},{7,15},{8,16},{9,17... | collective-permute-start | bytes 602120 | tf_op jit(solution)/shard_map/ppermute | solution.py:699
  43.2 24.2 %collective-permute-start.12 = (bf16[4,49,16,128]{3,2,1,0:T(8,128)(2,1)S(1)}, bf16[4,49,16,128]{3,2,1,0:T(8,128)(2,1)S(1)}, u32[]{:S(2)}, u32[]{:S(2)}) collective-permute-start(bf16[4,49,16,128]{3,2,1,0:T(8,128)(2,1)S(1)} %pad_maximum_fusion.rest_0_), channel_id=1, source_target_pairs={{0,2},{1,5},{2,0},{3,7},{4,6},{5,1},{6,4},{7,3},{8,10},{9,13},{10,... | collective-permute-start | bytes 2408456 | tf_op jit(solution)/shard_map/ppermute | solution.py:699
  45.6 21.8 %collective-permute-start.13 = (bf16[4,49,16,128]{3,2,1,0:T(8,128)(2,1)S(1)}, bf16[4,49,16,128]{3,2,1,0:T(8,128)(2,1)S(1)}, u32[]{:S(2)}, u32[]{:S(2)}) collective-permute-start(bf16[4,49,16,128]{3,2,1,0:T(8,128)(2,1)S(1)} %pad_maximum_fusion.rest_0_), channel_id=1, source_target_pairs={{0,4},{1,3},{2,6},{3,1},{4,0},{5,7},{6,2},{7,5},{8,12},{9,11},{10,... | collective-permute-start | bytes 2408456 | tf_op jit(solution)/shard_map/ppermute | solution.py:699
  45.6 15.7 %collective-permute-start.16 = (bf16[48,16,128]{2,1,0:T(8,128)(2,1)S(1)}, bf16[48,16,128]{2,1,0:T(8,128)(2,1)S(1)}, u32[]{:S(2)}, u32[]{:S(2)}) collective-permute-start(bf16[48,16,128]{2,1,0:T(8,128)(2,1)S(1)} %bitcast.138), channel_id=1, source_target_pairs={{0,24},{1,25},{2,26},{3,27},{4,28},{5,29},{6,30},{7,31},{8,0},{9,1... | collective-permute-start | bytes 589832 | tf_op jit(solution)/shard_map/ppermute | solution.py:699
  47.6 17.1 %collective-permute-start.15 = (bf16[48,16,128]{2,1,0:T(8,128)(2,1)S(1)}, bf16[48,16,128]{2,1,0:T(8,128)(2,1)S(1)}, u32[]{:S(2)}, u32[]{:S(2)}) collective-permute-start(bf16[48,16,128]{2,1,0:T(8,128)(2,1)S(1)} %bitcast.139), channel_id=1, source_target_pairs={{0,16},{1,17},{2,18},{3,19},{4,20},{5,21},{6,22},{7,23},{8,24},{9,... | collective-permute-start | bytes 589832 | tf_op jit(solution)/shard_map/ppermute | solution.py:699
  49.4 17.0 %collective-permute-start.14 = (bf16[48,16,128]{2,1,0:T(8,128)(2,1)S(1)}, bf16[48,16,128]{2,1,0:T(8,128)(2,1)S(1)}, u32[]{:S(2)}, u32[]{:S(2)}) collective-permute-start(bf16[48,16,128]{2,1,0:T(8,128)(2,1)S(1)} %bitcast.140), channel_id=1, source_target_pairs={{0,8},{1,9},{2,10},{3,11},{4,12},{5,13},{6,14},{7,15},{8,16},{9,17... | collective-permute-start | bytes 589832 | tf_op jit(solution)/shard_map/ppermute | solution.py:699
  67.4 12.2 %collective-permute-start.17 = (bf16[4,49,16,128]{3,2,1,0:T(8,128)(2,1)S(1)}, bf16[4,49,16,128]{3,2,1,0:T(8,128)(2,1)S(1)}, u32[]{:S(2)}, u32[]{:S(2)}) collective-permute-start(bf16[4,49,16,128]{3,2,1,0:T(8,128)(2,1)S(1)} %collective-permute-done.12.rest_1_), channel_id=1, source_target_pairs={{0,4},{1,3},{2,6},{3,1},{4,0},{5,7},{6,2},{7,5},{8,12},{9,11},{10,... | collective-permute-start | bytes 2408456 | tf_op jit(solution)/shard_map/ppermute | solution.py:699
  69.1 14.0 %collective-permute-start.19 = (bf16[4,49,16,128]{3,2,1,0:T(8,128)(2,1)S(1)}, bf16[4,49,16,128]{3,2,1,0:T(8,128)(2,1)}, u32[]{:S(2)}, u32[]{:S(2)}) collective-permute-start(bf16[4,49,16,128]{3,2,1,0:T(8,128)(2,1)S(1)} %collective-permute-done.12.rest_1_), channel_id=1, source_target_pairs={{0,1},{1,0},{2,3},{3,2},{4,5},{5,4},{6,7},{7,6},{8,9},{9,8},{10,11... | collective-permute-start | bytes 2408456 | tf_op jit(solution)/shard_map/ppermute | solution.py:699
  69.6 13.5 %collective-permute-start.20 = (bf16[4,49,16,128]{3,2,1,0:T(8,128)(2,1)S(1)}, bf16[4,49,16,128]{3,2,1,0:T(8,128)(2,1)}, u32[]{:S(2)}, u32[]{:S(2)}) collective-permute-start(bf16[4,49,16,128]{3,2,1,0:T(8,128)(2,1)S(1)} %collective-permute-done.13.rest_2_), channel_id=1, source_target_pairs={{0,1},{1,0},{2,3},{3,2},{4,5},{5,4},{6,7},{7,6},{8,9},{9,8},{10,11... | collective-permute-start | bytes 2408456 | tf_op jit(solution)/shard_map/ppermute | solution.py:699
  79.6 18.9 %collective-permute-start.22 = (bf16[4,48,16,128]{3,2,1,0:T(8,128)(2,1)}, bf16[4,48,16,128]{3,2,1,0:T(8,128)(2,1)}, u32[]{:S(2)}, u32[]{:S(2)}) collective-permute-start(bf16[4,48,16,128]{3,2,1,0:T(8,128)(2,1)} %pad_maximum_fusion.1.rest_0_), channel_id=1, source_target_pairs={{0,2},{1,5},{2,0},{3,7},{4,6},{5,1},{6,4},{7,3},{8,10},{9,13},{10,... | collective-permute-start | bytes 2359304 | tf_op jit(solution)/shard_map/ppermute | solution.py:699
  81.0 21.2 %collective-permute-start.26 = (bf16[4,48,16,128]{3,2,1,0:T(8,128)(2,1)}, bf16[4,48,16,128]{3,2,1,0:T(8,128)(2,1)}, u32[]{:S(2)}, u32[]{:S(2)}) collective-permute-start(bf16[4,48,16,128]{3,2,1,0:T(8,128)(2,1)} %pad_maximum_fusion.1.rest_0_), channel_id=1, source_target_pairs={{0,4},{1,3},{2,6},{3,1},{4,0},{5,7},{6,2},{7,5},{8,12},{9,11},{10,... | collective-permute-start | bytes 2359304 | tf_op jit(solution)/shard_map/ppermute | solution.py:699
  98.6 15.1 %collective-permute-start.23 = (bf16[4,48,16,128]{3,2,1,0:T(8,128)(2,1)}, bf16[4,48,16,128]{3,2,1,0:T(8,128)(2,1)S(1)}, u32[]{:S(2)}, u32[]{:S(2)}) collective-permute-start(bf16[4,48,16,128]{3,2,1,0:T(8,128)(2,1)} %collective-permute-done.22.rest_1_), channel_id=1, source_target_pairs={{0,4},{1,3},{2,6},{3,1},{4,0},{5,7},{6,2},{7,5},{8,12},{9,11},{10,... | collective-permute-start | bytes 2359304 | tf_op jit(solution)/shard_map/ppermute | solution.py:699
  101.6 12.0 %collective-permute-start.24 = (bf16[4,48,16,128]{3,2,1,0:T(8,128)(2,1)}, bf16[4,48,16,128]{3,2,1,0:T(8,128)(2,1)S(1)}, u32[]{:S(2)}, u32[]{:S(2)}) collective-permute-start(bf16[4,48,16,128]{3,2,1,0:T(8,128)(2,1)} %pad_maximum_fusion.1.rest_0_), channel_id=1, source_target_pairs={{0,1},{1,0},{2,3},{3,2},{4,5},{5,4},{6,7},{7,6},{8,9},{9,8},{10,11... | collective-permute-start | bytes 2359304 | tf_op jit(solution)/shard_map/ppermute | solution.py:699
  101.7 12.0 %collective-permute-start.25 = (bf16[4,48,16,128]{3,2,1,0:T(8,128)(2,1)}, bf16[4,48,16,128]{3,2,1,0:T(8,128)(2,1)S(1)}, u32[]{:S(2)}, u32[]{:S(2)}) collective-permute-start(bf16[4,48,16,128]{3,2,1,0:T(8,128)(2,1)} %collective-permute-done.22.rest_1_), channel_id=1, source_target_pairs={{0,1},{1,0},{2,3},{3,2},{4,5},{5,4},{6,7},{7,6},{8,9},{9,8},{10,11... | collective-permute-start | bytes 2359304 | tf_op jit(solution)/shard_map/ppermute | solution.py:699
  102.2 11.6 %collective-permute-start.27 = (bf16[4,48,16,128]{3,2,1,0:T(8,128)(2,1)}, bf16[4,48,16,128]{3,2,1,0:T(8,128)(2,1)S(1)}, u32[]{:S(2)}, u32[]{:S(2)}) collective-permute-start(bf16[4,48,16,128]{3,2,1,0:T(8,128)(2,1)} %collective-permute-done.26.rest_2_), channel_id=1, source_target_pairs={{0,1},{1,0},{2,3},{3,2},{4,5},{5,4},{6,7},{7,6},{8,9},{9,8},{10,11... | collective-permute-start | bytes 2359304 | tf_op jit(solution)/shard_map/ppermute | solution.py:699
  113.7 26.2 %collective-permute-start.36 = (bf16[4,48,16,128]{3,2,1,0:T(8,128)(2,1)S(1)}, bf16[4,48,16,128]{3,2,1,0:T(8,128)(2,1)S(1)}, u32[]{:S(2)}, u32[]{:S(2)}) collective-permute-start(bf16[4,48,16,128]{3,2,1,0:T(8,128)(2,1)S(1)} %collective-permute-done.23.rest_3_), channel_id=1, source_target_pairs={{0,1},{1,0},{2,3},{3,2},{4,5},{5,4},{6,7},{7,6},{8,9},{9,8},{10,11... | collective-permute-start | bytes 2359304 | tf_op jit(solution)/shard_map/ppermute | solution.py:699
  163.5 14.9 %collective-permute-start.37 = (bf16[64,512]{1,0:T(8,128)(2,1)}, bf16[64,512]{1,0:T(8,128)(2,1)S(1)}, u32[]{:S(2)}, u32[]{:S(2)}) collective-permute-start(bf16[64,512]{1,0:T(8,128)(2,1)} %get-tuple-element.149), channel_id=1, source_target_pairs={{1,0},{2,1},{3,2},{4,3},{5,4},{6,5},{7,6},{8,7},{9,8},{10,9},{11,1... | collective-permute-start | bytes 196616 | tf_op jit(solution)/shard_map/ppermute | solution.py:624
  202.3 21.4 %collective-permute-start.48 = (bf16[2,4,48,16,128]{4,3,2,1,0:T(8,128)(2,1)S(1)}, bf16[2,4,48,16,128]{4,3,2,1,0:T(8,128)(2,1)S(1)}, u32[]{:S(2)}, u32[]{:S(2)}) collective-permute-start(bf16[2,4,48,16,128]{4,3,2,1,0:T(8,128)(2,1)S(1)} %get-tuple-element.226), channel_id=1, source_target_pairs={{0,4},{1,3},{2,6},{3,1},{4,0},{5,7},{6,2},{7,5},{8,12},{9,11},{10,... | collective-permute-start | bytes 4718600 | tf_op jit(solution)/shard_map/ppermute | solution.py:699
  224.4 12.1 %collective-permute-start.49 = (bf16[4,48,16,128]{3,2,1,0:T(8,128)(2,1)S(1)}, bf16[4,48,16,128]{3,2,1,0:T(8,128)(2,1)S(1)}, u32[]{:S(2)}, u32[]{:S(2)}) collective-permute-start(bf16[4,48,16,128]{3,2,1,0:T(8,128)(2,1)S(1)} %get-tuple-element.228), channel_id=1, source_target_pairs={{0,2},{1,5},{2,0},{3,7},{4,6},{5,1},{6,4},{7,3},{8,10},{9,13},{10,... | collective-permute-start | bytes 2359304 | tf_op jit(solution)/shard_map/ppermute | solution.py:699
  251.4 20.8 %collective-permute-start.52 = (bf16[2,4,49,16,128]{4,3,2,1,0:T(8,128)(2,1)S(1)}, bf16[2,4,49,16,128]{4,3,2,1,0:T(8,128)(2,1)S(1)}, u32[]{:S(2)}, u32[]{:S(2)}) collective-permute-start(bf16[2,4,49,16,128]{4,3,2,1,0:T(8,128)(2,1)S(1)} %slice_bitcast_fusion), channel_id=1, source_target_pairs={{0,4},{1,3},{2,6},{3,1},{4,0},{5,7},{6,2},{7,5},{8,12},{9,11},{10,... | collective-permute-start | bytes 4816904 | tf_op jit(solution)/shard_map/ppermute | solution.py:699
  253.5 23.0 %collective-permute-start.55 = (bf16[48,16,128]{2,1,0:T(8,128)(2,1)}, bf16[48,16,128]{2,1,0:T(8,128)(2,1)S(1)}, u32[]{:S(2)}, u32[]{:S(2)}) collective-permute-start(bf16[48,16,128]{2,1,0:T(8,128)(2,1)} %get-tuple-element.237), channel_id=1, source_target_pairs={{0,24},{1,25},{2,26},{3,27},{4,28},{5,29},{6,30},{7,31},{8,0},{9,1... | collective-permute-start | bytes 589832 | tf_op jit(solution)/shard_map/ppermute | solution.py:699
  254.8 21.8 %collective-permute-start.54 = (bf16[48,16,128]{2,1,0:T(8,128)(2,1)S(1)}, bf16[48,16,128]{2,1,0:T(8,128)(2,1)S(1)}, u32[]{:S(2)}, u32[]{:S(2)}) collective-permute-start(bf16[48,16,128]{2,1,0:T(8,128)(2,1)S(1)} %get-tuple-element.238), channel_id=1, source_target_pairs={{0,16},{1,17},{2,18},{3,19},{4,20},{5,21},{6,22},{7,23},{8,24},{9,... | collective-permute-start | bytes 589832 | tf_op jit(solution)/shard_map/ppermute | solution.py:699
  262.4 15.9 %collective-permute-start.53 = (bf16[48,16,128]{2,1,0:T(8,128)(2,1)S(1)}, bf16[48,16,128]{2,1,0:T(8,128)(2,1)}, u32[]{:S(2)}, u32[]{:S(2)}) collective-permute-start(bf16[48,16,128]{2,1,0:T(8,128)(2,1)S(1)} %get-tuple-element.239), channel_id=1, source_target_pairs={{0,8},{1,9},{2,10},{3,11},{4,12},{5,13},{6,14},{7,15},{8,16},{9,17... | collective-permute-start | bytes 589832 | tf_op jit(solution)/shard_map/ppermute | solution.py:699
  272.8 17.0 %collective-permute-start.58 = (bf16[4,49,16,128]{3,2,1,0:T(8,128)(2,1)S(1)}, bf16[4,49,16,128]{3,2,1,0:T(8,128)(2,1)}, u32[]{:S(2)}, u32[]{:S(2)}) collective-permute-start(bf16[4,49,16,128]{3,2,1,0:T(8,128)(2,1)S(1)} %slice_bitcast_fusion.4), channel_id=1, source_target_pairs={{0,2},{1,5},{2,0},{3,7},{4,6},{5,1},{6,4},{7,3},{8,10},{9,13},{10,... | collective-permute-start | bytes 2408456 | tf_op jit(solution)/shard_map/ppermute | solution.py:699
  291.9 28.3 %collective-permute-start.65 = (bf16[49,16,128]{2,1,0:T(8,128)(2,1)}, bf16[49,16,128]{2,1,0:T(8,128)(2,1)S(1)}, u32[]{:S(2)}, u32[]{:S(2)}) collective-permute-start(bf16[49,16,128]{2,1,0:T(8,128)(2,1)} %get-tuple-element.230), channel_id=1, source_target_pairs={{0,24},{1,25},{2,26},{3,27},{4,28},{5,29},{6,30},{7,31},{8,0},{9,1... | collective-permute-start | bytes 602120 | tf_op jit(solution)/shard_map/ppermute | solution.py:699
  296.9 23.4 %collective-permute-start.64 = (bf16[49,16,128]{2,1,0:T(8,128)(2,1)S(1)}, bf16[49,16,128]{2,1,0:T(8,128)(2,1)S(1)}, u32[]{:S(2)}, u32[]{:S(2)}) collective-permute-start(bf16[49,16,128]{2,1,0:T(8,128)(2,1)S(1)} %get-tuple-element.231), channel_id=1, source_target_pairs={{0,16},{1,17},{2,18},{3,19},{4,20},{5,21},{6,22},{7,23},{8,24},{9,... | collective-permute-start | bytes 602120 | tf_op jit(solution)/shard_map/ppermute | solution.py:699
  296.9 23.4 %collective-permute-start.63 = (bf16[49,16,128]{2,1,0:T(8,128)(2,1)S(1)}, bf16[49,16,128]{2,1,0:T(8,128)(2,1)S(1)}, u32[]{:S(2)}, u32[]{:S(2)}) collective-permute-start(bf16[49,16,128]{2,1,0:T(8,128)(2,1)S(1)} %get-tuple-element.229), channel_id=1, source_target_pairs={{0,8},{1,9},{2,10},{3,11},{4,12},{5,13},{6,14},{7,15},{8,16},{9,17... | collective-permute-start | bytes 602120 | tf_op jit(solution)/shard_map/ppermute | solution.py:699
  320.5 14.3 %collective-permute-start.66 = (f32[1024]{0:T(1024)S(1)}, f32[1024]{0:T(1024)S(1)}, u32[]{:S(2)}, u32[]{:S(2)}) collective-permute-start(f32[1024]{0:T(1024)S(1)} %fusion.12), channel_id=1, source_target_pairs={{1,0},{2,1},{3,2},{4,3},{5,4},{6,5},{7,6},{8,7},{9,8},{10,9},{11,1... | collective-permute-start | bytes 12296 | tf_op jit(solution)/shard_map/ppermute | solution.py:624
  (68 other events, 792.4 us)
